TPU v7x, 128 devices: a whole 4x4x4 slice. The times are simulated.
128 devices in a mesh: outer: 16 (over x_hi, y, core), inner: 8 (over z, x_lo).
Axes of the slice: x: 4 (x_hi: 2, x_lo: 2; x = x_hi * 2 + x_lo), y: 4, z: 4, core: 2. Of those that a mesh axis runs over, the one named last changes fastest.
Arguments:
- tokens: bfloat16 [65536, 8192], P(('outer', 'inner')), may hold values from -24 to 24
- key_weight: bfloat16 [8192, 512], P('inner', 'outer'), may hold values from -0.0625 to 0.0625
- cotangent: bfloat16 [65536, 512], P(('outer', 'inner')), may hold values from -6 to 6
Outputs:
- keys: bfloat16 [65536, 512], P(('outer', 'inner'))
- input_gradient: bfloat16 [65536, 8192], P(('outer', 'inner'))
- grad_weight: float32 [8192, 512], P('inner', 'outer')
All inputs are finite; a program needn't handle non-finite values.
Results may differ from a plain program's by a relative error of at most 0.005.
Values may be sent and summed in bfloat16 or wider, within the bound.
No kernel may reach another device: no remote copies, remote signals or barrier semaphores. Data moves between devices by JAX's collectives and lax.ppermute only.
A program may use at most 192 MiB of HBM per device.

v0:
```python
import math

import jax
import jax.numpy as jnp
from jax import lax
from jax.sharding import PartitionSpec as P

HEAD = 128
KV_HEADS = 4
SEQ = 4096


EPS = 1e-05


def rope_tables(start, count):
    position = ((start + jnp.arange(count, dtype=jnp.int32)) % SEQ).astype(jnp.float32)
    half = HEAD // 2
    inv_freq = jnp.exp(-math.log(10000.0) * jnp.arange(half, dtype=jnp.float32) / half)
    angle = position[:, None] * inv_freq[None, :]
    return (jnp.cos(angle)[:, None, :], jnp.sin(angle)[:, None, :])


def apply_rotary(values, cosine, sine, sign):
    count = values.shape[0]
    split = values.reshape(count, KV_HEADS, 2, HEAD // 2)
    first = split[:, :, 0, :]
    second = split[:, :, 1, :]
    new_first = first * cosine - sign * second * sine
    new_second = second * cosine + sign * first * sine
    return jnp.stack([new_first, new_second], axis=2).reshape(count, KV_HEADS * HEAD)


def shards(tokens, key_weight, cotangent):
    rows = tokens.shape[0]
    width = tokens.shape[1]
    n_outer = lax.axis_size("outer")
    n_inner = lax.axis_size("inner")
    place = lax.axis_index("outer") * n_inner + lax.axis_index("inner")
    complete_input = tokens.astype(jnp.float32)
    reciprocal_root_mean = lax.rsqrt(
        jnp.mean(complete_input * complete_input, axis=1, keepdims=True) + EPS
    )
    centered_input = complete_input * reciprocal_root_mean
    normalized_tokens = centered_input.astype(jnp.bfloat16)
    cosine, sine = rope_tables(place * rows, rows)
    secondary = lax.all_gather(key_weight, "outer", axis=1, tiled=True)
    features = secondary.shape[1]
    pre = jnp.dot(
        normalized_tokens,
        lax.all_gather(secondary, "inner", axis=0, tiled=True),
        preferred_element_type=jnp.float32,
    )
    keys = apply_rotary(pre, cosine, sine, 1.0).astype(jnp.bfloat16)
    dpre = apply_rotary(cotangent.astype(jnp.float32), cosine, sine, -1.0).astype(jnp.bfloat16)
    term = jnp.einsum(
        "tid,toc->oidc",
        normalized_tokens.reshape(rows, n_inner, width // n_inner),
        dpre.reshape(rows, n_outer, features // n_outer),
        preferred_element_type=jnp.float32,
    )
    normalized_gradient = lax.dot_general(
        dpre,
        lax.all_gather(secondary, "inner", axis=0, tiled=True),
        (((1,), (1,)), ((), ())),
        preferred_element_type=jnp.float32,
    )
    input_gradient = (
        (
            normalized_gradient
            - centered_input * jnp.mean(normalized_gradient * centered_input, axis=1, keepdims=True)
        )
        * reciprocal_root_mean
    ).astype(jnp.bfloat16)
    flat = term.reshape(n_outer * n_inner, width // n_inner, features // n_outer)
    summed = lax.psum_scatter(flat, ("outer", "inner"), scatter_dimension=0, tiled=True)[0]
    scale = 1.0 / math.sqrt(rows * n_outer * n_inner)
    return (keys, input_gradient, summed * scale)


def solution(mesh):
    placed = (P(("outer", "inner"), None), P("inner", "outer"), P(("outer", "inner"), None))
    return jax.shard_map(
        shards,
        mesh=mesh,
        in_specs=placed,
        out_specs=(P(("outer", "inner"), None), P(("outer", "inner"), None), P("inner", "outer")),
        check_vma=False,
    )
```

profile of v0, /device:TPU:1, one launch (start us, length us, event | category | flops | bytes accessed | tf_op | source)
XLA Modules:
  0.0 925.0 jit_solution(17029966360979138966)
XLA Ops:
  7.2 0.0 all-gather.3.cloned.1.call-start
  7.2 0.7 all-gather.3.cloned.1.call-update
  7.9 0.0 all-gather.5.cloned.1.call-start
  7.9 50.9 %all-gather.3.cloned.1.call-done = bf16[1024,512]{0,1:T(8,128)(2,1)} async-done(((bf16[1024,32]{0,1:T(8,128)(2,1)}), bf16[1024,512]{0,1:T(8,128)(2,1)}) %all-gather.3.cloned.1.call-update) | async-done | bytes 1048592 | tf_op jit(solution)/shard_map/all_gather | solution.py:47
  58.9 0.0 all-gather.5.cloned.1.call-update
  58.9 0.0 reduce-scatter.2.cloned.1.call-start
  58.9 1.3 copy.10
  60.2 0.1 convert.9
  60.4 0.5 broadcast_multiply_fusion
  60.9 0.2 multiply_subtract_fusion
  61.1 0.1 maximum_convert_fusion
  61.1 5.1 fusion.7
  66.3 160.9 %all-gather.5.cloned.1.call-done = bf16[8192,512]{0,1:T(8,128)(2,1)} async-done(((bf16[1024,512]{0,1:T(8,128)(2,1)}), bf16[8192,512]{0,1:T(8,128)(2,1)}) %all-gather.5.cloned.1.call-update) | async-done | bytes 8388624 | tf_op jit(solution)/shard_map/all_gather | solution.py:51
  227.2 11.5 %fusion.3 = (f32[512]{0:T(512)S(1)}, f32[512,8192]{1,0:T(8,128)S(1)}) fusion(bf16[512,8192]{1,0:T(8,128)(2,1)} %param.3, f32[512]{0:T(512)S(1)} %add_rsqrt_fusion, bf16[512,512]{0,1:T(8,128)(2,1)S(1)} %bitcast.29, bf16[8192,512]{0,1:T(8,128)(2,1)} %all-gather.5.cloned.1.call-done), kind=kOutput, calls=%fused_computation.5 | convolution fusion | flops 4311744000 | bytes 34082816 | tf_op jit(solution)/shard_map/dot_general | solution.py:62
  238.7 11.1 %fusion.6 = (bf16[512,8192]{1,0:T(8,128)(2,1)}, bf16[512,8192]{1,0:T(8,128)(2,1)}) fusion(f32[512,8192]{1,0:T(8,128)S(1)} %get-tuple-element.16, bf16[512,8192]{1,0:T(8,128)(2,1)} %param.3, f32[512]{0:T(512)S(1)} %broadcast_multiply_fusion.1, f32[512]{0:T(512)S(1)} %add_rsqrt_fusion), kind=kLoop, calls=%fused_computation.8 | loop fusion | flops 29360128 | bytes 41947136 | tf_op jit(solution)/shard_map/convert_element_type | solution.py:74
  249.8 11.4 %fusion.8 = f32[16,32,8,1024]{3,1,2,0:T(8,128)} fusion(bf16[512,16,32,1]{0,2,3,1:T(8,128)(2,1)S(1)} %bitcast.30, bf16[64,8,8,1024]{3,2,1,0:T(8,128)(2,1)} %bitcast.28), kind=kOutput, calls=%fused_computation.11 | convolution fusion | flops 4294967296 | bytes 25690112 | tf_op jit(solution)/shard_map/tid,toc->oidc/dot_general | solution.py:56
  261.2 0.0 reduce-scatter.2.cloned.1.call-update
  261.2 9.4 %fusion.12 = f32[512,512]{0,1:T(8,128)S(1)} fusion(bf16[512,8192]{1,0:T(8,128)(2,1)} %get-tuple-element.7, bf16[8192,512]{0,1:T(8,128)(2,1)} %all-gather.5.cloned.1.call-done), kind=kOutput, calls=%fused_computation.31 | convolution fusion | flops 4294967296 | bytes 17825792 | tf_op jit(solution)/shard_map/dot_general | solution.py:49
  270.7 0.2 subtract_convert_fusion
  270.8 0.1 pad_maximum_fusion
  270.9 1.0 copy.12
  271.9 645.0 %reduce-scatter.2.cloned.1.call-done = f32[1,1024,32]{1,2,0:T(8,128)} async-done(((f32[128,1024,32]{1,2,0:T(8,128)}), f32[1,1024,32]{1,2,0:T(8,128)}) %reduce-scatter.2.cloned.1.call-update) | async-done | bytes 131088 | tf_op jit(solution)/shard_map/reduce_scatter | solution.py:76
  916.9 1.6 multiply_bitcast_fusion
  (4 shorter events, 0.0 us)
Async XLA Ops:
  7.2 51.7 %all-gather.3.cloned.1.call-start = ((), (), s32[]{:S(2)}) async-start(), calls=%async_computation.1 | async-start | bytes 1114112 | tf_op jit(solution)/shard_map/all_gather | solution.py:47
  7.9 219.3 %all-gather.5.cloned.1.call-start = ((), (), s32[]{:S(2)}) async-start(), calls=%async_computation.2 | async-start | bytes 9437184 | tf_op jit(solution)/shard_map/all_gather | solution.py:51
  58.9 858.1 %reduce-scatter.2.cloned.1.call-start = ((), (), s32[]{:S(2)}) async-start(), calls=%async_computation.3 | async-start | bytes 16908288 | tf_op jit(solution)/shard_map/reduce_scatter | solution.py:76
Sparse Core Ops, SparseCore 0:
  10.5 48.3 all-gather.2
  60.5 166.6 all-gather.4
  261.3 655.5 reduce-scatter.1
where the time goes:
time: 940 us; the launch traced here: 925 us
  waiting for transfers between devices  858 us (91%)
  matrix products  32.3 us (3%)
  other arithmetic  18.9 us (2%)
  between operations  13.8 us (1%)
    reduce_scatter x1, waiting for transfers between devices, shards(): lax.psum_scatter(flat, ('outer', 'inner'), scatter_dimension=0, tiled=True)  645 us
    all_gather x1, waiting for transfers between devices, shards(): lax.all_gather(secondary, 'inner', axis=0, tiled=True)  161 us
    all_gather x1, waiting for transfers between devices, shards(): secondary = lax.all_gather(key_weight, 'outer', axis=1, tiled=True)  50.9 us
  transfers between devices with their start and end apart: 3, of which 3 were waited for; matrix products, arithmetic and copies ran while one was open for 2% of the time, Pallas kernels for 0%

commit v1 on v0

v1 whole, which is shorter than its diff:
```python
import math

import jax
import jax.numpy as jnp
from jax import lax
from jax.experimental import pallas as pl
from jax.experimental.pallas import tpu as pltpu
from jax.sharding import Mesh
from jax.sharding import PartitionSpec as P

HEAD = 128
KV_HEADS = 4
SEQ = 4096
EPS = 1e-05
D = 8192
KV = 512
ROWS = 512
LANES = 512
STEPS = D // (2 * LANES)
AXES = ("xh", "y", "c", "z", "xl")
MIB = 1 << 20
F32 = jnp.float32
BF16 = jnp.bfloat16


def rope_tables(start, count):
    position = ((start + jnp.arange(count, dtype=jnp.int32)) % SEQ).astype(F32)
    half = HEAD // 2
    inv_freq = jnp.exp(-math.log(10000.0) * jnp.arange(half, dtype=F32) / half)
    angle = position[:, None] * inv_freq[None, :]
    return jnp.cos(angle), jnp.sin(angle)


def both_halves(cosine, sine):
    cos, sin = cosine[...], sine[...]
    return jnp.concatenate([cos, cos], 1), jnp.concatenate([-sin, sin], 1)


def rotate(values, cosine, sine):
    return values * cosine + pltpu.roll(values, HEAD // 2, 1) * sine


def params(mib):
    return pltpu.CompilerParams(vmem_limit_bytes=mib * MIB)


SMEM = pl.BlockSpec(memory_space=pltpu.SMEM)


VMEM = pl.BlockSpec(memory_space=pltpu.VMEM)


def stay(value):
    return pltpu.with_memory_space_constraint(value, pltpu.VMEM)


def prepare_kernel(start, x, cot, cosine, sine, normed, inv, dpre, dpre_t):
    rows = pl.ds(pl.multiple_of((pl.program_id(0) + start) * 128, 128), 128)
    acc = jnp.zeros((128, 128), F32)
    for k in range(D // 128):
        wide = x[:, k * 128 : (k + 1) * 128].astype(F32)
        acc += wide * wide
    scale = lax.rsqrt(jnp.sum(acc, axis=1, keepdims=True) / D + EPS)
    scale = jnp.broadcast_to(scale, (128, 128))
    inv[rows, :] = scale
    for k in range(D // 128):
        part, col = divmod(k * 128, LANES)
        value = x[:, k * 128 : (k + 1) * 128].astype(F32) * scale
        normed[part % 2, part // 2, rows, col : col + 128] = value.astype(BF16)
    cos, sin = both_halves(cosine, sine)
    for head in range(KV_HEADS):
        cols = slice(head * HEAD, (head + 1) * HEAD)
        turned = rotate(cot[:, cols].astype(F32), cos, -sin)
        dpre[rows, cols] = turned.astype(BF16)
        dpre_t[cols, rows] = turned.T.astype(BF16)


def prepare_call(half, tokens, cot, cosine, sine, before=()):
    blocks = ROWS // 256
    rows = lambda width: pl.BlockSpec((128, width), lambda j: (j + blocks * half, 0))

    def kernel(*refs):
        prepare_kernel(half * blocks, *refs[:4], *refs[4 + len(before) :])

    return pl.pallas_call(
        kernel,
        grid=(blocks,),
        in_specs=[rows(D), rows(KV), rows(HEAD // 2), rows(HEAD // 2)] + [VMEM] * len(before),
        out_specs=[VMEM] * 4,
        out_shape=[
            pltpu.VMEM((2, STEPS, ROWS, LANES), BF16),
            pltpu.VMEM((ROWS, 128), F32),
            pltpu.VMEM((ROWS, KV), BF16),
            pltpu.VMEM((KV, ROWS), BF16),
        ],
        input_output_aliases={4 + i: i for i in range(len(before))},
        compiler_params=params(16),
        cost_estimate=pl.CostEstimate(flops=5 * ROWS * D, bytes_accessed=9 * MIB, transcendentals=0),
        name="row_scales",
    )(
        pltpu.with_memory_space_constraint(tokens, pltpu.HBM),
        pltpu.with_memory_space_constraint(cot, pltpu.HBM),
        cosine,
        sine,
        *map(stay, before),
    )


def send_kernel(core, normed, dpre_t, out):
    @pl.loop(0, STEPS)
    def _(i):
        term = jnp.dot(dpre_t[...], normed[1 - core[0], i], preferred_element_type=F32)
        out[i] = term.astype(BF16).reshape(16, 32, LANES)


def send_call(core, normed, dpre_t):
    return pl.pallas_call(
        send_kernel,
        in_specs=[SMEM, VMEM, VMEM],
        out_specs=VMEM,
        out_shape=pltpu.VMEM((STEPS, 16, 32, LANES), BF16),
        compiler_params=params(8),
        cost_estimate=pl.CostEstimate(flops=ROWS * D * KV, bytes_accessed=9 * MIB, transcendentals=0),
        name="send_half",
    )(core, stay(normed), stay(dpre_t))


def keep_kernel(core, x, y, z, normed, dpre_t, came, *rest):
    outs, total = rest[:8], rest[8]

    @pl.loop(0, STEPS)
    def _(i):
        term = jnp.dot(dpre_t[...], normed[core[0], i], preferred_element_type=F32)
        total[i] = (term.reshape(16, 32, LANES) + came[i].astype(F32)).astype(BF16)

    first = core[0] == 0
    half = LANES // 2

    @pl.loop(0, 16)
    def _(n):
        a, b = n // 4, n % 4
        for r in range(4):
            xx, yy, zz = (x[0] + r) % 4, (y[0] + r) % 4, (z[0] + r) % 4
            for h in range(2):
                x_at = jnp.where(first, xx, b)
                y_at = jnp.where(first, a, yy if h == 0 else a)
                z_at = jnp.where(first, b, a if h == 0 else zz)
                outs[4 * h + r][a, b] = total[
                    2 * z_at + x_at % 2,
                    pl.ds(8 * (x_at // 2) + 2 * y_at, 2),
                    :,
                    h * half : (h + 1) * half,
                ]


def keep_call(core, x, y, z, normed, dpre_t, came):
    part = (4, 4, 2, 32, LANES // 2)
    return pl.pallas_call(
        keep_kernel,
        in_specs=[SMEM] * 4 + [VMEM] * 3,
        out_specs=[VMEM] * 8,
        out_shape=[pltpu.VMEM(part, BF16)] * 8,
        scratch_shapes=[pltpu.VMEM((STEPS, 16, 32, LANES), BF16)],
        compiler_params=params(16),
        cost_estimate=pl.CostEstimate(flops=ROWS * D * KV, bytes_accessed=13 * MIB, transcendentals=0),
        name="keep_half",
    )(core, x, y, z, stay(normed), stay(dpre_t), stay(came))


def sum_first_kernel(core, first, second, own, one, two, three, *outs):
    base = jnp.where(core[0] == 0, first[0], second[0])
    for r in range(4):
        k = (base + r) % 4
        total = own[k].astype(F32)
        for other in (one, two, three):
            total += other[k].astype(F32)
        outs[r][...] = total.astype(BF16)


def sum_first(core, first, second, parts):
    shape = parts[0].shape
    return pl.pallas_call(
        sum_first_kernel,
        in_specs=[SMEM] * 3 + [VMEM] * 4,
        out_specs=[VMEM] * 4,
        out_shape=[pltpu.VMEM(shape[1:], BF16)] * 4,
        compiler_params=params(8),
        cost_estimate=pl.CostEstimate(flops=0, bytes_accessed=10 * math.prod(shape), transcendentals=0),
        name="sum_first",
    )(core, first, second, *map(stay, parts))


def sum_second_kernel(core, first, second, *rest):
    parts, outs = rest[:8], rest[8:]
    base = jnp.where(core[0] == 0, first[0], second[0])
    half = LANES // 2
    for r in range(4):
        k = (base + r) % 4
        for h in range(2):
            total = parts[4 * h][k].astype(F32)
            for other in parts[4 * h + 1 : 4 * h + 4]:
                total += other[k].astype(F32)
            outs[r][:, :, h * half : (h + 1) * half] = total.astype(BF16)


def sum_second(core, first, second, parts):
    return pl.pallas_call(
        sum_second_kernel,
        in_specs=[SMEM] * 3 + [VMEM] * 8,
        out_specs=[VMEM] * 4,
        out_shape=[pltpu.VMEM((2, 32, LANES), BF16)] * 4,
        compiler_params=params(8),
        cost_estimate=pl.CostEstimate(flops=0, bytes_accessed=2 * MIB, transcendentals=0),
        name="sum_second",
    )(core, first, second, *map(stay, parts))


def weight_copies(core, y, z, pieces, ws, sems):
    copies = []
    for side in range(2):
        lane = core[0] if side == 0 else 1 - core[0]
        for r in range(4):
            for k in range(4):
                down, along = jnp.where(lane == 0, r, k), jnp.where(lane == 0, k, r)
                copies.append(
                    pltpu.make_async_copy(
                        pieces[4 * side + r].at[k],
                        ws.at[lane, (z[0] + down) % 4, :, :, (y[0] + along) % 4],
                        sems.at[lane, down, along],
                    )
                )
    return copies


def keys_kernel(core, y, z, normed, dpre, cosine, sine, *rest):
    pieces, (keys, coef, ws, pre, sems) = rest[:8], rest[8:]
    for copy in weight_copies(core, y, z, pieces, ws, sems):
        copy.start()

    @pl.loop(0, 4)
    def _(n):
        down = (z[0] + n) % 4
        for lane in range(2):
            for along in range(4):
                pltpu.make_async_copy(
                    pieces[0].at[0],
                    ws.at[lane, down, :, :, (y[0] + along) % 4],
                    sems.at[lane, n, along],
                ).wait()
        part = None
        for xl in range(2):
            for q in range(2):
                term = lax.dot_general(
                    normed[q, 2 * down + xl],
                    ws[q, down, :, xl].reshape(KV, LANES),
                    (((1,), (1,)), ((), ())),
                    preferred_element_type=F32,
                )
                part = term if part is None else part + term
        pre[...] = jnp.where(n == 0, part, pre[...] + part)

    total = jnp.zeros((ROWS, HEAD), F32)
    cos, sin = both_halves(cosine, sine)
    for head in range(KV_HEADS):
        cols = slice(head * HEAD, (head + 1) * HEAD)
        values = pre[:, cols]
        keys[:, cols] = rotate(values, cos, sin).astype(BF16)
        total += values * dpre[:, cols].astype(F32)
    coef[...] = jnp.broadcast_to(jnp.sum(total, axis=1, keepdims=True) / D, (ROWS, 128))


def keys_call(core, y, z, normed, dpre, cosine, sine, pieces):
    return pl.pallas_call(
        keys_kernel,
        in_specs=[SMEM] * 3 + [VMEM] * 12,
        out_specs=[VMEM] * 3,
        out_shape=[
            jax.ShapeDtypeStruct((ROWS, KV), BF16),
            pltpu.VMEM((ROWS, 128), F32),
            pltpu.VMEM((2, 4, 2, 2, 4, 2, 32, LANES), BF16),
        ],
        scratch_shapes=[pltpu.VMEM((ROWS, KV), F32), pltpu.SemaphoreType.DMA((2, 4, 4))],
        compiler_params=params(12),
        cost_estimate=pl.CostEstimate(flops=2 * ROWS * D * KV, bytes_accessed=18 * MIB, transcendentals=0),
        name="keys",
    )(core, y, z, stay(normed), stay(dpre), cosine, sine, *map(stay, pieces))


def grad_kernel(normed, dpre, inv, coef, ws, grad):
    j = pl.program_id(0)
    for q in range(2):
        weights = ws[q, j // 2, :, j % 2].reshape(KV, LANES)
        back = jnp.dot(dpre[...], weights, preferred_element_type=F32)
        for k in range(LANES // 128):
            cols = slice(k * 128, (k + 1) * 128)
            into = slice(q * LANES + k * 128, q * LANES + (k + 1) * 128)
            less = normed[q, j, :, cols].astype(F32) * coef[...]
            grad[:, into] = ((back[:, cols] - less) * inv[...]).astype(BF16)


def grad_call(normed, dpre, inv, coef, ws):
    return pl.pallas_call(
        grad_kernel,
        grid=(STEPS,),
        in_specs=[VMEM] * 5,
        out_specs=pl.BlockSpec((ROWS, 2 * LANES), lambda j: (0, j)),
        out_shape=jax.ShapeDtypeStruct((ROWS, D), BF16),
        compiler_params=params(16),
        cost_estimate=pl.CostEstimate(flops=2 * ROWS * D * KV, bytes_accessed=18 * MIB, transcendentals=0),
        name="input_gradient",
    )(*map(stay, (normed, dpre, inv, coef, ws)))


def hop(value, first, second, distance):
    pairs = []
    for x in range(4):
        for y in range(4):
            for z in range(4):
                for core in range(2):
                    there = [x, y, z]
                    axis = first if core == 0 else second
                    there[axis] = (there[axis] + distance) % 4
                    pairs.append(tuple(flat(*at, core) for at in ((x, y, z), there)))
    return lax.ppermute(value, AXES, pairs)


def flat(x, y, z, core):
    return ((((x // 2) * 4 + y) * 2 + core) * 4 + z) * 2 + x % 2


def swap_cores(value):
    return lax.ppermute(value, "c", [(0, 1), (1, 0)])


X, Y, Z = 0, 1, 2


def shards(tokens, key_weight, cotangent):
    barrier = lax.optimization_barrier
    one = lambda value: value.astype(jnp.int32).reshape(1)
    index = lax.axis_index
    core, y, z, x = one(index("c")), one(index("y")), one(index("z")), one(index("xh") * 2 + index("xl"))
    first, odd, far = core[0] == 0, (x[0] & 1) == 1, (x[0] & 2) == 2
    cosine, sine = rope_tables((index("z") * 2 + index("xl")) * ROWS, ROWS)

    rows = key_weight.T
    left, right = rows[:, :LANES], rows[:, LANES:]
    came = swap_cores(jnp.where(first, right, left))
    pair = jnp.where(first, jnp.stack([left, came]), jnp.stack([came, right]))

    tokens, pair, core, y, z, x, first, odd, far, cosine, sine = barrier(
        (tokens, pair, core, y, z, x, first, odd, far, cosine, sine)
    )
    ring = [pair] + [hop(pair, X, X, -r) for r in (1, 2, 3)]
    prepared = prepare_call(0, tokens, cotangent, cosine, sine)
    for bit, step in ((odd, 1), (far, 2)):
        ring = [jnp.where(bit, ring[(i - step) % 4], ring[i]) for i in range(4)]
    near = jnp.stack(ring).reshape(2, 2, 2, 32, LANES)

    near, prepared = barrier((near, prepared))
    line = jnp.stack([near] + [hop(near, Y, Z, -r) for r in (1, 2, 3)])
    prepared = prepare_call(1, tokens, cotangent, cosine, sine, prepared)

    line, (normed, inv, dpre, dpre_t) = barrier((line, prepared))
    own = [line] + [hop(line, Z, Y, -r) for r in (1, 2, 3)]
    pieces = own + [swap_cores(piece) for piece in own]
    came = swap_cores(send_call(core, normed, dpre_t))
    cut = keep_call(core, x, y, z, normed, dpre_t, came)

    arrived = [[part[0]] + [hop(part[r], X, axis, r) for r in (1, 2, 3)] for part, axis in ((cut[:4], Y), (cut[4:], Z))]
    cut = [sum_first(core, y, second, parts) for parts, second in zip(arrived, (z, y))]
    arrived = [[part[0]] + [hop(part[r], Y, axis, r) for r in (1, 2, 3)] for part, axis in zip(cut, (Z, Y))]
    keys, coef, ws = keys_call(core, y, z, normed, dpre, cosine, sine, pieces)
    arrived, coef = barrier((arrived, coef))
    cut = sum_second(core, z, x, arrived[0] + arrived[1])
    arrived = [cut[0]] + [hop(cut[r], Z, X, r) for r in (1, 2, 3)]
    grad = grad_call(normed, dpre, inv, coef, ws)
    arrived, grad = barrier((arrived, grad))
    total = sum(part.astype(F32) for part in arrived) * (1.0 / 256.0)
    mine = jnp.where(first, total[0], total[1])
    came = swap_cores(jnp.where(first, total[1], total[0]))
    summed = jnp.where(
        first, jnp.concatenate([mine, came], 1), jnp.concatenate([came, mine], 1)
    )
    return keys, grad, summed.T


def solution(mesh):
    fine = Mesh(mesh.devices.reshape(2, 4, 2, 4, 2), AXES)
    rows = P(AXES, None)
    weight = P(("z", "xl"), ("xh", "y", "c"))
    return jax.shard_map(
        shards,
        mesh=fine,
        in_specs=(rows, weight, rows),
        out_specs=(rows, rows, weight),
        check_vma=False,
    )
```

time: 940 us -> 121 us (0.13); the launches traced: 925 us -> 121 us
  waiting for transfers between devices: 858 us -> 29.9 us
  starting transfers between devices: 0.11 us -> 54.6 us
  Pallas kernels: 0 us -> 32.4 us
  matrix products: 32.3 us -> 0 us
  other arithmetic: 18.9 us -> 2.73 us
  between operations: 13.8 us -> 0.88 us
    reduce_scatter x1 -> x0, waiting for transfers between devices: 645 us -> none  [shards(): lax.psum_scatter(flat, ('outer', 'inner'), scatter_dimension=0, tiled=True)]
    all_gather x2 -> x0, waiting for transfers between devices: 212 us -> none  [the longest x1 161 us: shards(): lax.all_gather(secondary, 'inner', axis=0, tiled=True)]
    ppermute x0 -> x31, starting transfers between devices: none -> 54.6 us  [the longest x24 43 us: hop(): return lax.ppermute(value, AXES, pairs)]
    pallas_call x0 -> x9, Pallas kernels: none -> 32.4 us  [the longest x2 7.98 us: prepare_call(): pl.pallas_call(kernel, grid=(blocks,), in_specs=[rows(D), rows(KV), rows(...]
    dot_general x3 -> x0, matrix products: 32.3 us -> none  [the longest x1 11.5 us: shards(): lax.dot_general(dpre, lax.all_gather(secondary, 'inner', axis=0, tiled=Tr...]
    ppermute x0 -> x31, waiting for transfers between devices: none -> 29.9 us  [the longest x24 26.8 us: hop(): return lax.ppermute(value, AXES, pairs)]
    convert_element_type x3 -> x1, other arithmetic: 11.2 us -> 0.01 us  [rope_tables(): position = ((start + jnp.arange(count, dtype=jnp.int32)) % SEQ).astype(F32)]
  transfers between devices with their start and end apart: 3 -> 31, of which waited for: 3 -> 9; matrix products, arithmetic and copies ran while one was open for 2% -> 1% of each run, Pallas kernels for 0% -> 24%
where the time goes in v1:
time: 121 us
  starting transfers between devices  54.6 us (45%)
  Pallas kernels  32.4 us (27%)
  waiting for transfers between devices  29.9 us (25%)
  other arithmetic  2.73 us (2%)
    ppermute x24, starting transfers between devices, hop(): return lax.ppermute(value, AXES, pairs)  43 us
    ppermute x24, waiting for transfers between devices, hop(): return lax.ppermute(value, AXES, pairs)  26.8 us
    ppermute x7, starting transfers between devices, swap_cores(): return lax.ppermute(value, 'c', [(0, 1), (1, 0)])  11.6 us
    pallas_call x2, Pallas kernels, prepare_call(): pl.pallas_call(kernel, grid=(blocks,), in_specs=[rows(D), rows(KV), rows(...  7.98 us
    pallas_call x1, Pallas kernels, grad_call(): pl.pallas_call(grad_kernel, grid=(STEPS,), in_specs=[VMEM] * 5, out_specs...  7.65 us
    pallas_call x1, Pallas kernels, keys_call(): pl.pallas_call(keys_kernel, in_specs=[SMEM] * 3 + [VMEM] * 12, out_specs=...  7.59 us
    pallas_call x1, Pallas kernels, keep_call(): pl.pallas_call(keep_kernel, in_specs=[SMEM] * 4 + [VMEM] * 3, out_specs=[...  5.04 us
    pallas_call x1, Pallas kernels, send_call(): pl.pallas_call(send_kernel, in_specs=[SMEM, VMEM, VMEM], out_specs=VMEM,...  3.52 us
  transfers between devices with their start and end apart: 31, of which 9 were waited for; matrix products, arithmetic and copies ran while one was open for 1% of the time, Pallas kernels for 24%

profile of v1, /device:TPU:1, one launch (start us, length us, event | category | flops | bytes accessed | tf_op | source)
XLA Modules:
  0.0 120.5 jit_solution(7678462252140666098)
XLA Ops:
  0.6 0.8 slice_bitcast_fusion
  1.4 1.5 %collective-permute-start = (bf16[32,512]{1,0:T(8,128)(2,1)S(1)}, bf16[32,512]{1,0:T(8,128)(2,1)S(1)}, u32[]{:S(2)}, u32[]{:S(2)}) collective-permute-start(bf16[32,512]{1,0:T(8,128)(2,1)S(1)} %get-tuple-element.142), channel_id=1, source_target_pairs={{0,8},{8,0},{1,9},{9,1},{2,10},{10,2},{3,11},{11,3},{4,12},{12,4},... | collective-permute-start | bytes 98312 | tf_op jit(solution)/shard_map/ppermute | solution.py:332
  2.9 1.0 multiply_sine_fusion
  4.0 1.4 %collective-permute-start.3 = (bf16[2,32,512]{2,1,0:T(8,128)(2,1)S(1)}, bf16[2,32,512]{2,1,0:T(8,128)(2,1)S(1)}, u32[]{:S(2)}, u32[]{:S(2)}) collective-permute-start(bf16[2,32,512]{2,1,0:T(8,128)(2,1)S(1)} %maximum_select_fusion.1), channel_id=1, source_target_pairs={{0,1},{8,9},{2,3},{10,11},{4,5},{12,13},{6,7},{14,15},{16,17},{24,... | collective-permute-start | bytes 196616 | tf_op jit(solution)/shard_map/ppermute | solution.py:324
  5.3 2.5 %collective-permute-start.2 = (bf16[2,32,512]{2,1,0:T(8,128)(2,1)S(1)}, bf16[2,32,512]{2,1,0:T(8,128)(2,1)S(1)}, u32[]{:S(2)}, u32[]{:S(2)}) collective-permute-start(bf16[2,32,512]{2,1,0:T(8,128)(2,1)S(1)} %maximum_select_fusion.1), channel_id=1, source_target_pairs={{0,64},{8,72},{2,66},{10,74},{4,68},{12,76},{6,70},{14,78},{16,80}... | collective-permute-start | bytes 196616 | tf_op jit(solution)/shard_map/ppermute | solution.py:324
  7.8 1.2 collective-permute-start.1
  8.9 4.0 %row_scales.2 = (bf16[2,8,512,512]{3,2,1,0:T(8,128)(2,1)S(1)}, f32[512,128]{1,0:T(8,128)S(1)}, bf16[512,512]{1,0:T(8,128)(2,1)S(1)}, bf16[512,512]{1,0:T(8,128)(2,1)S(1)}) custom-call(bf16[512,8192]{1,0:T(8,128)(2,1)} %refs_0_.1, bf16[512,512]{1,0:T(8,128)(2,1)} %refs_1_.3, f32[512,64]{1,0:T(8,128)S(1)} %get-tuple-element.76.refs_2_.cosine, ...), custom_call_target="tpu_custom_call" | custom-call | flops 20971520 | bytes 9437184 | tf_op jit(solution)/shard_map/row_scales/pallas_call | solution.py:85
  13.1 1.7 %collective-permute-start.6 = (bf16[2,2,2,32,512]{4,3,2,1,0:T(8,128)(2,1)S(1)}, bf16[2,2,2,32,512]{4,3,2,1,0:T(8,128)(2,1)S(1)}, u32[]{:S(2)}, u32[]{:S(2)}) collective-permute-start(bf16[2,2,2,32,512]{4,3,2,1,0:T(8,128)(2,1)S(1)} %bitcast.29), channel_id=1, source_target_pairs={{0,16},{8,10},{2,18},{10,12},{4,20},{12,14},{6,22},{14,8},{16,32},... | collective-permute-start | bytes 786440 | tf_op jit(solution)/shard_map/ppermute | solution.py:324
  14.8 3.3 %collective-permute-start.5 = (bf16[2,2,2,32,512]{4,3,2,1,0:T(8,128)(2,1)S(1)}, bf16[2,2,2,32,512]{4,3,2,1,0:T(8,128)(2,1)S(1)}, u32[]{:S(2)}, u32[]{:S(2)}) collective-permute-start(bf16[2,2,2,32,512]{4,3,2,1,0:T(8,128)(2,1)S(1)} %bitcast.30), channel_id=1, source_target_pairs={{0,32},{8,12},{2,34},{10,14},{4,36},{12,8},{6,38},{14,10},{16,48},... | collective-permute-start | bytes 786440 | tf_op jit(solution)/shard_map/ppermute | solution.py:324
  18.1 0.7 collective-permute-start.4
  18.8 4.0 %row_scales.3 = (bf16[2,8,512,512]{3,2,1,0:T(8,128)(2,1)S(1)}, f32[512,128]{1,0:T(8,128)S(1)}, bf16[512,512]{1,0:T(8,128)(2,1)S(1)}, bf16[512,512]{1,0:T(8,128)(2,1)S(1)}) custom-call(bf16[512,8192]{1,0:T(8,128)(2,1)} %refs_0_.1, bf16[512,512]{1,0:T(8,128)(2,1)} %refs_1_.3, ...), custom_call_target="tpu_custom_call", output_to_operand_aliasing={{0}: (4, {}), {1}: (5, {}), {2}: (6, {}), {3}: (7, {})} | custom-call | flops 20971520 | bytes 9437184 | tf_op jit(solution)/shard_map/row_scales/pallas_call | solution.py:85
  22.8 2.1 %collective-permute-done.5 = bf16[2,2,2,32,512]{4,3,2,1,0:T(8,128)(2,1)S(1)} collective-permute-done((bf16[2,2,2,32,512]{4,3,2,1,0:T(8,128)(2,1)S(1)}, bf16[2,2,2,32,512]{4,3,2,1,0:T(8,128)(2,1)S(1)}, u32[]{:S(2)}, u32[]{:S(2)}) %collective-permute-start.5) | collective-permute-done | bytes 262176 | tf_op jit(solution)/shard_map/ppermute | solution.py:324
  24.9 0.1 pad_maximum_fusion.rest_0_
  25.1 3.5 %send_half.1 = bf16[8,16,32,512]{3,2,1,0:T(8,128)(2,1)S(1)} custom-call(s32[1]{0:T(128)} %bitcast.4.core, bf16[2,8,512,512]{3,2,1,0:T(8,128)(2,1)S(1)} %get-tuple-element.91.normed, bf16[512,512]{1,0:T(8,128)(2,1)S(1)} %get-tuple-element.96.dpre_t), custom_call_target="tpu_custom_call" | custom-call | flops 2147483648 | bytes 9437184 | tf_op jit(solution)/shard_map/send_half/pallas_call | solution.py:117
  28.6 0.9 collective-permute-start.14
  29.5 1.4 %collective-permute-start.9 = (bf16[4,2,2,2,32,512]{5,4,3,2,1,0:T(8,128)(2,1)S(1)}, bf16[4,2,2,2,32,512]{5,4,3,2,1,0:T(8,128)(2,1)S(1)}, u32[]{:S(2)}, u32[]{:S(2)}) collective-permute-start(bf16[4,2,2,2,32,512]{5,4,3,2,1,0:T(8,128)(2,1)S(1)} %pad_maximum_fusion.rest_0_), channel_id=1, source_target_pairs={{0,2},{8,24},{2,4},{10,26},{4,6},{12,28},{6,0},{14,30},{16,18},{24... | collective-permute-start | bytes 3145736 | tf_op jit(solution)/shard_map/ppermute | solution.py:324
  30.9 1.8 %collective-permute-start.8 = (bf16[4,2,2,2,32,512]{5,4,3,2,1,0:T(8,128)(2,1)S(1)}, bf16[4,2,2,2,32,512]{5,4,3,2,1,0:T(8,128)(2,1)S(1)}, u32[]{:S(2)}, u32[]{:S(2)}) collective-permute-start(bf16[4,2,2,2,32,512]{5,4,3,2,1,0:T(8,128)(2,1)S(1)} %pad_maximum_fusion.rest_0_), channel_id=1, source_target_pairs={{0,4},{8,40},{2,6},{10,42},{4,0},{12,44},{6,2},{14,46},{16,20},{24... | collective-permute-start | bytes 3145736 | tf_op jit(solution)/shard_map/ppermute | solution.py:324
  32.7 1.5 %collective-permute-start.7 = (bf16[4,2,2,2,32,512]{5,4,3,2,1,0:T(8,128)(2,1)S(1)}, bf16[4,2,2,2,32,512]{5,4,3,2,1,0:T(8,128)(2,1)S(1)}, u32[]{:S(2)}, u32[]{:S(2)}) collective-permute-start(bf16[4,2,2,2,32,512]{5,4,3,2,1,0:T(8,128)(2,1)S(1)} %pad_maximum_fusion.rest_0_), channel_id=1, source_target_pairs={{0,6},{8,56},{2,0},{10,58},{4,2},{12,60},{6,4},{14,62},{16,22},{24... | collective-permute-start | bytes 3145736 | tf_op jit(solution)/shard_map/ppermute | solution.py:324
  34.2 2.1 %collective-permute-done.14.came = bf16[8,16,32,512]{3,2,1,0:T(8,128)(2,1)S(1)} collective-permute-done((bf16[8,16,32,512]{3,2,1,0:T(8,128)(2,1)S(1)}, bf16[8,16,32,512]{3,2,1,0:T(8,128)(2,1)S(1)}, u32[]{:S(2)}, u32[]{:S(2)}) %collective-permute-start.14) | collective-permute-done | bytes 4194336 | tf_op jit(solution)/shard_map/ppermute | solution.py:332
  36.3 5.0 %keep_half.1 = (bf16[4,4,2,32,256]{4,3,2,1,0:T(8,128)(2,1)S(1)}, bf16[4,4,2,32,256]{4,3,2,1,0:T(8,128)(2,1)S(1)}, bf16[4,4,2,32,256]{4,3,2,1,0:T(8,128)(2,1)S(1)...) custom-call(s32[1]{0:T(128)} %bitcast.4.core, ...), custom_call_target="tpu_custom_call" | custom-call | flops 2147483648 | bytes 13631488 | tf_op jit(solution)/shard_map/keep_half/pallas_call | solution.py:158
  41.3 1.4 %collective-permute-start.15 = (bf16[4,4,2,32,256]{4,3,2,1,0:T(8,128)(2,1)S(1)}, bf16[4,4,2,32,256]{4,3,2,1,0:T(8,128)(2,1)S(1)}, u32[]{:S(2)}, u32[]{:S(2)}) collective-permute-start(bf16[4,4,2,32,256]{4,3,2,1,0:T(8,128)(2,1)S(1)} %get-tuple-element.98), channel_id=1, source_target_pairs={{0,1},{8,24},{2,3},{10,26},{4,5},{12,28},{6,7},{14,30},{16,17},{24... | collective-permute-start | bytes 1572872 | tf_op jit(solution)/shard_map/ppermute | solution.py:324
  42.8 1.8 %collective-permute-start.16 = (bf16[4,4,2,32,256]{4,3,2,1,0:T(8,128)(2,1)S(1)}, bf16[4,4,2,32,256]{4,3,2,1,0:T(8,128)(2,1)S(1)}, u32[]{:S(2)}, u32[]{:S(2)}) collective-permute-start(bf16[4,4,2,32,256]{4,3,2,1,0:T(8,128)(2,1)S(1)} %get-tuple-element.99), channel_id=1, source_target_pairs={{0,64},{8,40},{2,66},{10,42},{4,68},{12,44},{6,70},{14,46},{16,80}... | collective-permute-start | bytes 1572872 | tf_op jit(solution)/shard_map/ppermute | solution.py:324
  44.7 1.4 %collective-permute-start.17 = (bf16[4,4,2,32,256]{4,3,2,1,0:T(8,128)(2,1)S(1)}, bf16[4,4,2,32,256]{4,3,2,1,0:T(8,128)(2,1)S(1)}, u32[]{:S(2)}, u32[]{:S(2)}) collective-permute-start(bf16[4,4,2,32,256]{4,3,2,1,0:T(8,128)(2,1)S(1)} %get-tuple-element.100), channel_id=1, source_target_pairs={{0,65},{8,56},{2,67},{10,58},{4,69},{12,60},{6,71},{14,62},{16,81}... | collective-permute-start | bytes 1572872 | tf_op jit(solution)/shard_map/ppermute | solution.py:324
  46.1 10.4 %collective-permute-done.8.rest_2_ = bf16[4,2,2,2,32,512]{5,4,3,2,1,0:T(8,128)(2,1)S(1)} collective-permute-done((bf16[4,2,2,2,32,512]{5,4,3,2,1,0:T(8,128)(2,1)S(1)}, bf16[4,2,2,2,32,512]{5,4,3,2,1,0:T(8,128)(2,1)S(1)}, u32[]{:S(2)}, u32[]{:S(2)}) %collective-permute-start.8) | collective-permute-done | bytes 1048608 | tf_op jit(solution)/shard_map/ppermute | solution.py:324
  56.5 1.6 %collective-permute-start.21 = (bf16[4,4,2,32,256]{4,3,2,1,0:T(8,128)(2,1)S(1)}, bf16[4,4,2,32,256]{4,3,2,1,0:T(8,128)(2,1)S(1)}, u32[]{:S(2)}, u32[]{:S(2)}) collective-permute-start(bf16[4,4,2,32,256]{4,3,2,1,0:T(8,128)(2,1)S(1)} %get-tuple-element.106), channel_id=1, source_target_pairs={{0,1},{8,10},{2,3},{10,12},{4,5},{12,14},{6,7},{14,8},{16,17},{24,... | collective-permute-start | bytes 1572872 | tf_op jit(solution)/shard_map/ppermute | solution.py:324
  58.1 3.3 %collective-permute-start.22 = (bf16[4,4,2,32,256]{4,3,2,1,0:T(8,128)(2,1)S(1)}, bf16[4,4,2,32,256]{4,3,2,1,0:T(8,128)(2,1)S(1)}, u32[]{:S(2)}, u32[]{:S(2)}) collective-permute-start(bf16[4,4,2,32,256]{4,3,2,1,0:T(8,128)(2,1)S(1)} %get-tuple-element.107), channel_id=1, source_target_pairs={{0,64},{8,12},{2,66},{10,14},{4,68},{12,8},{6,70},{14,10},{16,80},... | collective-permute-start | bytes 1572872 | tf_op jit(solution)/shard_map/ppermute | solution.py:324
  61.4 0.3 collective-permute-done.15.one
  61.7 0.3 collective-permute-start.10
  62.0 5.4 %collective-permute-done.16.two = bf16[4,4,2,32,256]{4,3,2,1,0:T(8,128)(2,1)S(1)} collective-permute-done((bf16[4,4,2,32,256]{4,3,2,1,0:T(8,128)(2,1)S(1)}, bf16[4,4,2,32,256]{4,3,2,1,0:T(8,128)(2,1)S(1)}, u32[]{:S(2)}, u32[]{:S(2)}) %collective-permute-start.16) | collective-permute-done | bytes 524320 | tf_op jit(solution)/shard_map/ppermute | solution.py:324
  67.4 0.4 collective-permute-done.17.three
  67.8 0.1 collective-permute-start.12
  67.9 7.2 %collective-permute-start.11 = (bf16[4,2,2,2,32,512]{5,4,3,2,1,0:T(8,128)(2,1)S(1)}, bf16[4,2,2,2,32,512]{5,4,3,2,1,0:T(8,128)(2,1)S(1)}, u32[]{:S(2)}, u32[]{:S(2)}) collective-permute-start(bf16[4,2,2,2,32,512]{5,4,3,2,1,0:T(8,128)(2,1)S(1)} %collective-permute-done.7.rest_1_), channel_id=1, source_target_pairs={{0,8},{8,0},{1,9},{9,1},{2,10},{10,2},{3,11},{11,3},{4,12},{12,4},... | collective-permute-start | bytes 3145736 | tf_op jit(solution)/shard_map/ppermute | solution.py:332
  75.1 0.3 sum_first.2
  75.4 8.1 %collective-permute-done.23.three = bf16[4,4,2,32,256]{4,3,2,1,0:T(8,128)(2,1)S(1)} collective-permute-done((bf16[4,4,2,32,256]{4,3,2,1,0:T(8,128)(2,1)S(1)}, bf16[4,4,2,32,256]{4,3,2,1,0:T(8,128)(2,1)S(1)}, u32[]{:S(2)}, u32[]{:S(2)}) %collective-permute-start.23) | collective-permute-done | bytes 524320 | tf_op jit(solution)/shard_map/ppermute | solution.py:324
  83.5 0.3 sum_first.3
  83.7 2.2 %collective-permute-start.19 = (bf16[4,2,32,256]{3,2,1,0:T(8,128)(2,1)S(1)}, bf16[4,2,32,256]{3,2,1,0:T(8,128)(2,1)S(1)}, u32[]{:S(2)}, u32[]{:S(2)}) collective-permute-start(bf16[4,2,32,256]{3,2,1,0:T(8,128)(2,1)S(1)} %get-tuple-element.103), channel_id=1, source_target_pairs={{0,32},{8,12},{2,34},{10,14},{4,36},{12,8},{6,38},{14,10},{16,48},... | collective-permute-start | bytes 393224 | tf_op jit(solution)/shard_map/ppermute | solution.py:324
  85.9 1.5 %collective-permute-start.20 = (bf16[4,2,32,256]{3,2,1,0:T(8,128)(2,1)S(1)}, bf16[4,2,32,256]{3,2,1,0:T(8,128)(2,1)S(1)}, u32[]{:S(2)}, u32[]{:S(2)}) collective-permute-start(bf16[4,2,32,256]{3,2,1,0:T(8,128)(2,1)S(1)} %get-tuple-element.104), channel_id=1, source_target_pairs={{0,48},{8,14},{2,50},{10,8},{4,52},{12,10},{6,54},{14,12},{16,0},{... | collective-permute-start | bytes 393224 | tf_op jit(solution)/shard_map/ppermute | solution.py:324
  87.4 7.0 %collective-permute-start.24 = (bf16[4,2,32,256]{3,2,1,0:T(8,128)(2,1)S(1)}, bf16[4,2,32,256]{3,2,1,0:T(8,128)(2,1)S(1)}, u32[]{:S(2)}, u32[]{:S(2)}) collective-permute-start(bf16[4,2,32,256]{3,2,1,0:T(8,128)(2,1)S(1)} %get-tuple-element.110), channel_id=1, source_target_pairs={{0,16},{8,24},{2,18},{10,26},{4,20},{12,28},{6,22},{14,30},{16,32}... | collective-permute-start | bytes 393224 | tf_op jit(solution)/shard_map/ppermute | solution.py:324
  94.5 2.1 %collective-permute-start.25 = (bf16[4,2,32,256]{3,2,1,0:T(8,128)(2,1)S(1)}, bf16[4,2,32,256]{3,2,1,0:T(8,128)(2,1)S(1)}, u32[]{:S(2)}, u32[]{:S(2)}) collective-permute-start(bf16[4,2,32,256]{3,2,1,0:T(8,128)(2,1)S(1)} %get-tuple-element.111), channel_id=1, source_target_pairs={{0,32},{8,40},{2,34},{10,42},{4,36},{12,44},{6,38},{14,46},{16,48}... | collective-permute-start | bytes 393224 | tf_op jit(solution)/shard_map/ppermute | solution.py:324
  96.6 2.4 %collective-permute-start.26 = (bf16[4,2,32,256]{3,2,1,0:T(8,128)(2,1)S(1)}, bf16[4,2,32,256]{3,2,1,0:T(8,128)(2,1)S(1)}, u32[]{:S(2)}, u32[]{:S(2)}) collective-permute-start(bf16[4,2,32,256]{3,2,1,0:T(8,128)(2,1)S(1)} %get-tuple-element.112), channel_id=1, source_target_pairs={{0,48},{8,56},{2,50},{10,58},{4,52},{12,60},{6,54},{14,62},{16,0},... | collective-permute-start | bytes 393224 | tf_op jit(solution)/shard_map/ppermute | solution.py:324
  99.0 7.6 %keys.1 = (bf16[512,512]{1,0:T(8,128)(2,1)}, f32[512,128]{1,0:T(8,128)S(1)}, bf16[2,4,2,2,4,2,32,512]{7,6,5,4,3,2,1,0:T(8,128)(2,1)S(1)}) custom-call(s32[1]{0:T(128)} %bitcast.4.core, s32[1]{0:T(128)} %bitcast.5.y.first.second, s32[1]{0:T(128)} %bitcast.6.z.second.first, bf16[2,8,512,512]{3,2,1,0:T(8,128)(2,1)S(1)} %get-tuple-element.91.normed, ...), custom_call_target="tpu_custom_call" | custom-call | flops 4294967296 | bytes 18874368 | tf_op jit(solution)/shard_map/keys/pallas_call | solution.py:273
  106.7 0.1 sum_second.1
  106.9 0.2 collective-permute-start.28
  107.1 2.5 %collective-permute-start.29 = (bf16[2,32,512]{2,1,0:T(8,128)(2,1)S(1)}, bf16[2,32,512]{2,1,0:T(8,128)(2,1)S(1)}, u32[]{:S(2)}, u32[]{:S(2)}) collective-permute-start(bf16[2,32,512]{2,1,0:T(8,128)(2,1)S(1)} %get-tuple-element.125), channel_id=1, source_target_pairs={{0,6},{8,73},{2,0},{10,75},{4,2},{12,77},{6,4},{14,79},{16,22},{24... | collective-permute-start | bytes 196616 | tf_op jit(solution)/shard_map/ppermute | solution.py:324
  109.6 7.6 %input_gradient.1 = bf16[512,8192]{1,0:T(8,128)(2,1)} custom-call(bf16[2,8,512,512]{3,2,1,0:T(8,128)(2,1)S(1)} %get-tuple-element.91.normed, bf16[512,512]{1,0:T(8,128)(2,1)S(1)} %get-tuple-element.92.dpre, f32[512,128]{1,0:T(8,128)S(1)} %get-tuple-element.126.inv, f32[512,128]{1,0:T(8,128)S(1)} %get-tuple-element.127.coef, ...), custom_call_target="tpu_custom_call" | custom-call | flops 4294967296 | bytes 18874368 | tf_op jit(solution)/shard_map/input_gradient/pallas_call | solution.py:302
  117.3 1.7 %collective-permute-start.30 = (f32[32,512]{1,0:T(8,128)S(1)}, f32[32,512]{1,0:T(8,128)S(1)}, u32[]{:S(2)}, u32[]{:S(2)}) collective-permute-start(f32[32,512]{1,0:T(8,128)S(1)} %get-tuple-element.140), channel_id=1, source_target_pairs={{0,8},{8,0},{1,9},{9,1},{2,10},{10,2},{3,11},{11,3},{4,12},{12,4},... | collective-permute-start | bytes 196616 | tf_op jit(solution)/shard_map/ppermute | solution.py:332
  118.9 0.9 collective-permute-done.30
  119.9 0.7 fusion
  (34 shorter events, 0.4 us)
Async XLA Ops:
  1.4 2.5 %collective-permute-start = (bf16[32,512]{1,0:T(8,128)(2,1)S(1)}, bf16[32,512]{1,0:T(8,128)(2,1)S(1)}, u32[]{:S(2)}, u32[]{:S(2)}) collective-permute-start(bf16[32,512]{1,0:T(8,128)(2,1)S(1)} %get-tuple-element.142), channel_id=1, source_target_pairs={{0,8},{8,0},{1,9},{9,1},{2,10},{10,2},{3,11},{11,3},{4,12},{12,4},... | collective-permute-start | bytes 98312 | tf_op jit(solution)/shard_map/ppermute | solution.py:332
  4.0 9.0 %collective-permute-start.3 = (bf16[2,32,512]{2,1,0:T(8,128)(2,1)S(1)}, bf16[2,32,512]{2,1,0:T(8,128)(2,1)S(1)}, u32[]{:S(2)}, u32[]{:S(2)}) collective-permute-start(bf16[2,32,512]{2,1,0:T(8,128)(2,1)S(1)} %maximum_select_fusion.1), channel_id=1, source_target_pairs={{0,1},{8,9},{2,3},{10,11},{4,5},{12,13},{6,7},{14,15},{16,17},{24,... | collective-permute-start | bytes 196616 | tf_op jit(solution)/shard_map/ppermute | solution.py:324
  5.3 7.6 %collective-permute-start.2 = (bf16[2,32,512]{2,1,0:T(8,128)(2,1)S(1)}, bf16[2,32,512]{2,1,0:T(8,128)(2,1)S(1)}, u32[]{:S(2)}, u32[]{:S(2)}) collective-permute-start(bf16[2,32,512]{2,1,0:T(8,128)(2,1)S(1)} %maximum_select_fusion.1), channel_id=1, source_target_pairs={{0,64},{8,72},{2,66},{10,74},{4,68},{12,76},{6,70},{14,78},{16,80}... | collective-permute-start | bytes 196616 | tf_op jit(solution)/shard_map/ppermute | solution.py:324
  7.8 5.2 %collective-permute-start.1 = (bf16[2,32,512]{2,1,0:T(8,128)(2,1)S(1)}, bf16[2,32,512]{2,1,0:T(8,128)(2,1)S(1)}, u32[]{:S(2)}, u32[]{:S(2)}) collective-permute-start(bf16[2,32,512]{2,1,0:T(8,128)(2,1)S(1)} %maximum_select_fusion.1), channel_id=1, source_target_pairs={{0,65},{8,73},{2,67},{10,75},{4,69},{12,77},{6,71},{14,79},{16,81}... | collective-permute-start | bytes 196616 | tf_op jit(solution)/shard_map/ppermute | solution.py:324
  13.1 9.7 %collective-permute-start.6 = (bf16[2,2,2,32,512]{4,3,2,1,0:T(8,128)(2,1)S(1)}, bf16[2,2,2,32,512]{4,3,2,1,0:T(8,128)(2,1)S(1)}, u32[]{:S(2)}, u32[]{:S(2)}) collective-permute-start(bf16[2,2,2,32,512]{4,3,2,1,0:T(8,128)(2,1)S(1)} %bitcast.29), channel_id=1, source_target_pairs={{0,16},{8,10},{2,18},{10,12},{4,20},{12,14},{6,22},{14,8},{16,32},... | collective-permute-start | bytes 786440 | tf_op jit(solution)/shard_map/ppermute | solution.py:324
  14.8 10.2 %collective-permute-start.5 = (bf16[2,2,2,32,512]{4,3,2,1,0:T(8,128)(2,1)S(1)}, bf16[2,2,2,32,512]{4,3,2,1,0:T(8,128)(2,1)S(1)}, u32[]{:S(2)}, u32[]{:S(2)}) collective-permute-start(bf16[2,2,2,32,512]{4,3,2,1,0:T(8,128)(2,1)S(1)} %bitcast.30), channel_id=1, source_target_pairs={{0,32},{8,12},{2,34},{10,14},{4,36},{12,8},{6,38},{14,10},{16,48},... | collective-permute-start | bytes 786440 | tf_op jit(solution)/shard_map/ppermute | solution.py:324
  18.1 6.9 %collective-permute-start.4 = (bf16[2,2,2,32,512]{4,3,2,1,0:T(8,128)(2,1)S(1)}, bf16[2,2,2,32,512]{4,3,2,1,0:T(8,128)(2,1)S(1)}, u32[]{:S(2)}, u32[]{:S(2)}) collective-permute-start(bf16[2,2,2,32,512]{4,3,2,1,0:T(8,128)(2,1)S(1)} %bitcast.31), channel_id=1, source_target_pairs={{0,48},{8,14},{2,50},{10,8},{4,52},{12,10},{6,54},{14,12},{16,0},{... | collective-permute-start | bytes 786440 | tf_op jit(solution)/shard_map/ppermute | solution.py:324
  28.6 7.7 %collective-permute-start.14 = (bf16[8,16,32,512]{3,2,1,0:T(8,128)(2,1)S(1)}, bf16[8,16,32,512]{3,2,1,0:T(8,128)(2,1)S(1)}, u32[]{:S(2)}, u32[]{:S(2)}) collective-permute-start(bf16[8,16,32,512]{3,2,1,0:T(8,128)(2,1)S(1)} %send_half.1), channel_id=1, source_target_pairs={{0,8},{8,0},{1,9},{9,1},{2,10},{10,2},{3,11},{11,3},{4,12},{12,4},... | collective-permute-start | bytes 12582920 | tf_op jit(solution)/shard_map/ppermute | solution.py:332
  29.5 15.2 %collective-permute-start.9 = (bf16[4,2,2,2,32,512]{5,4,3,2,1,0:T(8,128)(2,1)S(1)}, bf16[4,2,2,2,32,512]{5,4,3,2,1,0:T(8,128)(2,1)S(1)}, u32[]{:S(2)}, u32[]{:S(2)}) collective-permute-start(bf16[4,2,2,2,32,512]{5,4,3,2,1,0:T(8,128)(2,1)S(1)} %pad_maximum_fusion.rest_0_), channel_id=1, source_target_pairs={{0,2},{8,24},{2,4},{10,26},{4,6},{12,28},{6,0},{14,30},{16,18},{24... | collective-permute-start | bytes 3145736 | tf_op jit(solution)/shard_map/ppermute | solution.py:324
  30.9 25.6 %collective-permute-start.8 = (bf16[4,2,2,2,32,512]{5,4,3,2,1,0:T(8,128)(2,1)S(1)}, bf16[4,2,2,2,32,512]{5,4,3,2,1,0:T(8,128)(2,1)S(1)}, u32[]{:S(2)}, u32[]{:S(2)}) collective-permute-start(bf16[4,2,2,2,32,512]{5,4,3,2,1,0:T(8,128)(2,1)S(1)} %pad_maximum_fusion.rest_0_), channel_id=1, source_target_pairs={{0,4},{8,40},{2,6},{10,42},{4,0},{12,44},{6,2},{14,46},{16,20},{24... | collective-permute-start | bytes 3145736 | tf_op jit(solution)/shard_map/ppermute | solution.py:324
  32.7 25.4 %collective-permute-start.7 = (bf16[4,2,2,2,32,512]{5,4,3,2,1,0:T(8,128)(2,1)S(1)}, bf16[4,2,2,2,32,512]{5,4,3,2,1,0:T(8,128)(2,1)S(1)}, u32[]{:S(2)}, u32[]{:S(2)}) collective-permute-start(bf16[4,2,2,2,32,512]{5,4,3,2,1,0:T(8,128)(2,1)S(1)} %pad_maximum_fusion.rest_0_), channel_id=1, source_target_pairs={{0,6},{8,56},{2,0},{10,58},{4,2},{12,60},{6,4},{14,62},{16,22},{24... | collective-permute-start | bytes 3145736 | tf_op jit(solution)/shard_map/ppermute | solution.py:324
  41.3 20.4 %collective-permute-start.15 = (bf16[4,4,2,32,256]{4,3,2,1,0:T(8,128)(2,1)S(1)}, bf16[4,4,2,32,256]{4,3,2,1,0:T(8,128)(2,1)S(1)}, u32[]{:S(2)}, u32[]{:S(2)}) collective-permute-start(bf16[4,4,2,32,256]{4,3,2,1,0:T(8,128)(2,1)S(1)} %get-tuple-element.98), channel_id=1, source_target_pairs={{0,1},{8,24},{2,3},{10,26},{4,5},{12,28},{6,7},{14,30},{16,17},{24... | collective-permute-start | bytes 1572872 | tf_op jit(solution)/shard_map/ppermute | solution.py:324
  42.8 24.6 %collective-permute-start.16 = (bf16[4,4,2,32,256]{4,3,2,1,0:T(8,128)(2,1)S(1)}, bf16[4,4,2,32,256]{4,3,2,1,0:T(8,128)(2,1)S(1)}, u32[]{:S(2)}, u32[]{:S(2)}) collective-permute-start(bf16[4,4,2,32,256]{4,3,2,1,0:T(8,128)(2,1)S(1)} %get-tuple-element.99), channel_id=1, source_target_pairs={{0,64},{8,40},{2,66},{10,42},{4,68},{12,44},{6,70},{14,46},{16,80}... | collective-permute-start | bytes 1572872 | tf_op jit(solution)/shard_map/ppermute | solution.py:324
  44.7 23.1 %collective-permute-start.17 = (bf16[4,4,2,32,256]{4,3,2,1,0:T(8,128)(2,1)S(1)}, bf16[4,4,2,32,256]{4,3,2,1,0:T(8,128)(2,1)S(1)}, u32[]{:S(2)}, u32[]{:S(2)}) collective-permute-start(bf16[4,4,2,32,256]{4,3,2,1,0:T(8,128)(2,1)S(1)} %get-tuple-element.100), channel_id=1, source_target_pairs={{0,65},{8,56},{2,67},{10,58},{4,69},{12,60},{6,71},{14,62},{16,81}... | collective-permute-start | bytes 1572872 | tf_op jit(solution)/shard_map/ppermute | solution.py:324
  56.5 11.5 %collective-permute-start.21 = (bf16[4,4,2,32,256]{4,3,2,1,0:T(8,128)(2,1)S(1)}, bf16[4,4,2,32,256]{4,3,2,1,0:T(8,128)(2,1)S(1)}, u32[]{:S(2)}, u32[]{:S(2)}) collective-permute-start(bf16[4,4,2,32,256]{4,3,2,1,0:T(8,128)(2,1)S(1)} %get-tuple-element.106), channel_id=1, source_target_pairs={{0,1},{8,10},{2,3},{10,12},{4,5},{12,14},{6,7},{14,8},{16,17},{24,... | collective-permute-start | bytes 1572872 | tf_op jit(solution)/shard_map/ppermute | solution.py:324
  58.1 17.0 %collective-permute-start.22 = (bf16[4,4,2,32,256]{4,3,2,1,0:T(8,128)(2,1)S(1)}, bf16[4,4,2,32,256]{4,3,2,1,0:T(8,128)(2,1)S(1)}, u32[]{:S(2)}, u32[]{:S(2)}) collective-permute-start(bf16[4,4,2,32,256]{4,3,2,1,0:T(8,128)(2,1)S(1)} %get-tuple-element.107), channel_id=1, source_target_pairs={{0,64},{8,12},{2,66},{10,14},{4,68},{12,8},{6,70},{14,10},{16,80},... | collective-permute-start | bytes 1572872 | tf_op jit(solution)/shard_map/ppermute | solution.py:324
  61.7 22.0 %collective-permute-start.10 = (bf16[4,2,2,2,32,512]{5,4,3,2,1,0:T(8,128)(2,1)S(1)}, bf16[4,2,2,2,32,512]{5,4,3,2,1,0:T(8,128)(2,1)S(1)}, u32[]{:S(2)}, u32[]{:S(2)}) collective-permute-start(bf16[4,2,2,2,32,512]{5,4,3,2,1,0:T(8,128)(2,1)S(1)} %pad_maximum_fusion.rest_0_), channel_id=1, source_target_pairs={{0,8},{8,0},{1,9},{9,1},{2,10},{10,2},{3,11},{11,3},{4,12},{12,4},... | collective-permute-start | bytes 3145736 | tf_op jit(solution)/shard_map/ppermute | solution.py:332
  67.4 18.5 %collective-permute-start.13 = (bf16[4,2,2,2,32,512]{5,4,3,2,1,0:T(8,128)(2,1)S(1)}, bf16[4,2,2,2,32,512]{5,4,3,2,1,0:T(8,128)(2,1)S(1)}, u32[]{:S(2)}, u32[]{:S(2)}) collective-permute-start(bf16[4,2,2,2,32,512]{5,4,3,2,1,0:T(8,128)(2,1)S(1)} %collective-permute-done.9.rest_3_), channel_id=1, source_target_pairs={{0,8},{8,0},{1,9},{9,1},{2,10},{10,2},{3,11},{11,3},{4,12},{12,4},... | collective-permute-start | bytes 3145736 | tf_op jit(solution)/shard_map/ppermute | solution.py:332
  67.8 19.6 %collective-permute-start.12 = (bf16[4,2,2,2,32,512]{5,4,3,2,1,0:T(8,128)(2,1)S(1)}, bf16[4,2,2,2,32,512]{5,4,3,2,1,0:T(8,128)(2,1)S(1)}, u32[]{:S(2)}, u32[]{:S(2)}) collective-permute-start(bf16[4,2,2,2,32,512]{5,4,3,2,1,0:T(8,128)(2,1)S(1)} %collective-permute-done.8.rest_2_), channel_id=1, source_target_pairs={{0,8},{8,0},{1,9},{9,1},{2,10},{10,2},{3,11},{11,3},{4,12},{12,4},... | collective-permute-start | bytes 3145736 | tf_op jit(solution)/shard_map/ppermute | solution.py:332
  67.9 26.6 %collective-permute-start.11 = (bf16[4,2,2,2,32,512]{5,4,3,2,1,0:T(8,128)(2,1)S(1)}, bf16[4,2,2,2,32,512]{5,4,3,2,1,0:T(8,128)(2,1)S(1)}, u32[]{:S(2)}, u32[]{:S(2)}) collective-permute-start(bf16[4,2,2,2,32,512]{5,4,3,2,1,0:T(8,128)(2,1)S(1)} %collective-permute-done.7.rest_1_), channel_id=1, source_target_pairs={{0,8},{8,0},{1,9},{9,1},{2,10},{10,2},{3,11},{11,3},{4,12},{12,4},... | collective-permute-start | bytes 3145736 | tf_op jit(solution)/shard_map/ppermute | solution.py:332
  75.1 8.3 %collective-permute-start.23 = (bf16[4,4,2,32,256]{4,3,2,1,0:T(8,128)(2,1)S(1)}, bf16[4,4,2,32,256]{4,3,2,1,0:T(8,128)(2,1)S(1)}, u32[]{:S(2)}, u32[]{:S(2)}) collective-permute-start(bf16[4,4,2,32,256]{4,3,2,1,0:T(8,128)(2,1)S(1)} %get-tuple-element.108), channel_id=1, source_target_pairs={{0,65},{8,14},{2,67},{10,8},{4,69},{12,10},{6,71},{14,12},{16,81},... | collective-permute-start | bytes 1572872 | tf_op jit(solution)/shard_map/ppermute | solution.py:324
  83.4 13.1 %collective-permute-start.18 = (bf16[4,2,32,256]{3,2,1,0:T(8,128)(2,1)S(1)}, bf16[4,2,32,256]{3,2,1,0:T(8,128)(2,1)S(1)}, u32[]{:S(2)}, u32[]{:S(2)}) collective-permute-start(bf16[4,2,32,256]{3,2,1,0:T(8,128)(2,1)S(1)} %get-tuple-element.102), channel_id=1, source_target_pairs={{0,16},{8,10},{2,18},{10,12},{4,20},{12,14},{6,22},{14,8},{16,32},... | collective-permute-start | bytes 393224 | tf_op jit(solution)/shard_map/ppermute | solution.py:324
  83.7 22.9 %collective-permute-start.19 = (bf16[4,2,32,256]{3,2,1,0:T(8,128)(2,1)S(1)}, bf16[4,2,32,256]{3,2,1,0:T(8,128)(2,1)S(1)}, u32[]{:S(2)}, u32[]{:S(2)}) collective-permute-start(bf16[4,2,32,256]{3,2,1,0:T(8,128)(2,1)S(1)} %get-tuple-element.103), channel_id=1, source_target_pairs={{0,32},{8,12},{2,34},{10,14},{4,36},{12,8},{6,38},{14,10},{16,48},... | collective-permute-start | bytes 393224 | tf_op jit(solution)/shard_map/ppermute | solution.py:324
  85.9 20.7 %collective-permute-start.20 = (bf16[4,2,32,256]{3,2,1,0:T(8,128)(2,1)S(1)}, bf16[4,2,32,256]{3,2,1,0:T(8,128)(2,1)S(1)}, u32[]{:S(2)}, u32[]{:S(2)}) collective-permute-start(bf16[4,2,32,256]{3,2,1,0:T(8,128)(2,1)S(1)} %get-tuple-element.104), channel_id=1, source_target_pairs={{0,48},{8,14},{2,50},{10,8},{4,52},{12,10},{6,54},{14,12},{16,0},{... | collective-permute-start | bytes 393224 | tf_op jit(solution)/shard_map/ppermute | solution.py:324
  87.4 19.2 %collective-permute-start.24 = (bf16[4,2,32,256]{3,2,1,0:T(8,128)(2,1)S(1)}, bf16[4,2,32,256]{3,2,1,0:T(8,128)(2,1)S(1)}, u32[]{:S(2)}, u32[]{:S(2)}) collective-permute-start(bf16[4,2,32,256]{3,2,1,0:T(8,128)(2,1)S(1)} %get-tuple-element.110), channel_id=1, source_target_pairs={{0,16},{8,24},{2,18},{10,26},{4,20},{12,28},{6,22},{14,30},{16,32}... | collective-permute-start | bytes 393224 | tf_op jit(solution)/shard_map/ppermute | solution.py:324
  94.5 12.1 %collective-permute-start.25 = (bf16[4,2,32,256]{3,2,1,0:T(8,128)(2,1)S(1)}, bf16[4,2,32,256]{3,2,1,0:T(8,128)(2,1)S(1)}, u32[]{:S(2)}, u32[]{:S(2)}) collective-permute-start(bf16[4,2,32,256]{3,2,1,0:T(8,128)(2,1)S(1)} %get-tuple-element.111), channel_id=1, source_target_pairs={{0,32},{8,40},{2,34},{10,42},{4,36},{12,44},{6,38},{14,46},{16,48}... | collective-permute-start | bytes 393224 | tf_op jit(solution)/shard_map/ppermute | solution.py:324
  96.6 10.1 %collective-permute-start.26 = (bf16[4,2,32,256]{3,2,1,0:T(8,128)(2,1)S(1)}, bf16[4,2,32,256]{3,2,1,0:T(8,128)(2,1)S(1)}, u32[]{:S(2)}, u32[]{:S(2)}) collective-permute-start(bf16[4,2,32,256]{3,2,1,0:T(8,128)(2,1)S(1)} %get-tuple-element.112), channel_id=1, source_target_pairs={{0,48},{8,56},{2,50},{10,58},{4,52},{12,60},{6,54},{14,62},{16,0},... | collective-permute-start | bytes 393224 | tf_op jit(solution)/shard_map/ppermute | solution.py:324
  106.8 10.4 %collective-permute-start.27 = (bf16[2,32,512]{2,1,0:T(8,128)(2,1)S(1)}, bf16[2,32,512]{2,1,0:T(8,128)(2,1)S(1)}, u32[]{:S(2)}, u32[]{:S(2)}) collective-permute-start(bf16[2,32,512]{2,1,0:T(8,128)(2,1)S(1)} %get-tuple-element.123), channel_id=1, source_target_pairs={{0,2},{8,9},{2,4},{10,11},{4,6},{12,13},{6,0},{14,15},{16,18},{24,... | collective-permute-start | bytes 196616 | tf_op jit(solution)/shard_map/ppermute | solution.py:324
  106.9 10.3 %collective-permute-start.28 = (bf16[2,32,512]{2,1,0:T(8,128)(2,1)S(1)}, bf16[2,32,512]{2,1,0:T(8,128)(2,1)S(1)}, u32[]{:S(2)}, u32[]{:S(2)}) collective-permute-start(bf16[2,32,512]{2,1,0:T(8,128)(2,1)S(1)} %get-tuple-element.124), channel_id=1, source_target_pairs={{0,4},{8,72},{2,6},{10,74},{4,0},{12,76},{6,2},{14,78},{16,20},{24... | collective-permute-start | bytes 196616 | tf_op jit(solution)/shard_map/ppermute | solution.py:324
  107.1 10.2 %collective-permute-start.29 = (bf16[2,32,512]{2,1,0:T(8,128)(2,1)S(1)}, bf16[2,32,512]{2,1,0:T(8,128)(2,1)S(1)}, u32[]{:S(2)}, u32[]{:S(2)}) collective-permute-start(bf16[2,32,512]{2,1,0:T(8,128)(2,1)S(1)} %get-tuple-element.125), channel_id=1, source_target_pairs={{0,6},{8,73},{2,0},{10,75},{4,2},{12,77},{6,4},{14,79},{16,22},{24... | collective-permute-start | bytes 196616 | tf_op jit(solution)/shard_map/ppermute | solution.py:324
  117.3 2.6 %collective-permute-start.30 = (f32[32,512]{1,0:T(8,128)S(1)}, f32[32,512]{1,0:T(8,128)S(1)}, u32[]{:S(2)}, u32[]{:S(2)}) collective-permute-start(f32[32,512]{1,0:T(8,128)S(1)} %get-tuple-element.140), channel_id=1, source_target_pairs={{0,8},{8,0},{1,9},{9,1},{2,10},{10,2},{3,11},{11,3},{4,12},{12,4},... | collective-permute-start | bytes 196616 | tf_op jit(solution)/shard_map/ppermute | solution.py:332

commit v2 on v1

v2 whole, which is shorter than its diff:
```python
import math

import jax
import jax.numpy as jnp
from jax import lax
from jax.experimental import pallas as pl
from jax.experimental.pallas import tpu as pltpu
from jax.sharding import Mesh
from jax.sharding import PartitionSpec as P

HEAD = 128
KV_HEADS = 4
SEQ = 4096
EPS = 1e-05
D = 8192
KV = 512
ROWS = 512
LANES = 512
STEPS = D // (2 * LANES)
AXES = ("xh", "y", "c", "z", "xl")
MIB = 1 << 20
F32 = jnp.float32
BF16 = jnp.bfloat16


def rope_tables(start, count):
    position = ((start + jnp.arange(count, dtype=jnp.int32)) % SEQ).astype(F32)
    half = HEAD // 2
    inv_freq = jnp.exp(-math.log(10000.0) * jnp.arange(half, dtype=F32) / half)
    angle = position[:, None] * inv_freq[None, :]
    return jnp.cos(angle), jnp.sin(angle)


def both_halves(cosine, sine):
    cos, sin = cosine[...], sine[...]
    return jnp.concatenate([cos, cos], 1), jnp.concatenate([-sin, sin], 1)


def rotate(values, cosine, sine):
    return values * cosine + pltpu.roll(values, HEAD // 2, 1) * sine


def params(mib):
    return pltpu.CompilerParams(vmem_limit_bytes=mib * MIB)


SMEM = pl.BlockSpec(memory_space=pltpu.SMEM)


VMEM = pl.BlockSpec(memory_space=pltpu.VMEM)


def stay(value):
    return pltpu.with_memory_space_constraint(value, pltpu.VMEM)


def prepare_kernel(x, cot, cosine, sine, normed, inv, dpre, dpre_t):
    rows = pl.ds(pl.multiple_of(pl.program_id(0) * 128, 128), 128)
    acc = jnp.zeros((128, 128), F32)
    for k in range(D // 128):
        wide = x[:, k * 128 : (k + 1) * 128].astype(F32)
        acc += wide * wide
    scale = lax.rsqrt(jnp.sum(acc, axis=1, keepdims=True) / D + EPS)
    scale = jnp.broadcast_to(scale, (128, 128))
    inv[rows, :] = scale
    for k in range(D // 128):
        part, col = divmod(k * 128, LANES)
        value = x[:, k * 128 : (k + 1) * 128].astype(F32) * scale
        normed[part % 2, part // 2, rows, col : col + 128] = value.astype(BF16)
    cos, sin = both_halves(cosine, sine)
    for head in range(KV_HEADS):
        cols = slice(head * HEAD, (head + 1) * HEAD)
        turned = rotate(cot[:, cols].astype(F32), cos, -sin)
        dpre[rows, cols] = turned.astype(BF16)
        dpre_t[cols, rows] = turned.T.astype(BF16)


def prepare_call(tokens, cot, cosine, sine):
    rows = lambda width: pl.BlockSpec((128, width), lambda j: (j, 0))
    return pl.pallas_call(
        prepare_kernel,
        grid=(ROWS // 128,),
        in_specs=[rows(D), rows(KV), rows(HEAD // 2), rows(HEAD // 2)],
        out_specs=[VMEM] * 4,
        out_shape=[
            pltpu.VMEM((2, STEPS, ROWS, LANES), BF16),
            pltpu.VMEM((ROWS, 128), F32),
            pltpu.VMEM((ROWS, KV), BF16),
            pltpu.VMEM((KV, ROWS), BF16),
        ],
        compiler_params=params(16),
        cost_estimate=pl.CostEstimate(flops=10 * ROWS * D, bytes_accessed=18 * MIB, transcendentals=0),
        name="row_scales",
    )(
        pltpu.with_memory_space_constraint(tokens, pltpu.HBM),
        pltpu.with_memory_space_constraint(cot, pltpu.HBM),
        cosine,
        sine,
    )


def send_kernel(core, normed, dpre_t, out):
    @pl.loop(0, STEPS)
    def _(i):
        term = jnp.dot(dpre_t[...], normed[1 - core[0], i], preferred_element_type=F32)
        out[i] = term.astype(BF16).reshape(16, 32, LANES)


def send_call(core, normed, dpre_t):
    return pl.pallas_call(
        send_kernel,
        in_specs=[SMEM, VMEM, VMEM],
        out_specs=VMEM,
        out_shape=pltpu.VMEM((STEPS, 16, 32, LANES), BF16),
        compiler_params=params(8),
        cost_estimate=pl.CostEstimate(flops=ROWS * D * KV, bytes_accessed=9 * MIB, transcendentals=0),
        name="send_half",
    )(core, stay(normed), stay(dpre_t))


def keep_kernel(core, x, y, normed, dpre_t, came, *rest):
    (own, up, down, far_up, far_down), total = rest[:5], rest[5]

    @pl.loop(0, STEPS)
    def _(i):
        term = jnp.dot(dpre_t[...], normed[core[0], i], preferred_element_type=F32)
        total[i] = (term.reshape(16, 32, LANES) + came[i].astype(F32)).astype(BF16)

    first = core[0] == 0

    @pl.loop(0, 16)
    def _(n):
        a, b = n // 4, n % 4
        for r in range(4):
            x_at = jnp.where(first, (x[0] + r) % 4, a)
            y_at = jnp.where(first, a, (y[0] + r) % 4)
            block = total[2 * b + x_at % 2, pl.ds(8 * (x_at // 2) + 2 * y_at, 2)]
            if r != 2:
                {0: own, 1: up, 3: down}[r][a, b] = block
                continue

            @pl.when(a < 2)
            def _():
                far_up[a, b] = block

            @pl.when(a >= 2)
            def _():
                far_down[a - 2, b] = block


def keep_call(core, x, y, normed, dpre_t, came):
    part, half = (4, 4, 2, 32, LANES), (2, 4, 2, 32, LANES)
    return pl.pallas_call(
        keep_kernel,
        in_specs=[SMEM] * 3 + [VMEM] * 3,
        out_specs=[VMEM] * 5,
        out_shape=[pltpu.VMEM(part, BF16)] * 3 + [pltpu.VMEM(half, BF16)] * 2,
        scratch_shapes=[pltpu.VMEM((STEPS, 16, 32, LANES), BF16)],
        compiler_params=params(16),
        cost_estimate=pl.CostEstimate(flops=ROWS * D * KV, bytes_accessed=13 * MIB, transcendentals=0),
        name="keep_half",
    )(core, x, y, stay(normed), stay(dpre_t), stay(came))


def pass_on_kernel(up, down, from_below, from_above, up_out, down_out):
    up_out[:2] = (up[:2].astype(F32) + from_below[...].astype(F32)).astype(BF16)
    down_out[2:] = (down[2:].astype(F32) + from_above[...].astype(F32)).astype(BF16)


def pass_on(up, down, from_below, from_above):
    return pl.pallas_call(
        pass_on_kernel,
        in_specs=[VMEM] * 4,
        out_specs=[VMEM] * 2,
        out_shape=[pltpu.VMEM(up.shape, BF16)] * 2,
        input_output_aliases={0: 0, 1: 1},
        compiler_params=params(8),
        cost_estimate=pl.CostEstimate(flops=0, bytes_accessed=3 * MIB, transcendentals=0),
        name="pass_on",
    )(*map(stay, (up, down, from_below, from_above)))


def sum_cut_kernel(core, x, y, own, one, two, *outs):
    base = jnp.where(core[0] == 0, y[0], x[0])
    for r in range(4):
        k = (base + r) % 4
        total = own[k].astype(F32) + one[k].astype(F32) + two[k].astype(F32)
        outs[r][...] = total.astype(BF16)


def sum_cut(core, x, y, parts):
    shape = parts[0].shape
    return pl.pallas_call(
        sum_cut_kernel,
        in_specs=[SMEM] * 3 + [VMEM] * 3,
        out_specs=[VMEM] * 4,
        out_shape=[pltpu.VMEM(shape[1:], BF16)] * 4,
        compiler_params=params(8),
        cost_estimate=pl.CostEstimate(flops=64424509440, bytes_accessed=125829120, transcendentals=0),
        name="sum_first",
    )(core, x, y, *map(stay, parts))


def cut_kernel(z, one, two, three, four, *outs):
    for r in range(4):
        k = (z[0] + r) % 4
        total = one[k].astype(F32) + two[k].astype(F32)
        outs[r][...] = (total + three[k].astype(F32) + four[k].astype(F32)).astype(BF16)


def cut_call(z, parts):
    shape = parts[0].shape
    return pl.pallas_call(
        cut_kernel,
        in_specs=[SMEM] + [VMEM] * 4,
        out_specs=[VMEM] * 4,
        out_shape=[pltpu.VMEM(shape[1:], BF16)] * 4,
        compiler_params=params(8),
        cost_estimate=pl.CostEstimate(flops=0, bytes_accessed=2 * MIB, transcendentals=0),
        name="sum_second",
    )(z, *map(stay, parts))


def assemble_kernel(core, y, z, *refs):
    pieces, out = refs[:5], refs[5]
    for piece, r, start in zip(pieces, (0, 1, 3, 2, 2), (0, 0, 0, 0, 2)):

        @pl.loop(0, piece.shape[0])
        def _(i):
            k = i + start
            down, along = jnp.where(core[0] == 0, r, k), jnp.where(core[0] == 0, k, r)
            out[(z[0] + down) % 4, :, :, (y[0] + along) % 4] = piece[i]


def assemble(core, y, z, pieces):
    return pl.pallas_call(
        assemble_kernel,
        in_specs=[SMEM] * 3 + [VMEM] * 5,
        out_specs=VMEM,
        out_shape=pltpu.VMEM((4, 2, 2, 4, 2, 32, LANES), BF16),
        compiler_params=params(8),
        cost_estimate=pl.CostEstimate(flops=0, bytes_accessed=8 * MIB, transcendentals=0),
        name="assemble",
    )(core, y, z, *map(stay, pieces))


def products(half, normed, weights, pre):
    @pl.loop(0, 4)
    def _(n):
        part = None
        for xl in range(2):
            term = lax.dot_general(
                normed[half, 2 * n + xl],
                weights[n, :, xl].reshape(KV, LANES),
                (((1,), (1,)), ((), ())),
                preferred_element_type=F32,
            )
            part = term if part is None else part + term
        pre[...] += part


def own_kernel(core, normed, weights, pre):
    pre[...] = jnp.zeros_like(pre)
    products(core[0], normed, weights, pre)


def own_call(core, normed, weights):
    return pl.pallas_call(
        own_kernel,
        in_specs=[SMEM] + [VMEM] * 2,
        out_specs=VMEM,
        out_shape=pltpu.VMEM((ROWS, KV), F32),
        compiler_params=params(12),
        cost_estimate=pl.CostEstimate(flops=6442450944, bytes_accessed=12582912, transcendentals=0),
        name="keys_own_half",
    )(core, stay(normed), stay(weights))


def keys_kernel(core, normed, dpre, cosine, sine, weights, so_far, keys, coef, pre):
    pre[...] = so_far[...]
    products(1 - core[0], normed, weights, pre)
    total = jnp.zeros((ROWS, HEAD), F32)
    cos, sin = both_halves(cosine, sine)
    for head in range(KV_HEADS):
        cols = slice(head * HEAD, (head + 1) * HEAD)
        values = pre[:, cols]
        keys[:, cols] = rotate(values, cos, sin).astype(BF16)
        total += values * dpre[:, cols].astype(F32)
    coef[...] = jnp.broadcast_to(jnp.sum(total, axis=1, keepdims=True) / D, (ROWS, 128))


def keys_call(core, normed, dpre, cosine, sine, weights, so_far):
    return pl.pallas_call(
        keys_kernel,
        in_specs=[SMEM] + [VMEM] * 6,
        out_specs=[VMEM] * 2,
        out_shape=[
            jax.ShapeDtypeStruct((ROWS, KV), BF16),
            pltpu.VMEM((ROWS, 128), F32),
        ],
        scratch_shapes=[pltpu.VMEM((ROWS, KV), F32)],
        compiler_params=params(12),
        cost_estimate=pl.CostEstimate(flops=ROWS * D * KV, bytes_accessed=9 * MIB, transcendentals=0),
        name="keys",
    )(core, stay(normed), stay(dpre), cosine, sine, stay(weights), stay(so_far))


def grad_kernel(core, normed, dpre, inv, coef, own, other, grad):
    j = pl.program_id(0)
    for half, weights in ((core[0], own), (1 - core[0], other)):
        here = weights[j // 2, :, j % 2].reshape(KV, LANES)
        back = jnp.dot(dpre[...], here, preferred_element_type=F32)
        for k in range(LANES // 128):
            cols = slice(k * 128, (k + 1) * 128)
            into = pl.ds(pl.multiple_of(half * LANES + k * 128, 128), 128)
            less = normed[half, j, :, cols].astype(F32) * coef[...]
            grad[:, into] = ((back[:, cols] - less) * inv[...]).astype(BF16)


def grad_call(core, normed, dpre, inv, coef, own, other):
    return pl.pallas_call(
        grad_kernel,
        grid=(STEPS,),
        in_specs=[SMEM] + [VMEM] * 6,
        out_specs=pl.BlockSpec((ROWS, 2 * LANES), lambda j: (0, j)),
        out_shape=jax.ShapeDtypeStruct((ROWS, D), BF16),
        compiler_params=params(16),
        cost_estimate=pl.CostEstimate(flops=2 * ROWS * D * KV, bytes_accessed=18 * MIB, transcendentals=0),
        name="input_gradient",
    )(core, *map(stay, (normed, dpre, inv, coef, own, other)))


def hop(value, first, second, distance):
    pairs = []
    for x in range(4):
        for y in range(4):
            for z in range(4):
                for core in range(2):
                    there = [x, y, z]
                    axis = first if core == 0 else second
                    there[axis] = (there[axis] + distance) % 4
                    pairs.append(tuple(flat(*at, core) for at in ((x, y, z), there)))
    return lax.ppermute(value, AXES, pairs)


def flat(x, y, z, core):
    return ((((x // 2) * 4 + y) * 2 + core) * 4 + z) * 2 + x % 2


def swap_cores(value):
    return lax.ppermute(value, "c", [(0, 1), (1, 0)])


X, Y, Z = 0, 1, 2


def shards(tokens, key_weight, cotangent):
    barrier = lax.optimization_barrier
    one = lambda value: value.astype(jnp.int32).reshape(1)
    index = lax.axis_index
    core, y, z, x = one(index("c")), one(index("y")), one(index("z")), one(index("xh") * 2 + index("xl"))
    first, odd, far = core[0] == 0, (x[0] & 1) == 1, (x[0] & 2) == 2
    cosine, sine = rope_tables((index("z") * 2 + index("xl")) * ROWS, ROWS)

    rows = key_weight.T
    left, right = rows[:, :LANES], rows[:, LANES:]
    came = swap_cores(jnp.where(first, right, left))
    pair = jnp.where(first, jnp.stack([left, came]), jnp.stack([came, right]))

    tokens, pair, core, y, z, x, first, odd, far, cosine, sine = barrier(
        (tokens, pair, core, y, z, x, first, odd, far, cosine, sine)
    )
    ring = [pair] + [hop(pair, X, X, -r) for r in (1, 2, 3)]
    normed, inv, dpre, dpre_t = prepare_call(tokens, cotangent, cosine, sine)
    for bit, step in ((odd, 1), (far, 2)):
        ring = [jnp.where(bit, ring[(i - step) % 4], ring[i]) for i in range(4)]
    near = jnp.stack(ring).reshape(2, 2, 2, 32, LANES)

    near, normed = barrier((near, normed))
    line = jnp.stack([near] + [hop(near, Y, Z, -r) for r in (1, 2, 3)])
    send = send_call(core, normed, dpre_t)

    line, send = barrier((line, send))
    above, below = hop(line, Z, Y, -1), hop(line, Z, Y, 1)
    came = swap_cores(send)
    own, up, down, far_up, far_down = keep_call(core, x, y, normed, dpre_t, came)

    from_below, from_above = hop(far_up, X, Y, 1), hop(far_down, X, Y, -1)
    above, below = barrier((above, below, own))[:2]
    across = hop(above[:2], Z, Y, -1), hop(below[2:], Z, Y, 1)
    up, down = pass_on(up, down, from_below, from_above)
    arrived = [own, hop(up, X, Y, 1), hop(down, X, Y, -1)]
    weights = assemble(core, y, z, [line, above, below, across[0], across[1]])
    so_far = own_call(core, normed, weights)
    others = swap_cores(barrier((weights, so_far))[0])
    keys, coef = keys_call(core, normed, dpre, cosine, sine, others, so_far)
    cut = sum_cut(core, x, y, arrived)
    arrived = [cut[0]] + [hop(cut[r], Y, X, r) for r in (2, 1, 3)]
    arrived, coef = barrier((arrived, coef))
    cut = cut_call(z, arrived)
    arrived = [cut[0]] + [hop(cut[r], Z, Z, r) for r in (2, 1, 3)]
    grad = grad_call(core, normed, dpre, inv, coef, weights, others)
    arrived, grad = barrier((arrived, grad))
    total = sum(part.astype(F32) for part in arrived) * (1.0 / 256.0)
    mine = jnp.where(first, total[0], total[1])
    came = swap_cores(jnp.where(first, total[1], total[0]))
    summed = jnp.where(
        first, jnp.concatenate([mine, came], 1), jnp.concatenate([came, mine], 1)
    )
    return keys, grad, summed.T


def solution(mesh):
    fine = Mesh(mesh.devices.reshape(2, 4, 2, 4, 2), AXES)
    rows = P(AXES, None)
    weight = P(("z", "xl"), ("xh", "y", "c"))
    return jax.shard_map(
        shards,
        mesh=fine,
        in_specs=(rows, weight, rows),
        out_specs=(rows, rows, weight),
        check_vma=False,
    )
```

time: 121 us -> 96.8 us (0.80)
  starting transfers between devices: 54.6 us -> 35.9 us
  waiting for transfers between devices: 29.9 us -> 23.8 us
    ppermute x24 -> x20, starting transfers between devices: 43 us -> 29 us  [hop(): return lax.ppermute(value, AXES, pairs)]
    ppermute x24 -> x20, waiting for transfers between devices: 26.8 us -> 18.1 us  [hop(): return lax.ppermute(value, AXES, pairs)]
    ppermute x7 -> x4, starting transfers between devices: 11.6 us -> 6.89 us  [swap_cores(): return lax.ppermute(value, 'c', [(0, 1), (1, 0)])]
    ppermute x7 -> x4, waiting for transfers between devices: 3.06 us -> 5.68 us  [swap_cores(): return lax.ppermute(value, 'c', [(0, 1), (1, 0)])]
    pallas_call x8 -> x9, Pallas kernels: 28.9 us -> 29.8 us  [the longest x1 8.84 us: grad_call(): pl.pallas_call(grad_kernel, grid=(STEPS,), in_specs=[SMEM] + [VMEM] * 6,...]
  transfers between devices with their start and end apart: 31 -> 24, of which waited for: 9 -> 9; matrix products, arithmetic and copies ran while one was open for 1% -> 1% of each run, Pallas kernels for 24% -> 34%
where the time goes in v2:
time: 96.8 us; the launch traced here: 96.6 us
  starting transfers between devices  35.9 us (37%)
  Pallas kernels  33.3 us (34%)
  waiting for transfers between devices  23.8 us (25%)
  other arithmetic  2.73 us (3%)
    ppermute x20, starting transfers between devices, hop(): return lax.ppermute(value, AXES, pairs)  29 us
    ppermute x20, waiting for transfers between devices, hop(): return lax.ppermute(value, AXES, pairs)  18.1 us
    pallas_call x1, Pallas kernels, grad_call(): pl.pallas_call(grad_kernel, grid=(STEPS,), in_specs=[SMEM] + [VMEM] * 6,...  8.84 us
    ppermute x4, starting transfers between devices, swap_cores(): return lax.ppermute(value, 'c', [(0, 1), (1, 0)])  6.89 us
    pallas_call x1, Pallas kernels, prepare_call(): pl.pallas_call(prepare_kernel, grid=(ROWS // 128,), in_specs=[rows(D), ro...  6.88 us
    ppermute x4, waiting for transfers between devices, swap_cores(): return lax.ppermute(value, 'c', [(0, 1), (1, 0)])  5.68 us
    pallas_call x1, Pallas kernels, keep_call(): pl.pallas_call(keep_kernel, in_specs=[SMEM] * 3 + [VMEM] * 3, out_specs=[...  4.92 us
    pallas_call x1, Pallas kernels, keys_call(): pl.pallas_call(keys_kernel, in_specs=[SMEM] + [VMEM] * 6, out_specs=[VMEM...  4.35 us
  transfers between devices with their start and end apart: 24, of which 9 were waited for; matrix products, arithmetic and copies ran while one was open for 1% of the time, Pallas kernels for 34%

profile of v2, /device:TPU:1, one launch (start us, length us, event | category | flops | bytes accessed | tf_op | source)
XLA Modules:
  0.0 96.6 jit_solution(2299160814453626982)
XLA Ops:
  0.6 0.8 slice_bitcast_fusion
  1.4 1.5 %collective-permute-start = (bf16[32,512]{1,0:T(8,128)(2,1)S(1)}, bf16[32,512]{1,0:T(8,128)(2,1)S(1)}, u32[]{:S(2)}, u32[]{:S(2)}) collective-permute-start(bf16[32,512]{1,0:T(8,128)(2,1)S(1)} %get-tuple-element.108), channel_id=1, source_target_pairs={{0,8},{8,0},{1,9},{9,1},{2,10},{10,2},{3,11},{11,3},{4,12},{12,4},... | collective-permute-start | bytes 98312 | tf_op jit(solution)/shard_map/ppermute | solution.py:351
  2.9 1.0 %multiply_sine_fusion = (f32[512,64]{1,0:T(8,128)S(1)}, f32[512,64]{1,0:T(8,128)S(1)}) fusion(f32[64]{0:T(128)S(1)} %multiply_exponential_fusion, f32[512]{0:T(512)S(1)} %fusion.2), kind=kLoop, calls=%fused_computation.1 | loop fusion | flops 32768 | bytes 264448 | tf_op jit(solution)/shard_map/sin | solution.py:31
  3.9 0.0 collective-permute-done
  4.0 2.6 %collective-permute-start.1 = (bf16[2,32,512]{2,1,0:T(8,128)(2,1)S(1)}, bf16[2,32,512]{2,1,0:T(8,128)(2,1)S(1)}, u32[]{:S(2)}, u32[]{:S(2)}) collective-permute-start(bf16[2,32,512]{2,1,0:T(8,128)(2,1)S(1)} %maximum_select_fusion.1), channel_id=1, source_target_pairs={{0,65},{8,73},{2,67},{10,75},{4,69},{12,77},{6,71},{14,79},{16,81}... | collective-permute-start | bytes 196616 | tf_op jit(solution)/shard_map/ppermute | solution.py:343
  6.6 0.5 collective-permute-start.2
  7.1 0.6 collective-permute-start.3
  7.7 6.9 %row_scales.1 = (bf16[2,8,512,512]{3,2,1,0:T(8,128)(2,1)S(1)}, f32[512,128]{1,0:T(8,128)S(1)}, bf16[512,512]{1,0:T(8,128)(2,1)S(1)}, bf16[512,512]{1,0:T(8,128)(2,1)S(1)}) custom-call(bf16[512,8192]{1,0:T(8,128)(2,1)} %x, bf16[512,512]{1,0:T(8,128)(2,1)} %cot.1, f32[512,64]{1,0:T(8,128)S(1)} %get-tuple-element.57.cosine, f32[512,64]{1,0:T(8,128)S(1)} %get-tuple-element.58.sine), custom_call_target="tpu_custom_call" | custom-call | flops 41943040 | bytes 18874368 | tf_op jit(solution)/shard_map/row_scales/pallas_call | solution.py:80
  14.6 0.0 collective-permute-done.3
  14.7 1.7 %collective-permute-start.6 = (bf16[2,2,2,32,512]{4,3,2,1,0:T(8,128)(2,1)S(1)}, bf16[2,2,2,32,512]{4,3,2,1,0:T(8,128)(2,1)S(1)}, u32[]{:S(2)}, u32[]{:S(2)}) collective-permute-start(bf16[2,2,2,32,512]{4,3,2,1,0:T(8,128)(2,1)S(1)} %bitcast.29), channel_id=1, source_target_pairs={{0,16},{8,10},{2,18},{10,12},{4,20},{12,14},{6,22},{14,8},{16,32},... | collective-permute-start | bytes 786440 | tf_op jit(solution)/shard_map/ppermute | solution.py:343
  16.4 3.3 %collective-permute-start.5 = (bf16[2,2,2,32,512]{4,3,2,1,0:T(8,128)(2,1)S(1)}, bf16[2,2,2,32,512]{4,3,2,1,0:T(8,128)(2,1)S(1)}, u32[]{:S(2)}, u32[]{:S(2)}) collective-permute-start(bf16[2,2,2,32,512]{4,3,2,1,0:T(8,128)(2,1)S(1)} %bitcast.30), channel_id=1, source_target_pairs={{0,32},{8,12},{2,34},{10,14},{4,36},{12,8},{6,38},{14,10},{16,48},... | collective-permute-start | bytes 786440 | tf_op jit(solution)/shard_map/ppermute | solution.py:343
  19.7 0.7 collective-permute-start.4
  20.5 3.5 %send_half.1 = bf16[8,16,32,512]{3,2,1,0:T(8,128)(2,1)S(1)} custom-call(s32[1]{0:T(128)} %bitcast.4.core, bf16[2,8,512,512]{3,2,1,0:T(8,128)(2,1)S(1)} %get-tuple-element.60.normed, bf16[512,512]{1,0:T(8,128)(2,1)S(1)} %get-tuple-element.65.dpre_t), custom_call_target="tpu_custom_call" | custom-call | flops 2147483648 | bytes 9437184 | tf_op jit(solution)/shard_map/send_half/pallas_call | solution.py:110
  24.0 2.6 %collective-permute-done.5 = bf16[2,2,2,32,512]{4,3,2,1,0:T(8,128)(2,1)S(1)} collective-permute-done((bf16[2,2,2,32,512]{4,3,2,1,0:T(8,128)(2,1)S(1)}, bf16[2,2,2,32,512]{4,3,2,1,0:T(8,128)(2,1)S(1)}, u32[]{:S(2)}, u32[]{:S(2)}) %collective-permute-start.5) | collective-permute-done | bytes 262176 | tf_op jit(solution)/shard_map/ppermute | solution.py:343
  26.6 0.1 pad_maximum_fusion.refs_0_
  26.7 0.9 collective-permute-start.9
  27.7 2.0 %collective-permute-start.7 = (bf16[4,2,2,2,32,512]{5,4,3,2,1,0:T(8,128)(2,1)S(1)}, bf16[4,2,2,2,32,512]{5,4,3,2,1,0:T(8,128)(2,1)S(1)}, u32[]{:S(2)}, u32[]{:S(2)}) collective-permute-start(bf16[4,2,2,2,32,512]{5,4,3,2,1,0:T(8,128)(2,1)S(1)} %pad_maximum_fusion.refs_0_), channel_id=1, source_target_pairs={{0,6},{8,56},{2,0},{10,58},{4,2},{12,60},{6,4},{14,62},{16,22},{24... | collective-permute-start | bytes 3145736 | tf_op jit(solution)/shard_map/ppermute | solution.py:343
  29.7 4.8 %collective-permute-done.9.came = bf16[8,16,32,512]{3,2,1,0:T(8,128)(2,1)S(1)} collective-permute-done((bf16[8,16,32,512]{3,2,1,0:T(8,128)(2,1)S(1)}, bf16[8,16,32,512]{3,2,1,0:T(8,128)(2,1)S(1)}, u32[]{:S(2)}, u32[]{:S(2)}) %collective-permute-start.9) | collective-permute-done | bytes 4194336 | tf_op jit(solution)/shard_map/ppermute | solution.py:351
  34.5 4.9 %keep_half.1 = (bf16[4,4,2,32,512]{4,3,2,1,0:T(8,128)(2,1)S(1)}, bf16[4,4,2,32,512]{4,3,2,1,0:T(8,128)(2,1)S(1)}, bf16[4,4,2,32,512]{4,3,2,1,0:T(8,128)(2,1)S(1)...) custom-call(s32[1]{0:T(128)} %bitcast.4.core, s32[1]{0:T(128)} %bitcast.7.x, s32[1]{0:T(128)} %bitcast.5.y, ...), custom_call_target="tpu_custom_call" | custom-call | flops 2147483648 | bytes 13631488 | tf_op jit(solution)/shard_map/keep_half/pallas_call | solution.py:153
  39.4 1.4 %collective-permute-start.13 = (bf16[2,4,2,32,512]{4,3,2,1,0:T(8,128)(2,1)S(1)}, bf16[2,4,2,32,512]{4,3,2,1,0:T(8,128)(2,1)S(1)}, u32[]{:S(2)}, u32[]{:S(2)}) collective-permute-start(bf16[2,4,2,32,512]{4,3,2,1,0:T(8,128)(2,1)S(1)} %get-tuple-element.76), channel_id=1, source_target_pairs={{0,1},{8,24},{2,3},{10,26},{4,5},{12,28},{6,7},{14,30},{16,17},{24... | collective-permute-start | bytes 1572872 | tf_op jit(solution)/shard_map/ppermute | solution.py:343
  40.8 1.3 %collective-permute-start.14 = (bf16[2,4,2,32,512]{4,3,2,1,0:T(8,128)(2,1)S(1)}, bf16[2,4,2,32,512]{4,3,2,1,0:T(8,128)(2,1)S(1)}, u32[]{:S(2)}, u32[]{:S(2)}) collective-permute-start(bf16[2,4,2,32,512]{4,3,2,1,0:T(8,128)(2,1)S(1)} %get-tuple-element.77), channel_id=1, source_target_pairs={{0,65},{8,56},{2,67},{10,58},{4,69},{12,60},{6,71},{14,62},{16,81}... | collective-permute-start | bytes 1572872 | tf_op jit(solution)/shard_map/ppermute | solution.py:343
  42.1 2.7 %collective-permute-done.8.refs_2_ = bf16[4,2,2,2,32,512]{5,4,3,2,1,0:T(8,128)(2,1)S(1)} collective-permute-done((bf16[4,2,2,2,32,512]{5,4,3,2,1,0:T(8,128)(2,1)S(1)}, bf16[4,2,2,2,32,512]{5,4,3,2,1,0:T(8,128)(2,1)S(1)}, u32[]{:S(2)}, u32[]{:S(2)}) %collective-permute-start.8) | collective-permute-done | bytes 1048608 | tf_op jit(solution)/shard_map/ppermute | solution.py:343
  44.9 0.1 collective-permute-start.10
  45.0 1.5 %collective-permute-start.11 = (bf16[2,2,2,2,32,512]{5,4,3,2,1,0:T(8,128)(2,1)S(1)}, bf16[2,2,2,2,32,512]{5,4,3,2,1,0:T(8,128)(2,1)S(1)}, u32[]{:S(2)}, u32[]{:S(2)}) collective-permute-start(bf16[2,2,2,2,32,512]{5,4,3,2,1,0:T(8,128)(2,1)S(1)} %slice.23), channel_id=1, source_target_pairs={{0,2},{8,24},{2,4},{10,26},{4,6},{12,28},{6,0},{14,30},{16,18},{24... | collective-permute-start | bytes 1572872 | tf_op jit(solution)/shard_map/ppermute | solution.py:343
  46.5 3.6 %collective-permute-done.13.from_below = bf16[2,4,2,32,512]{4,3,2,1,0:T(8,128)(2,1)S(1)} collective-permute-done((bf16[2,4,2,32,512]{4,3,2,1,0:T(8,128)(2,1)S(1)}, bf16[2,4,2,32,512]{4,3,2,1,0:T(8,128)(2,1)S(1)}, u32[]{:S(2)}, u32[]{:S(2)}) %collective-permute-start.13) | collective-permute-done | bytes 524320 | tf_op jit(solution)/shard_map/ppermute | solution.py:343
  50.2 0.8 pass_on.1
  51.0 0.1 collective-permute-start.15
  51.0 2.7 %collective-permute-start.16 = (bf16[4,4,2,32,512]{4,3,2,1,0:T(8,128)(2,1)S(1)}, bf16[4,4,2,32,512]{4,3,2,1,0:T(8,128)(2,1)S(1)}, u32[]{:S(2)}, u32[]{:S(2)}) collective-permute-start(bf16[4,4,2,32,512]{4,3,2,1,0:T(8,128)(2,1)S(1)} %get-tuple-element.79), channel_id=1, source_target_pairs={{0,65},{8,56},{2,67},{10,58},{4,69},{12,60},{6,71},{14,62},{16,81}... | collective-permute-start | bytes 3145736 | tf_op jit(solution)/shard_map/ppermute | solution.py:343
  53.7 1.0 %collective-permute-done.10.refs_3_ = bf16[2,2,2,2,32,512]{5,4,3,2,1,0:T(8,128)(2,1)S(1)} collective-permute-done((bf16[2,2,2,2,32,512]{5,4,3,2,1,0:T(8,128)(2,1)S(1)}, bf16[2,2,2,2,32,512]{5,4,3,2,1,0:T(8,128)(2,1)S(1)}, u32[]{:S(2)}, u32[]{:S(2)}) %collective-permute-start.10) | collective-permute-done | bytes 524320 | tf_op jit(solution)/shard_map/ppermute | solution.py:343
  54.8 1.3 %collective-permute-done.11.refs_4_ = bf16[2,2,2,2,32,512]{5,4,3,2,1,0:T(8,128)(2,1)S(1)} collective-permute-done((bf16[2,2,2,2,32,512]{5,4,3,2,1,0:T(8,128)(2,1)S(1)}, bf16[2,2,2,2,32,512]{5,4,3,2,1,0:T(8,128)(2,1)S(1)}, u32[]{:S(2)}, u32[]{:S(2)}) %collective-permute-start.11) | collective-permute-done | bytes 524320 | tf_op jit(solution)/shard_map/ppermute | solution.py:343
  56.1 0.5 assemble.1.weights.own
  56.6 3.0 %keys_own_half.1.so_far = f32[512,512]{1,0:T(8,128)S(1)} custom-call(s32[1]{0:T(128)} %bitcast.4.core, bf16[2,8,512,512]{3,2,1,0:T(8,128)(2,1)S(1)} %get-tuple-element.60.normed, bf16[4,2,2,4,2,32,512]{6,5,4,3,2,1,0:T(8,128)(2,1)S(1)} %assemble.1.weights.own), custom_call_target="tpu_custom_call" | custom-call | flops 6442450944 | bytes 12582912 | tf_op jit(solution)/shard_map/keys_own_half/pallas_call | solution.py:268
  59.6 2.4 %collective-permute-start.12 = (bf16[4,2,2,4,2,32,512]{6,5,4,3,2,1,0:T(8,128)(2,1)S(1)}, bf16[4,2,2,4,2,32,512]{6,5,4,3,2,1,0:T(8,128)(2,1)S(1)}, u32[]{:S(2)}, u32[]{:S(2)}) collective-permute-start(bf16[4,2,2,4,2,32,512]{6,5,4,3,2,1,0:T(8,128)(2,1)S(1)} %assemble.1.weights.own), channel_id=1, source_target_pairs={{0,8},{8,0},{1,9},{9,1},{2,10},{10,2},{3,11},{11,3},{4,12},{12,4},... | collective-permute-start | bytes 12582920 | tf_op jit(solution)/shard_map/ppermute | solution.py:351
  62.0 5.3 %collective-permute-done.15.one = bf16[4,4,2,32,512]{4,3,2,1,0:T(8,128)(2,1)S(1)} collective-permute-done((bf16[4,4,2,32,512]{4,3,2,1,0:T(8,128)(2,1)S(1)}, bf16[4,4,2,32,512]{4,3,2,1,0:T(8,128)(2,1)S(1)}, u32[]{:S(2)}, u32[]{:S(2)}) %collective-permute-start.15) | collective-permute-done | bytes 1048608 | tf_op jit(solution)/shard_map/ppermute | solution.py:343
  67.3 0.4 sum_first.1
  67.7 1.4 %collective-permute-start.17 = (bf16[4,2,32,512]{3,2,1,0:T(8,128)(2,1)S(1)}, bf16[4,2,32,512]{3,2,1,0:T(8,128)(2,1)S(1)}, u32[]{:S(2)}, u32[]{:S(2)}) collective-permute-start(bf16[4,2,32,512]{3,2,1,0:T(8,128)(2,1)S(1)} %get-tuple-element.81), channel_id=1, source_target_pairs={{0,32},{8,72},{2,34},{10,74},{4,36},{12,76},{6,38},{14,78},{16,48}... | collective-permute-start | bytes 786440 | tf_op jit(solution)/shard_map/ppermute | solution.py:343
  69.0 1.4 %collective-permute-start.18 = (bf16[4,2,32,512]{3,2,1,0:T(8,128)(2,1)S(1)}, bf16[4,2,32,512]{3,2,1,0:T(8,128)(2,1)S(1)}, u32[]{:S(2)}, u32[]{:S(2)}) collective-permute-start(bf16[4,2,32,512]{3,2,1,0:T(8,128)(2,1)S(1)} %get-tuple-element.82), channel_id=1, source_target_pairs={{0,16},{8,9},{2,18},{10,11},{4,20},{12,13},{6,22},{14,15},{16,32},... | collective-permute-start | bytes 786440 | tf_op jit(solution)/shard_map/ppermute | solution.py:343
  70.4 1.3 %collective-permute-start.19 = (bf16[4,2,32,512]{3,2,1,0:T(8,128)(2,1)S(1)}, bf16[4,2,32,512]{3,2,1,0:T(8,128)(2,1)S(1)}, u32[]{:S(2)}, u32[]{:S(2)}) collective-permute-start(bf16[4,2,32,512]{3,2,1,0:T(8,128)(2,1)S(1)} %get-tuple-element.83), channel_id=1, source_target_pairs={{0,48},{8,73},{2,50},{10,75},{4,52},{12,77},{6,54},{14,79},{16,0},... | collective-permute-start | bytes 786440 | tf_op jit(solution)/shard_map/ppermute | solution.py:343
  71.7 4.4 %keys.1 = (bf16[512,512]{1,0:T(8,128)(2,1)}, f32[512,128]{1,0:T(8,128)S(1)}) custom-call(s32[1]{0:T(128)} %bitcast.4.core, bf16[2,8,512,512]{3,2,1,0:T(8,128)(2,1)S(1)} %get-tuple-element.60.normed, bf16[512,512]{1,0:T(8,128)(2,1)S(1)} %get-tuple-element.61.dpre, f32[512,64]{1,0:T(8,128)S(1)} %get-tuple-element.57.cosine, ...), custom_call_target="tpu_custom_call" | custom-call | flops 2147483648 | bytes 9437184 | tf_op jit(solution)/shard_map/keys/pallas_call | solution.py:293
  76.1 1.5 %collective-permute-done.18.three = bf16[4,2,32,512]{3,2,1,0:T(8,128)(2,1)S(1)} collective-permute-done((bf16[4,2,32,512]{3,2,1,0:T(8,128)(2,1)S(1)}, bf16[4,2,32,512]{3,2,1,0:T(8,128)(2,1)S(1)}, u32[]{:S(2)}, u32[]{:S(2)}) %collective-permute-start.18) | collective-permute-done | bytes 262176 | tf_op jit(solution)/shard_map/ppermute | solution.py:343
  77.6 0.1 sum_second.1
  77.7 3.7 %collective-permute-start.20 = (bf16[2,32,512]{2,1,0:T(8,128)(2,1)S(1)}, bf16[2,32,512]{2,1,0:T(8,128)(2,1)S(1)}, u32[]{:S(2)}, u32[]{:S(2)}) collective-permute-start(bf16[2,32,512]{2,1,0:T(8,128)(2,1)S(1)} %get-tuple-element.90), channel_id=1, source_target_pairs={{0,4},{8,12},{2,6},{10,14},{4,0},{12,8},{6,2},{14,10},{16,20},{24,... | collective-permute-start | bytes 196616 | tf_op jit(solution)/shard_map/ppermute | solution.py:343
  81.4 0.7 collective-permute-start.21
  82.1 1.9 %collective-permute-start.22 = (bf16[2,32,512]{2,1,0:T(8,128)(2,1)S(1)}, bf16[2,32,512]{2,1,0:T(8,128)(2,1)S(1)}, u32[]{:S(2)}, u32[]{:S(2)}) collective-permute-start(bf16[2,32,512]{2,1,0:T(8,128)(2,1)S(1)} %get-tuple-element.92), channel_id=1, source_target_pairs={{0,6},{8,14},{2,0},{10,8},{4,2},{12,10},{6,4},{14,12},{16,22},{24,... | collective-permute-start | bytes 196616 | tf_op jit(solution)/shard_map/ppermute | solution.py:343
  84.1 8.8 %input_gradient.1 = bf16[512,8192]{1,0:T(8,128)(2,1)} custom-call(s32[1]{0:T(128)} %bitcast.4.core, bf16[2,8,512,512]{3,2,1,0:T(8,128)(2,1)S(1)} %get-tuple-element.60.normed, bf16[512,512]{1,0:T(8,128)(2,1)S(1)} %get-tuple-element.61.dpre, f32[512,128]{1,0:T(8,128)S(1)} %get-tuple-element.93.inv, f32[512,128]{1,0:T(8,128)S(1)} %get-tuple-element.94.coef, ...), custom_call_target="tpu_custom_call" | custom-call | flops 4294967296 | bytes 18874368 | tf_op jit(solution)/shard_map/input_gradient/pallas_call | solution.py:321
  93.0 2.0 %collective-permute-start.23 = (f32[32,512]{1,0:T(8,128)S(1)}, f32[32,512]{1,0:T(8,128)S(1)}, u32[]{:S(2)}, u32[]{:S(2)}) collective-permute-start(f32[32,512]{1,0:T(8,128)S(1)} %get-tuple-element.106), channel_id=1, source_target_pairs={{0,8},{8,0},{1,9},{9,1},{2,10},{10,2},{3,11},{11,3},{4,12},{12,4},... | collective-permute-start | bytes 196616 | tf_op jit(solution)/shard_map/ppermute | solution.py:351
  95.0 0.9 collective-permute-done.23
  96.0 0.7 fusion
  (23 shorter events, 0.3 us)
Async XLA Ops:
  1.4 2.5 %collective-permute-start = (bf16[32,512]{1,0:T(8,128)(2,1)S(1)}, bf16[32,512]{1,0:T(8,128)(2,1)S(1)}, u32[]{:S(2)}, u32[]{:S(2)}) collective-permute-start(bf16[32,512]{1,0:T(8,128)(2,1)S(1)} %get-tuple-element.108), channel_id=1, source_target_pairs={{0,8},{8,0},{1,9},{9,1},{2,10},{10,2},{3,11},{11,3},{4,12},{12,4},... | collective-permute-start | bytes 98312 | tf_op jit(solution)/shard_map/ppermute | solution.py:351
  4.0 10.6 %collective-permute-start.1 = (bf16[2,32,512]{2,1,0:T(8,128)(2,1)S(1)}, bf16[2,32,512]{2,1,0:T(8,128)(2,1)S(1)}, u32[]{:S(2)}, u32[]{:S(2)}) collective-permute-start(bf16[2,32,512]{2,1,0:T(8,128)(2,1)S(1)} %maximum_select_fusion.1), channel_id=1, source_target_pairs={{0,65},{8,73},{2,67},{10,75},{4,69},{12,77},{6,71},{14,79},{16,81}... | collective-permute-start | bytes 196616 | tf_op jit(solution)/shard_map/ppermute | solution.py:343
  6.6 8.0 %collective-permute-start.2 = (bf16[2,32,512]{2,1,0:T(8,128)(2,1)S(1)}, bf16[2,32,512]{2,1,0:T(8,128)(2,1)S(1)}, u32[]{:S(2)}, u32[]{:S(2)}) collective-permute-start(bf16[2,32,512]{2,1,0:T(8,128)(2,1)S(1)} %maximum_select_fusion.1), channel_id=1, source_target_pairs={{0,64},{8,72},{2,66},{10,74},{4,68},{12,76},{6,70},{14,78},{16,80}... | collective-permute-start | bytes 196616 | tf_op jit(solution)/shard_map/ppermute | solution.py:343
  7.1 7.5 %collective-permute-start.3 = (bf16[2,32,512]{2,1,0:T(8,128)(2,1)S(1)}, bf16[2,32,512]{2,1,0:T(8,128)(2,1)S(1)}, u32[]{:S(2)}, u32[]{:S(2)}) collective-permute-start(bf16[2,32,512]{2,1,0:T(8,128)(2,1)S(1)} %maximum_select_fusion.1), channel_id=1, source_target_pairs={{0,1},{8,9},{2,3},{10,11},{4,5},{12,13},{6,7},{14,15},{16,17},{24,... | collective-permute-start | bytes 196616 | tf_op jit(solution)/shard_map/ppermute | solution.py:343
  14.7 9.3 %collective-permute-start.6 = (bf16[2,2,2,32,512]{4,3,2,1,0:T(8,128)(2,1)S(1)}, bf16[2,2,2,32,512]{4,3,2,1,0:T(8,128)(2,1)S(1)}, u32[]{:S(2)}, u32[]{:S(2)}) collective-permute-start(bf16[2,2,2,32,512]{4,3,2,1,0:T(8,128)(2,1)S(1)} %bitcast.29), channel_id=1, source_target_pairs={{0,16},{8,10},{2,18},{10,12},{4,20},{12,14},{6,22},{14,8},{16,32},... | collective-permute-start | bytes 786440 | tf_op jit(solution)/shard_map/ppermute | solution.py:343
  16.4 10.2 %collective-permute-start.5 = (bf16[2,2,2,32,512]{4,3,2,1,0:T(8,128)(2,1)S(1)}, bf16[2,2,2,32,512]{4,3,2,1,0:T(8,128)(2,1)S(1)}, u32[]{:S(2)}, u32[]{:S(2)}) collective-permute-start(bf16[2,2,2,32,512]{4,3,2,1,0:T(8,128)(2,1)S(1)} %bitcast.30), channel_id=1, source_target_pairs={{0,32},{8,12},{2,34},{10,14},{4,36},{12,8},{6,38},{14,10},{16,48},... | collective-permute-start | bytes 786440 | tf_op jit(solution)/shard_map/ppermute | solution.py:343
  19.7 6.9 %collective-permute-start.4 = (bf16[2,2,2,32,512]{4,3,2,1,0:T(8,128)(2,1)S(1)}, bf16[2,2,2,32,512]{4,3,2,1,0:T(8,128)(2,1)S(1)}, u32[]{:S(2)}, u32[]{:S(2)}) collective-permute-start(bf16[2,2,2,32,512]{4,3,2,1,0:T(8,128)(2,1)S(1)} %bitcast.31), channel_id=1, source_target_pairs={{0,48},{8,14},{2,50},{10,8},{4,52},{12,10},{6,54},{14,12},{16,0},{... | collective-permute-start | bytes 786440 | tf_op jit(solution)/shard_map/ppermute | solution.py:343
  26.7 7.7 %collective-permute-start.9 = (bf16[8,16,32,512]{3,2,1,0:T(8,128)(2,1)S(1)}, bf16[8,16,32,512]{3,2,1,0:T(8,128)(2,1)S(1)}, u32[]{:S(2)}, u32[]{:S(2)}) collective-permute-start(bf16[8,16,32,512]{3,2,1,0:T(8,128)(2,1)S(1)} %send_half.1), channel_id=1, source_target_pairs={{0,8},{8,0},{1,9},{9,1},{2,10},{10,2},{3,11},{11,3},{4,12},{12,4},... | collective-permute-start | bytes 12582920 | tf_op jit(solution)/shard_map/ppermute | solution.py:351
  27.7 14.5 %collective-permute-start.7 = (bf16[4,2,2,2,32,512]{5,4,3,2,1,0:T(8,128)(2,1)S(1)}, bf16[4,2,2,2,32,512]{5,4,3,2,1,0:T(8,128)(2,1)S(1)}, u32[]{:S(2)}, u32[]{:S(2)}) collective-permute-start(bf16[4,2,2,2,32,512]{5,4,3,2,1,0:T(8,128)(2,1)S(1)} %pad_maximum_fusion.refs_0_), channel_id=1, source_target_pairs={{0,6},{8,56},{2,0},{10,58},{4,2},{12,60},{6,4},{14,62},{16,22},{24... | collective-permute-start | bytes 3145736 | tf_op jit(solution)/shard_map/ppermute | solution.py:343
  29.7 15.2 %collective-permute-start.8 = (bf16[4,2,2,2,32,512]{5,4,3,2,1,0:T(8,128)(2,1)S(1)}, bf16[4,2,2,2,32,512]{5,4,3,2,1,0:T(8,128)(2,1)S(1)}, u32[]{:S(2)}, u32[]{:S(2)}) collective-permute-start(bf16[4,2,2,2,32,512]{5,4,3,2,1,0:T(8,128)(2,1)S(1)} %pad_maximum_fusion.refs_0_), channel_id=1, source_target_pairs={{0,2},{8,24},{2,4},{10,26},{4,6},{12,28},{6,0},{14,30},{16,18},{24... | collective-permute-start | bytes 3145736 | tf_op jit(solution)/shard_map/ppermute | solution.py:343
  39.4 10.8 %collective-permute-start.13 = (bf16[2,4,2,32,512]{4,3,2,1,0:T(8,128)(2,1)S(1)}, bf16[2,4,2,32,512]{4,3,2,1,0:T(8,128)(2,1)S(1)}, u32[]{:S(2)}, u32[]{:S(2)}) collective-permute-start(bf16[2,4,2,32,512]{4,3,2,1,0:T(8,128)(2,1)S(1)} %get-tuple-element.76), channel_id=1, source_target_pairs={{0,1},{8,24},{2,3},{10,26},{4,5},{12,28},{6,7},{14,30},{16,17},{24... | collective-permute-start | bytes 1572872 | tf_op jit(solution)/shard_map/ppermute | solution.py:343
  40.8 9.3 %collective-permute-start.14 = (bf16[2,4,2,32,512]{4,3,2,1,0:T(8,128)(2,1)S(1)}, bf16[2,4,2,32,512]{4,3,2,1,0:T(8,128)(2,1)S(1)}, u32[]{:S(2)}, u32[]{:S(2)}) collective-permute-start(bf16[2,4,2,32,512]{4,3,2,1,0:T(8,128)(2,1)S(1)} %get-tuple-element.77), channel_id=1, source_target_pairs={{0,65},{8,56},{2,67},{10,58},{4,69},{12,60},{6,71},{14,62},{16,81}... | collective-permute-start | bytes 1572872 | tf_op jit(solution)/shard_map/ppermute | solution.py:343
  44.9 9.9 %collective-permute-start.10 = (bf16[2,2,2,2,32,512]{5,4,3,2,1,0:T(8,128)(2,1)S(1)}, bf16[2,2,2,2,32,512]{5,4,3,2,1,0:T(8,128)(2,1)S(1)}, u32[]{:S(2)}, u32[]{:S(2)}) collective-permute-start(bf16[2,2,2,2,32,512]{5,4,3,2,1,0:T(8,128)(2,1)S(1)} %slice.22), channel_id=1, source_target_pairs={{0,6},{8,56},{2,0},{10,58},{4,2},{12,60},{6,4},{14,62},{16,22},{24... | collective-permute-start | bytes 1572872 | tf_op jit(solution)/shard_map/ppermute | solution.py:343
  45.0 11.1 %collective-permute-start.11 = (bf16[2,2,2,2,32,512]{5,4,3,2,1,0:T(8,128)(2,1)S(1)}, bf16[2,2,2,2,32,512]{5,4,3,2,1,0:T(8,128)(2,1)S(1)}, u32[]{:S(2)}, u32[]{:S(2)}) collective-permute-start(bf16[2,2,2,2,32,512]{5,4,3,2,1,0:T(8,128)(2,1)S(1)} %slice.23), channel_id=1, source_target_pairs={{0,2},{8,24},{2,4},{10,26},{4,6},{12,28},{6,0},{14,30},{16,18},{24... | collective-permute-start | bytes 1572872 | tf_op jit(solution)/shard_map/ppermute | solution.py:343
  51.0 16.3 %collective-permute-start.15 = (bf16[4,4,2,32,512]{4,3,2,1,0:T(8,128)(2,1)S(1)}, bf16[4,4,2,32,512]{4,3,2,1,0:T(8,128)(2,1)S(1)}, u32[]{:S(2)}, u32[]{:S(2)}) collective-permute-start(bf16[4,4,2,32,512]{4,3,2,1,0:T(8,128)(2,1)S(1)} %get-tuple-element.78), channel_id=1, source_target_pairs={{0,1},{8,24},{2,3},{10,26},{4,5},{12,28},{6,7},{14,30},{16,17},{24... | collective-permute-start | bytes 3145736 | tf_op jit(solution)/shard_map/ppermute | solution.py:343
  51.0 16.3 %collective-permute-start.16 = (bf16[4,4,2,32,512]{4,3,2,1,0:T(8,128)(2,1)S(1)}, bf16[4,4,2,32,512]{4,3,2,1,0:T(8,128)(2,1)S(1)}, u32[]{:S(2)}, u32[]{:S(2)}) collective-permute-start(bf16[4,4,2,32,512]{4,3,2,1,0:T(8,128)(2,1)S(1)} %get-tuple-element.79), channel_id=1, source_target_pairs={{0,65},{8,56},{2,67},{10,58},{4,69},{12,60},{6,71},{14,62},{16,81}... | collective-permute-start | bytes 3145736 | tf_op jit(solution)/shard_map/ppermute | solution.py:343
  59.6 12.1 %collective-permute-start.12 = (bf16[4,2,2,4,2,32,512]{6,5,4,3,2,1,0:T(8,128)(2,1)S(1)}, bf16[4,2,2,4,2,32,512]{6,5,4,3,2,1,0:T(8,128)(2,1)S(1)}, u32[]{:S(2)}, u32[]{:S(2)}) collective-permute-start(bf16[4,2,2,4,2,32,512]{6,5,4,3,2,1,0:T(8,128)(2,1)S(1)} %assemble.1.weights.own), channel_id=1, source_target_pairs={{0,8},{8,0},{1,9},{9,1},{2,10},{10,2},{3,11},{11,3},{4,12},{12,4},... | collective-permute-start | bytes 12582920 | tf_op jit(solution)/shard_map/ppermute | solution.py:351
  67.7 8.4 %collective-permute-start.17 = (bf16[4,2,32,512]{3,2,1,0:T(8,128)(2,1)S(1)}, bf16[4,2,32,512]{3,2,1,0:T(8,128)(2,1)S(1)}, u32[]{:S(2)}, u32[]{:S(2)}) collective-permute-start(bf16[4,2,32,512]{3,2,1,0:T(8,128)(2,1)S(1)} %get-tuple-element.81), channel_id=1, source_target_pairs={{0,32},{8,72},{2,34},{10,74},{4,36},{12,76},{6,38},{14,78},{16,48}... | collective-permute-start | bytes 786440 | tf_op jit(solution)/shard_map/ppermute | solution.py:343
  69.0 8.6 %collective-permute-start.18 = (bf16[4,2,32,512]{3,2,1,0:T(8,128)(2,1)S(1)}, bf16[4,2,32,512]{3,2,1,0:T(8,128)(2,1)S(1)}, u32[]{:S(2)}, u32[]{:S(2)}) collective-permute-start(bf16[4,2,32,512]{3,2,1,0:T(8,128)(2,1)S(1)} %get-tuple-element.82), channel_id=1, source_target_pairs={{0,16},{8,9},{2,18},{10,11},{4,20},{12,13},{6,22},{14,15},{16,32},... | collective-permute-start | bytes 786440 | tf_op jit(solution)/shard_map/ppermute | solution.py:343
  70.4 7.2 %collective-permute-start.19 = (bf16[4,2,32,512]{3,2,1,0:T(8,128)(2,1)S(1)}, bf16[4,2,32,512]{3,2,1,0:T(8,128)(2,1)S(1)}, u32[]{:S(2)}, u32[]{:S(2)}) collective-permute-start(bf16[4,2,32,512]{3,2,1,0:T(8,128)(2,1)S(1)} %get-tuple-element.83), channel_id=1, source_target_pairs={{0,48},{8,73},{2,50},{10,75},{4,52},{12,77},{6,54},{14,79},{16,0},... | collective-permute-start | bytes 786440 | tf_op jit(solution)/shard_map/ppermute | solution.py:343
  77.7 15.2 %collective-permute-start.20 = (bf16[2,32,512]{2,1,0:T(8,128)(2,1)S(1)}, bf16[2,32,512]{2,1,0:T(8,128)(2,1)S(1)}, u32[]{:S(2)}, u32[]{:S(2)}) collective-permute-start(bf16[2,32,512]{2,1,0:T(8,128)(2,1)S(1)} %get-tuple-element.90), channel_id=1, source_target_pairs={{0,4},{8,12},{2,6},{10,14},{4,0},{12,8},{6,2},{14,10},{16,20},{24,... | collective-permute-start | bytes 196616 | tf_op jit(solution)/shard_map/ppermute | solution.py:343
  81.4 11.5 %collective-permute-start.21 = (bf16[2,32,512]{2,1,0:T(8,128)(2,1)S(1)}, bf16[2,32,512]{2,1,0:T(8,128)(2,1)S(1)}, u32[]{:S(2)}, u32[]{:S(2)}) collective-permute-start(bf16[2,32,512]{2,1,0:T(8,128)(2,1)S(1)} %get-tuple-element.91), channel_id=1, source_target_pairs={{0,2},{8,10},{2,4},{10,12},{4,6},{12,14},{6,0},{14,8},{16,18},{24,... | collective-permute-start | bytes 196616 | tf_op jit(solution)/shard_map/ppermute | solution.py:343
  82.1 10.8 %collective-permute-start.22 = (bf16[2,32,512]{2,1,0:T(8,128)(2,1)S(1)}, bf16[2,32,512]{2,1,0:T(8,128)(2,1)S(1)}, u32[]{:S(2)}, u32[]{:S(2)}) collective-permute-start(bf16[2,32,512]{2,1,0:T(8,128)(2,1)S(1)} %get-tuple-element.92), channel_id=1, source_target_pairs={{0,6},{8,14},{2,0},{10,8},{4,2},{12,10},{6,4},{14,12},{16,22},{24,... | collective-permute-start | bytes 196616 | tf_op jit(solution)/shard_map/ppermute | solution.py:343
  93.0 2.9 %collective-permute-start.23 = (f32[32,512]{1,0:T(8,128)S(1)}, f32[32,512]{1,0:T(8,128)S(1)}, u32[]{:S(2)}, u32[]{:S(2)}) collective-permute-start(f32[32,512]{1,0:T(8,128)S(1)} %get-tuple-element.106), channel_id=1, source_target_pairs={{0,8},{8,0},{1,9},{9,1},{2,10},{10,2},{3,11},{11,3},{4,12},{12,4},... | collective-permute-start | bytes 196616 | tf_op jit(solution)/shard_map/ppermute | solution.py:351

commit v3 on v2

--- a/solution.py
+++ b/solution.py
@@ -99,33 +99,27 @@
     )
 
 
-def send_kernel(core, normed, dpre_t, out):
-    @pl.loop(0, STEPS)
-    def _(i):
-        term = jnp.dot(dpre_t[...], normed[1 - core[0], i], preferred_element_type=F32)
-        out[i] = term.astype(BF16).reshape(16, 32, LANES)
-
-
-def send_call(core, normed, dpre_t):
-    return pl.pallas_call(
-        send_kernel,
+def terms_call(core, normed, dpre_t, other):
+    def kernel(core, normed, dpre_t, out):
+        half = 1 - core[0] if other else core[0]
+
+        @pl.loop(0, STEPS)
+        def _(i):
+            term = jnp.dot(dpre_t[...], normed[half, i], preferred_element_type=F32)
+            out[i] = term.astype(BF16).reshape(16, 32, LANES)
+
+    return pl.pallas_call(
+        kernel,
         in_specs=[SMEM, VMEM, VMEM],
         out_specs=VMEM,
         out_shape=pltpu.VMEM((STEPS, 16, 32, LANES), BF16),
         compiler_params=params(8),
         cost_estimate=pl.CostEstimate(flops=ROWS * D * KV, bytes_accessed=9 * MIB, transcendentals=0),
-        name="send_half",
+        name="send_half" if other else "keep_half",
     )(core, stay(normed), stay(dpre_t))
 
 
-def keep_kernel(core, x, y, normed, dpre_t, came, *rest):
-    (own, up, down, far_up, far_down), total = rest[:5], rest[5]
-
-    @pl.loop(0, STEPS)
-    def _(i):
-        term = jnp.dot(dpre_t[...], normed[core[0], i], preferred_element_type=F32)
-        total[i] = (term.reshape(16, 32, LANES) + came[i].astype(F32)).astype(BF16)
-
+def add_kernel(core, x, y, kept, came, own, up, down, far_up, far_down):
     first = core[0] == 0
 
     @pl.loop(0, 16)
@@ -134,7 +128,8 @@
         for r in range(4):
             x_at = jnp.where(first, (x[0] + r) % 4, a)
             y_at = jnp.where(first, a, (y[0] + r) % 4)
-            block = total[2 * b + x_at % 2, pl.ds(8 * (x_at // 2) + 2 * y_at, 2)]
+            at = (2 * b + x_at % 2, pl.ds(8 * (x_at // 2) + 2 * y_at, 2))
+            block = kept[at] + came[at]
             if r != 2:
                 {0: own, 1: up, 3: down}[r][a, b] = block
                 continue
@@ -148,18 +143,17 @@
                 far_down[a - 2, b] = block
 
 
-def keep_call(core, x, y, normed, dpre_t, came):
+def add_call(core, x, y, kept, came):
     part, half = (4, 4, 2, 32, LANES), (2, 4, 2, 32, LANES)
     return pl.pallas_call(
-        keep_kernel,
-        in_specs=[SMEM] * 3 + [VMEM] * 3,
+        add_kernel,
+        in_specs=[SMEM] * 3 + [VMEM] * 2,
         out_specs=[VMEM] * 5,
         out_shape=[pltpu.VMEM(part, BF16)] * 3 + [pltpu.VMEM(half, BF16)] * 2,
-        scratch_shapes=[pltpu.VMEM((STEPS, 16, 32, LANES), BF16)],
         compiler_params=params(16),
-        cost_estimate=pl.CostEstimate(flops=ROWS * D * KV, bytes_accessed=13 * MIB, transcendentals=0),
-        name="keep_half",
-    )(core, x, y, stay(normed), stay(dpre_t), stay(came))
+        cost_estimate=pl.CostEstimate(flops=0, bytes_accessed=12 * MIB, transcendentals=0),
+        name="add_cores",
+    )(core, x, y, stay(kept), stay(came))
 
 
 def pass_on_kernel(up, down, from_below, from_above, up_out, down_out):
@@ -378,12 +372,13 @@
 
     near, normed = barrier((near, normed))
     line = jnp.stack([near] + [hop(near, Y, Z, -r) for r in (1, 2, 3)])
-    send = send_call(core, normed, dpre_t)
+    send = terms_call(core, normed, dpre_t, True)
 
     line, send = barrier((line, send))
     above, below = hop(line, Z, Y, -1), hop(line, Z, Y, 1)
     came = swap_cores(send)
-    own, up, down, far_up, far_down = keep_call(core, x, y, normed, dpre_t, came)
+    kept = terms_call(core, normed, dpre_t, False)
+    own, up, down, far_up, far_down = add_call(core, x, y, kept, came)
 
     from_below, from_above = hop(far_up, X, Y, 1), hop(far_down, X, Y, -1)
     above, below = barrier((above, below, own))[:2]

time: 96.8 us -> 94.5 us (0.976)
  starting transfers between devices: 35.9 us -> 33.9 us
    ppermute x4, waiting for transfers between devices: 5.68 us -> 2.5 us  [swap_cores(): return lax.ppermute(value, 'c', [(0, 1), (1, 0)])]
    ppermute x20, waiting for transfers between devices: 18.1 us -> 20.8 us  [hop(): return lax.ppermute(value, AXES, pairs)]
    ppermute x4, starting transfers between devices: 6.89 us -> 4.94 us  [swap_cores(): return lax.ppermute(value, 'c', [(0, 1), (1, 0)])]
    pallas_call x2 -> x3, Pallas kernels: 8.44 us -> 8.59 us  [the longest x2 7.02 us: terms_call(): pl.pallas_call(kernel, in_specs=[SMEM, VMEM, VMEM], out_specs=VMEM, out_s...]
  transfers between devices with their start and end apart: 24 -> 24, of which waited for: 9 -> 9; matrix products, arithmetic and copies ran while one was open for 1% -> 1% of each run, Pallas kernels for 34% -> 35%
where the time goes in v3:
time: 94.5 us; the launch traced here: 94.3 us
  starting transfers between devices  33.9 us (36%)
  Pallas kernels  33.4 us (35%)
  waiting for transfers between devices  23.3 us (25%)
  other arithmetic  2.73 us (3%)
    ppermute x20, starting transfers between devices, hop(): return lax.ppermute(value, AXES, pairs)  29 us
    ppermute x20, waiting for transfers between devices, hop(): return lax.ppermute(value, AXES, pairs)  20.8 us
    pallas_call x1, Pallas kernels, grad_call(): pl.pallas_call(grad_kernel, grid=(STEPS,), in_specs=[SMEM] + [VMEM] * 6,...  8.7 us
    pallas_call x2, Pallas kernels, terms_call(): pl.pallas_call(kernel, in_specs=[SMEM, VMEM, VMEM], out_specs=VMEM, out_s...  7.02 us
    pallas_call x1, Pallas kernels, prepare_call(): pl.pallas_call(prepare_kernel, grid=(ROWS // 128,), in_specs=[rows(D), ro...  6.88 us
    ppermute x4, starting transfers between devices, swap_cores(): return lax.ppermute(value, 'c', [(0, 1), (1, 0)])  4.94 us
    pallas_call x1, Pallas kernels, keys_call(): pl.pallas_call(keys_kernel, in_specs=[SMEM] + [VMEM] * 6, out_specs=[VMEM...  4.41 us
    pallas_call x1, Pallas kernels, own_call(): pl.pallas_call(own_kernel, in_specs=[SMEM] + [VMEM] * 2, out_specs=VMEM,...  3.02 us
  transfers between devices with their start and end apart: 24, of which 9 were waited for; matrix products, arithmetic and copies ran while one was open for 1% of the time, Pallas kernels for 35%

profile of v3, /device:TPU:1, one launch (start us, length us, event | category | flops | bytes accessed | tf_op | source)
XLA Modules:
  0.0 94.3 jit_solution(3240062579864907588)
XLA Ops:
  0.6 0.8 slice_bitcast_fusion
  1.4 1.5 %collective-permute-start = (bf16[32,512]{1,0:T(8,128)(2,1)S(1)}, bf16[32,512]{1,0:T(8,128)(2,1)S(1)}, u32[]{:S(2)}, u32[]{:S(2)}) collective-permute-start(bf16[32,512]{1,0:T(8,128)(2,1)S(1)} %get-tuple-element.108), channel_id=1, source_target_pairs={{0,8},{8,0},{1,9},{9,1},{2,10},{10,2},{3,11},{11,3},{4,12},{12,4},... | collective-permute-start | bytes 98312 | tf_op jit(solution)/shard_map/ppermute | solution.py:345
  2.9 1.0 %multiply_sine_fusion = (f32[512,64]{1,0:T(8,128)S(1)}, f32[512,64]{1,0:T(8,128)S(1)}) fusion(f32[64]{0:T(128)S(1)} %multiply_exponential_fusion, f32[512]{0:T(512)S(1)} %fusion.2), kind=kLoop, calls=%fused_computation.1 | loop fusion | flops 32768 | bytes 264448 | tf_op jit(solution)/shard_map/sin | solution.py:31
  3.9 0.0 collective-permute-done
  4.0 2.6 %collective-permute-start.1 = (bf16[2,32,512]{2,1,0:T(8,128)(2,1)S(1)}, bf16[2,32,512]{2,1,0:T(8,128)(2,1)S(1)}, u32[]{:S(2)}, u32[]{:S(2)}) collective-permute-start(bf16[2,32,512]{2,1,0:T(8,128)(2,1)S(1)} %maximum_select_fusion.1), channel_id=1, source_target_pairs={{0,65},{8,73},{2,67},{10,75},{4,69},{12,77},{6,71},{14,79},{16,81}... | collective-permute-start | bytes 196616 | tf_op jit(solution)/shard_map/ppermute | solution.py:337
  6.6 0.5 collective-permute-start.2
  7.1 0.6 collective-permute-start.3
  7.7 6.9 %row_scales.1 = (bf16[2,8,512,512]{3,2,1,0:T(8,128)(2,1)S(1)}, f32[512,128]{1,0:T(8,128)S(1)}, bf16[512,512]{1,0:T(8,128)(2,1)S(1)}, bf16[512,512]{1,0:T(8,128)(2,1)S(1)}) custom-call(bf16[512,8192]{1,0:T(8,128)(2,1)} %x, bf16[512,512]{1,0:T(8,128)(2,1)} %cot.1, f32[512,64]{1,0:T(8,128)S(1)} %get-tuple-element.57.cosine, f32[512,64]{1,0:T(8,128)S(1)} %get-tuple-element.58.sine), custom_call_target="tpu_custom_call" | custom-call | flops 41943040 | bytes 18874368 | tf_op jit(solution)/shard_map/row_scales/pallas_call | solution.py:80
  14.7 1.7 %collective-permute-start.6 = (bf16[2,2,2,32,512]{4,3,2,1,0:T(8,128)(2,1)S(1)}, bf16[2,2,2,32,512]{4,3,2,1,0:T(8,128)(2,1)S(1)}, u32[]{:S(2)}, u32[]{:S(2)}) collective-permute-start(bf16[2,2,2,32,512]{4,3,2,1,0:T(8,128)(2,1)S(1)} %bitcast.29), channel_id=1, source_target_pairs={{0,16},{8,10},{2,18},{10,12},{4,20},{12,14},{6,22},{14,8},{16,32},... | collective-permute-start | bytes 786440 | tf_op jit(solution)/shard_map/ppermute | solution.py:337
  16.4 3.3 %collective-permute-start.5 = (bf16[2,2,2,32,512]{4,3,2,1,0:T(8,128)(2,1)S(1)}, bf16[2,2,2,32,512]{4,3,2,1,0:T(8,128)(2,1)S(1)}, u32[]{:S(2)}, u32[]{:S(2)}) collective-permute-start(bf16[2,2,2,32,512]{4,3,2,1,0:T(8,128)(2,1)S(1)} %bitcast.30), channel_id=1, source_target_pairs={{0,32},{8,12},{2,34},{10,14},{4,36},{12,8},{6,38},{14,10},{16,48},... | collective-permute-start | bytes 786440 | tf_op jit(solution)/shard_map/ppermute | solution.py:337
  19.7 0.7 collective-permute-start.4
  20.5 3.5 %send_half.1 = bf16[8,16,32,512]{3,2,1,0:T(8,128)(2,1)S(1)} custom-call(s32[1]{0:T(128)} %bitcast.4.core, bf16[2,8,512,512]{3,2,1,0:T(8,128)(2,1)S(1)} %get-tuple-element.60.normed, bf16[512,512]{1,0:T(8,128)(2,1)S(1)} %get-tuple-element.65.dpre_t), custom_call_target="tpu_custom_call" | custom-call | flops 2147483648 | bytes 9437184 | tf_op jit(solution)/shard_map/send_half/pallas_call | solution.py:111
  24.0 2.6 %collective-permute-done.5 = bf16[2,2,2,32,512]{4,3,2,1,0:T(8,128)(2,1)S(1)} collective-permute-done((bf16[2,2,2,32,512]{4,3,2,1,0:T(8,128)(2,1)S(1)}, bf16[2,2,2,32,512]{4,3,2,1,0:T(8,128)(2,1)S(1)}, u32[]{:S(2)}, u32[]{:S(2)}) %collective-permute-start.5) | collective-permute-done | bytes 262176 | tf_op jit(solution)/shard_map/ppermute | solution.py:337
  26.6 0.1 pad_maximum_fusion.refs_0_
  26.7 0.9 collective-permute-start.9
  27.7 2.0 %collective-permute-start.7 = (bf16[4,2,2,2,32,512]{5,4,3,2,1,0:T(8,128)(2,1)S(1)}, bf16[4,2,2,2,32,512]{5,4,3,2,1,0:T(8,128)(2,1)S(1)}, u32[]{:S(2)}, u32[]{:S(2)}) collective-permute-start(bf16[4,2,2,2,32,512]{5,4,3,2,1,0:T(8,128)(2,1)S(1)} %pad_maximum_fusion.refs_0_), channel_id=1, source_target_pairs={{0,6},{8,56},{2,0},{10,58},{4,2},{12,60},{6,4},{14,62},{16,22},{24... | collective-permute-start | bytes 3145736 | tf_op jit(solution)/shard_map/ppermute | solution.py:337
  29.7 3.5 %keep_half.1.kept = bf16[8,16,32,512]{3,2,1,0:T(8,128)(2,1)S(1)} custom-call(s32[1]{0:T(128)} %bitcast.4.core, bf16[2,8,512,512]{3,2,1,0:T(8,128)(2,1)S(1)} %get-tuple-element.60.normed, bf16[512,512]{1,0:T(8,128)(2,1)S(1)} %get-tuple-element.65.dpre_t), custom_call_target="tpu_custom_call" | custom-call | flops 2147483648 | bytes 9437184 | tf_op jit(solution)/shard_map/keep_half/pallas_call | solution.py:111
  33.2 1.3 %collective-permute-done.9.came = bf16[8,16,32,512]{3,2,1,0:T(8,128)(2,1)S(1)} collective-permute-done((bf16[8,16,32,512]{3,2,1,0:T(8,128)(2,1)S(1)}, bf16[8,16,32,512]{3,2,1,0:T(8,128)(2,1)S(1)}, u32[]{:S(2)}, u32[]{:S(2)}) %collective-permute-start.9) | collective-permute-done | bytes 4194336 | tf_op jit(solution)/shard_map/ppermute | solution.py:345
  34.5 1.6 %add_cores.1 = (bf16[4,4,2,32,512]{4,3,2,1,0:T(8,128)(2,1)S(1)}, bf16[4,4,2,32,512]{4,3,2,1,0:T(8,128)(2,1)S(1)}, bf16[4,4,2,32,512]{4,3,2,1,0:T(8,128)(2,1)S(1)...) custom-call(s32[1]{0:T(128)} %bitcast.4.core, s32[1]{0:T(128)} %bitcast.7.x, s32[1]{0:T(128)} %bitcast.5.y, ...), custom_call_target="tpu_custom_call" | custom-call | bytes 12582912 | tf_op jit(solution)/shard_map/add_cores/pallas_call | solution.py:148
  36.0 1.4 %collective-permute-start.13 = (bf16[2,4,2,32,512]{4,3,2,1,0:T(8,128)(2,1)S(1)}, bf16[2,4,2,32,512]{4,3,2,1,0:T(8,128)(2,1)S(1)}, u32[]{:S(2)}, u32[]{:S(2)}) collective-permute-start(bf16[2,4,2,32,512]{4,3,2,1,0:T(8,128)(2,1)S(1)} %get-tuple-element.76), channel_id=1, source_target_pairs={{0,1},{8,24},{2,3},{10,26},{4,5},{12,28},{6,7},{14,30},{16,17},{24... | collective-permute-start | bytes 1572872 | tf_op jit(solution)/shard_map/ppermute | solution.py:337
  37.5 1.3 %collective-permute-start.14 = (bf16[2,4,2,32,512]{4,3,2,1,0:T(8,128)(2,1)S(1)}, bf16[2,4,2,32,512]{4,3,2,1,0:T(8,128)(2,1)S(1)}, u32[]{:S(2)}, u32[]{:S(2)}) collective-permute-start(bf16[2,4,2,32,512]{4,3,2,1,0:T(8,128)(2,1)S(1)} %get-tuple-element.77), channel_id=1, source_target_pairs={{0,65},{8,56},{2,67},{10,58},{4,69},{12,60},{6,71},{14,62},{16,81}... | collective-permute-start | bytes 1572872 | tf_op jit(solution)/shard_map/ppermute | solution.py:337
  38.8 2.8 %collective-permute-done.7.refs_1_ = bf16[4,2,2,2,32,512]{5,4,3,2,1,0:T(8,128)(2,1)S(1)} collective-permute-done((bf16[4,2,2,2,32,512]{5,4,3,2,1,0:T(8,128)(2,1)S(1)}, bf16[4,2,2,2,32,512]{5,4,3,2,1,0:T(8,128)(2,1)S(1)}, u32[]{:S(2)}, u32[]{:S(2)}) %collective-permute-start.7) | collective-permute-done | bytes 1048608 | tf_op jit(solution)/shard_map/ppermute | solution.py:337
  41.6 3.2 %collective-permute-done.8.refs_2_ = bf16[4,2,2,2,32,512]{5,4,3,2,1,0:T(8,128)(2,1)S(1)} collective-permute-done((bf16[4,2,2,2,32,512]{5,4,3,2,1,0:T(8,128)(2,1)S(1)}, bf16[4,2,2,2,32,512]{5,4,3,2,1,0:T(8,128)(2,1)S(1)}, u32[]{:S(2)}, u32[]{:S(2)}) %collective-permute-start.8) | collective-permute-done | bytes 1048608 | tf_op jit(solution)/shard_map/ppermute | solution.py:337
  44.9 0.1 collective-permute-start.10
  45.0 1.5 %collective-permute-start.11 = (bf16[2,2,2,2,32,512]{5,4,3,2,1,0:T(8,128)(2,1)S(1)}, bf16[2,2,2,2,32,512]{5,4,3,2,1,0:T(8,128)(2,1)S(1)}, u32[]{:S(2)}, u32[]{:S(2)}) collective-permute-start(bf16[2,2,2,2,32,512]{5,4,3,2,1,0:T(8,128)(2,1)S(1)} %slice.23), channel_id=1, source_target_pairs={{0,2},{8,24},{2,4},{10,26},{4,6},{12,28},{6,0},{14,30},{16,18},{24... | collective-permute-start | bytes 1572872 | tf_op jit(solution)/shard_map/ppermute | solution.py:337
  46.5 3.6 %collective-permute-done.13.from_below = bf16[2,4,2,32,512]{4,3,2,1,0:T(8,128)(2,1)S(1)} collective-permute-done((bf16[2,4,2,32,512]{4,3,2,1,0:T(8,128)(2,1)S(1)}, bf16[2,4,2,32,512]{4,3,2,1,0:T(8,128)(2,1)S(1)}, u32[]{:S(2)}, u32[]{:S(2)}) %collective-permute-start.13) | collective-permute-done | bytes 524320 | tf_op jit(solution)/shard_map/ppermute | solution.py:337
  50.2 0.8 pass_on.1
  51.0 0.1 collective-permute-start.15
  51.0 2.7 %collective-permute-start.16 = (bf16[4,4,2,32,512]{4,3,2,1,0:T(8,128)(2,1)S(1)}, bf16[4,4,2,32,512]{4,3,2,1,0:T(8,128)(2,1)S(1)}, u32[]{:S(2)}, u32[]{:S(2)}) collective-permute-start(bf16[4,4,2,32,512]{4,3,2,1,0:T(8,128)(2,1)S(1)} %get-tuple-element.79), channel_id=1, source_target_pairs={{0,65},{8,56},{2,67},{10,58},{4,69},{12,60},{6,71},{14,62},{16,81}... | collective-permute-start | bytes 3145736 | tf_op jit(solution)/shard_map/ppermute | solution.py:337
  53.7 2.3 %collective-permute-done.11.refs_4_ = bf16[2,2,2,2,32,512]{5,4,3,2,1,0:T(8,128)(2,1)S(1)} collective-permute-done((bf16[2,2,2,2,32,512]{5,4,3,2,1,0:T(8,128)(2,1)S(1)}, bf16[2,2,2,2,32,512]{5,4,3,2,1,0:T(8,128)(2,1)S(1)}, u32[]{:S(2)}, u32[]{:S(2)}) %collective-permute-start.11) | collective-permute-done | bytes 524320 | tf_op jit(solution)/shard_map/ppermute | solution.py:337
  56.1 0.5 assemble.1.weights.own
  56.6 3.0 %keys_own_half.1.so_far = f32[512,512]{1,0:T(8,128)S(1)} custom-call(s32[1]{0:T(128)} %bitcast.4.core, bf16[2,8,512,512]{3,2,1,0:T(8,128)(2,1)S(1)} %get-tuple-element.60.normed, bf16[4,2,2,4,2,32,512]{6,5,4,3,2,1,0:T(8,128)(2,1)S(1)} %assemble.1.weights.own), custom_call_target="tpu_custom_call" | custom-call | flops 6442450944 | bytes 12582912 | tf_op jit(solution)/shard_map/keys_own_half/pallas_call | solution.py:262
  59.6 2.4 %collective-permute-start.12 = (bf16[4,2,2,4,2,32,512]{6,5,4,3,2,1,0:T(8,128)(2,1)S(1)}, bf16[4,2,2,4,2,32,512]{6,5,4,3,2,1,0:T(8,128)(2,1)S(1)}, u32[]{:S(2)}, u32[]{:S(2)}) collective-permute-start(bf16[4,2,2,4,2,32,512]{6,5,4,3,2,1,0:T(8,128)(2,1)S(1)} %assemble.1.weights.own), channel_id=1, source_target_pairs={{0,8},{8,0},{1,9},{9,1},{2,10},{10,2},{3,11},{11,3},{4,12},{12,4},... | collective-permute-start | bytes 12582920 | tf_op jit(solution)/shard_map/ppermute | solution.py:345
  62.0 5.0 %collective-permute-done.15.one = bf16[4,4,2,32,512]{4,3,2,1,0:T(8,128)(2,1)S(1)} collective-permute-done((bf16[4,4,2,32,512]{4,3,2,1,0:T(8,128)(2,1)S(1)}, bf16[4,4,2,32,512]{4,3,2,1,0:T(8,128)(2,1)S(1)}, u32[]{:S(2)}, u32[]{:S(2)}) %collective-permute-start.15) | collective-permute-done | bytes 1048608 | tf_op jit(solution)/shard_map/ppermute | solution.py:337
  67.0 0.4 sum_first.1
  67.4 1.6 %collective-permute-start.17 = (bf16[4,2,32,512]{3,2,1,0:T(8,128)(2,1)S(1)}, bf16[4,2,32,512]{3,2,1,0:T(8,128)(2,1)S(1)}, u32[]{:S(2)}, u32[]{:S(2)}) collective-permute-start(bf16[4,2,32,512]{3,2,1,0:T(8,128)(2,1)S(1)} %get-tuple-element.81), channel_id=1, source_target_pairs={{0,32},{8,72},{2,34},{10,74},{4,36},{12,76},{6,38},{14,78},{16,48}... | collective-permute-start | bytes 786440 | tf_op jit(solution)/shard_map/ppermute | solution.py:337
  69.0 1.4 %collective-permute-start.18 = (bf16[4,2,32,512]{3,2,1,0:T(8,128)(2,1)S(1)}, bf16[4,2,32,512]{3,2,1,0:T(8,128)(2,1)S(1)}, u32[]{:S(2)}, u32[]{:S(2)}) collective-permute-start(bf16[4,2,32,512]{3,2,1,0:T(8,128)(2,1)S(1)} %get-tuple-element.82), channel_id=1, source_target_pairs={{0,16},{8,9},{2,18},{10,11},{4,20},{12,13},{6,22},{14,15},{16,32},... | collective-permute-start | bytes 786440 | tf_op jit(solution)/shard_map/ppermute | solution.py:337
  70.4 1.3 %collective-permute-start.19 = (bf16[4,2,32,512]{3,2,1,0:T(8,128)(2,1)S(1)}, bf16[4,2,32,512]{3,2,1,0:T(8,128)(2,1)S(1)}, u32[]{:S(2)}, u32[]{:S(2)}) collective-permute-start(bf16[4,2,32,512]{3,2,1,0:T(8,128)(2,1)S(1)} %get-tuple-element.83), channel_id=1, source_target_pairs={{0,48},{8,73},{2,50},{10,75},{4,52},{12,77},{6,54},{14,79},{16,0},... | collective-permute-start | bytes 786440 | tf_op jit(solution)/shard_map/ppermute | solution.py:337
  71.7 4.4 %keys.1 = (bf16[512,512]{1,0:T(8,128)(2,1)}, f32[512,128]{1,0:T(8,128)S(1)}) custom-call(s32[1]{0:T(128)} %bitcast.4.core, bf16[2,8,512,512]{3,2,1,0:T(8,128)(2,1)S(1)} %get-tuple-element.60.normed, bf16[512,512]{1,0:T(8,128)(2,1)S(1)} %get-tuple-element.61.dpre, f32[512,64]{1,0:T(8,128)S(1)} %get-tuple-element.57.cosine, ...), custom_call_target="tpu_custom_call" | custom-call | flops 2147483648 | bytes 9437184 | tf_op jit(solution)/shard_map/keys/pallas_call | solution.py:287
  76.1 1.2 %collective-permute-done.18.three = bf16[4,2,32,512]{3,2,1,0:T(8,128)(2,1)S(1)} collective-permute-done((bf16[4,2,32,512]{3,2,1,0:T(8,128)(2,1)S(1)}, bf16[4,2,32,512]{3,2,1,0:T(8,128)(2,1)S(1)}, u32[]{:S(2)}, u32[]{:S(2)}) %collective-permute-start.18) | collective-permute-done | bytes 262176 | tf_op jit(solution)/shard_map/ppermute | solution.py:337
  77.3 0.1 sum_second.1
  77.4 3.4 %collective-permute-start.20 = (bf16[2,32,512]{2,1,0:T(8,128)(2,1)S(1)}, bf16[2,32,512]{2,1,0:T(8,128)(2,1)S(1)}, u32[]{:S(2)}, u32[]{:S(2)}) collective-permute-start(bf16[2,32,512]{2,1,0:T(8,128)(2,1)S(1)} %get-tuple-element.90), channel_id=1, source_target_pairs={{0,4},{8,12},{2,6},{10,14},{4,0},{12,8},{6,2},{14,10},{16,20},{24,... | collective-permute-start | bytes 196616 | tf_op jit(solution)/shard_map/ppermute | solution.py:337
  80.8 0.7 collective-permute-start.21
  81.6 1.9 %collective-permute-start.22 = (bf16[2,32,512]{2,1,0:T(8,128)(2,1)S(1)}, bf16[2,32,512]{2,1,0:T(8,128)(2,1)S(1)}, u32[]{:S(2)}, u32[]{:S(2)}) collective-permute-start(bf16[2,32,512]{2,1,0:T(8,128)(2,1)S(1)} %get-tuple-element.92), channel_id=1, source_target_pairs={{0,6},{8,14},{2,0},{10,8},{4,2},{12,10},{6,4},{14,12},{16,22},{24,... | collective-permute-start | bytes 196616 | tf_op jit(solution)/shard_map/ppermute | solution.py:337
  83.5 8.7 %input_gradient.1 = bf16[512,8192]{1,0:T(8,128)(2,1)} custom-call(s32[1]{0:T(128)} %bitcast.4.core, bf16[2,8,512,512]{3,2,1,0:T(8,128)(2,1)S(1)} %get-tuple-element.60.normed, bf16[512,512]{1,0:T(8,128)(2,1)S(1)} %get-tuple-element.61.dpre, f32[512,128]{1,0:T(8,128)S(1)} %get-tuple-element.93.inv, f32[512,128]{1,0:T(8,128)S(1)} %get-tuple-element.94.coef, ...), custom_call_target="tpu_custom_call" | custom-call | flops 4294967296 | bytes 18874368 | tf_op jit(solution)/shard_map/input_gradient/pallas_call | solution.py:315
  92.3 0.1 collective-permute-start.23
  92.4 1.2 %collective-permute-done.23 = f32[32,512]{1,0:T(8,128)S(1)} collective-permute-done((f32[32,512]{1,0:T(8,128)S(1)}, f32[32,512]{1,0:T(8,128)S(1)}, u32[]{:S(2)}, u32[]{:S(2)}) %collective-permute-start.23) | collective-permute-done | bytes 65568 | tf_op jit(solution)/shard_map/ppermute | solution.py:345
  93.6 0.7 fusion
  (24 shorter events, 0.3 us)
Async XLA Ops:
  1.4 2.5 %collective-permute-start = (bf16[32,512]{1,0:T(8,128)(2,1)S(1)}, bf16[32,512]{1,0:T(8,128)(2,1)S(1)}, u32[]{:S(2)}, u32[]{:S(2)}) collective-permute-start(bf16[32,512]{1,0:T(8,128)(2,1)S(1)} %get-tuple-element.108), channel_id=1, source_target_pairs={{0,8},{8,0},{1,9},{9,1},{2,10},{10,2},{3,11},{11,3},{4,12},{12,4},... | collective-permute-start | bytes 98312 | tf_op jit(solution)/shard_map/ppermute | solution.py:345
  4.0 10.6 %collective-permute-start.1 = (bf16[2,32,512]{2,1,0:T(8,128)(2,1)S(1)}, bf16[2,32,512]{2,1,0:T(8,128)(2,1)S(1)}, u32[]{:S(2)}, u32[]{:S(2)}) collective-permute-start(bf16[2,32,512]{2,1,0:T(8,128)(2,1)S(1)} %maximum_select_fusion.1), channel_id=1, source_target_pairs={{0,65},{8,73},{2,67},{10,75},{4,69},{12,77},{6,71},{14,79},{16,81}... | collective-permute-start | bytes 196616 | tf_op jit(solution)/shard_map/ppermute | solution.py:337
  6.6 8.0 %collective-permute-start.2 = (bf16[2,32,512]{2,1,0:T(8,128)(2,1)S(1)}, bf16[2,32,512]{2,1,0:T(8,128)(2,1)S(1)}, u32[]{:S(2)}, u32[]{:S(2)}) collective-permute-start(bf16[2,32,512]{2,1,0:T(8,128)(2,1)S(1)} %maximum_select_fusion.1), channel_id=1, source_target_pairs={{0,64},{8,72},{2,66},{10,74},{4,68},{12,76},{6,70},{14,78},{16,80}... | collective-permute-start | bytes 196616 | tf_op jit(solution)/shard_map/ppermute | solution.py:337
  7.1 7.5 %collective-permute-start.3 = (bf16[2,32,512]{2,1,0:T(8,128)(2,1)S(1)}, bf16[2,32,512]{2,1,0:T(8,128)(2,1)S(1)}, u32[]{:S(2)}, u32[]{:S(2)}) collective-permute-start(bf16[2,32,512]{2,1,0:T(8,128)(2,1)S(1)} %maximum_select_fusion.1), channel_id=1, source_target_pairs={{0,1},{8,9},{2,3},{10,11},{4,5},{12,13},{6,7},{14,15},{16,17},{24,... | collective-permute-start | bytes 196616 | tf_op jit(solution)/shard_map/ppermute | solution.py:337
  14.7 9.3 %collective-permute-start.6 = (bf16[2,2,2,32,512]{4,3,2,1,0:T(8,128)(2,1)S(1)}, bf16[2,2,2,32,512]{4,3,2,1,0:T(8,128)(2,1)S(1)}, u32[]{:S(2)}, u32[]{:S(2)}) collective-permute-start(bf16[2,2,2,32,512]{4,3,2,1,0:T(8,128)(2,1)S(1)} %bitcast.29), channel_id=1, source_target_pairs={{0,16},{8,10},{2,18},{10,12},{4,20},{12,14},{6,22},{14,8},{16,32},... | collective-permute-start | bytes 786440 | tf_op jit(solution)/shard_map/ppermute | solution.py:337
  16.4 10.2 %collective-permute-start.5 = (bf16[2,2,2,32,512]{4,3,2,1,0:T(8,128)(2,1)S(1)}, bf16[2,2,2,32,512]{4,3,2,1,0:T(8,128)(2,1)S(1)}, u32[]{:S(2)}, u32[]{:S(2)}) collective-permute-start(bf16[2,2,2,32,512]{4,3,2,1,0:T(8,128)(2,1)S(1)} %bitcast.30), channel_id=1, source_target_pairs={{0,32},{8,12},{2,34},{10,14},{4,36},{12,8},{6,38},{14,10},{16,48},... | collective-permute-start | bytes 786440 | tf_op jit(solution)/shard_map/ppermute | solution.py:337
  19.7 6.9 %collective-permute-start.4 = (bf16[2,2,2,32,512]{4,3,2,1,0:T(8,128)(2,1)S(1)}, bf16[2,2,2,32,512]{4,3,2,1,0:T(8,128)(2,1)S(1)}, u32[]{:S(2)}, u32[]{:S(2)}) collective-permute-start(bf16[2,2,2,32,512]{4,3,2,1,0:T(8,128)(2,1)S(1)} %bitcast.31), channel_id=1, source_target_pairs={{0,48},{8,14},{2,50},{10,8},{4,52},{12,10},{6,54},{14,12},{16,0},{... | collective-permute-start | bytes 786440 | tf_op jit(solution)/shard_map/ppermute | solution.py:337
  26.7 7.7 %collective-permute-start.9 = (bf16[8,16,32,512]{3,2,1,0:T(8,128)(2,1)S(1)}, bf16[8,16,32,512]{3,2,1,0:T(8,128)(2,1)S(1)}, u32[]{:S(2)}, u32[]{:S(2)}) collective-permute-start(bf16[8,16,32,512]{3,2,1,0:T(8,128)(2,1)S(1)} %send_half.1), channel_id=1, source_target_pairs={{0,8},{8,0},{1,9},{9,1},{2,10},{10,2},{3,11},{11,3},{4,12},{12,4},... | collective-permute-start | bytes 12582920 | tf_op jit(solution)/shard_map/ppermute | solution.py:345
  27.7 13.9 %collective-permute-start.7 = (bf16[4,2,2,2,32,512]{5,4,3,2,1,0:T(8,128)(2,1)S(1)}, bf16[4,2,2,2,32,512]{5,4,3,2,1,0:T(8,128)(2,1)S(1)}, u32[]{:S(2)}, u32[]{:S(2)}) collective-permute-start(bf16[4,2,2,2,32,512]{5,4,3,2,1,0:T(8,128)(2,1)S(1)} %pad_maximum_fusion.refs_0_), channel_id=1, source_target_pairs={{0,6},{8,56},{2,0},{10,58},{4,2},{12,60},{6,4},{14,62},{16,22},{24... | collective-permute-start | bytes 3145736 | tf_op jit(solution)/shard_map/ppermute | solution.py:337
  29.7 15.2 %collective-permute-start.8 = (bf16[4,2,2,2,32,512]{5,4,3,2,1,0:T(8,128)(2,1)S(1)}, bf16[4,2,2,2,32,512]{5,4,3,2,1,0:T(8,128)(2,1)S(1)}, u32[]{:S(2)}, u32[]{:S(2)}) collective-permute-start(bf16[4,2,2,2,32,512]{5,4,3,2,1,0:T(8,128)(2,1)S(1)} %pad_maximum_fusion.refs_0_), channel_id=1, source_target_pairs={{0,2},{8,24},{2,4},{10,26},{4,6},{12,28},{6,0},{14,30},{16,18},{24... | collective-permute-start | bytes 3145736 | tf_op jit(solution)/shard_map/ppermute | solution.py:337
  36.0 14.1 %collective-permute-start.13 = (bf16[2,4,2,32,512]{4,3,2,1,0:T(8,128)(2,1)S(1)}, bf16[2,4,2,32,512]{4,3,2,1,0:T(8,128)(2,1)S(1)}, u32[]{:S(2)}, u32[]{:S(2)}) collective-permute-start(bf16[2,4,2,32,512]{4,3,2,1,0:T(8,128)(2,1)S(1)} %get-tuple-element.76), channel_id=1, source_target_pairs={{0,1},{8,24},{2,3},{10,26},{4,5},{12,28},{6,7},{14,30},{16,17},{24... | collective-permute-start | bytes 1572872 | tf_op jit(solution)/shard_map/ppermute | solution.py:337
  37.5 12.7 %collective-permute-start.14 = (bf16[2,4,2,32,512]{4,3,2,1,0:T(8,128)(2,1)S(1)}, bf16[2,4,2,32,512]{4,3,2,1,0:T(8,128)(2,1)S(1)}, u32[]{:S(2)}, u32[]{:S(2)}) collective-permute-start(bf16[2,4,2,32,512]{4,3,2,1,0:T(8,128)(2,1)S(1)} %get-tuple-element.77), channel_id=1, source_target_pairs={{0,65},{8,56},{2,67},{10,58},{4,69},{12,60},{6,71},{14,62},{16,81}... | collective-permute-start | bytes 1572872 | tf_op jit(solution)/shard_map/ppermute | solution.py:337
  44.9 8.8 %collective-permute-start.10 = (bf16[2,2,2,2,32,512]{5,4,3,2,1,0:T(8,128)(2,1)S(1)}, bf16[2,2,2,2,32,512]{5,4,3,2,1,0:T(8,128)(2,1)S(1)}, u32[]{:S(2)}, u32[]{:S(2)}) collective-permute-start(bf16[2,2,2,2,32,512]{5,4,3,2,1,0:T(8,128)(2,1)S(1)} %slice.22), channel_id=1, source_target_pairs={{0,6},{8,56},{2,0},{10,58},{4,2},{12,60},{6,4},{14,62},{16,22},{24... | collective-permute-start | bytes 1572872 | tf_op jit(solution)/shard_map/ppermute | solution.py:337
  45.0 11.1 %collective-permute-start.11 = (bf16[2,2,2,2,32,512]{5,4,3,2,1,0:T(8,128)(2,1)S(1)}, bf16[2,2,2,2,32,512]{5,4,3,2,1,0:T(8,128)(2,1)S(1)}, u32[]{:S(2)}, u32[]{:S(2)}) collective-permute-start(bf16[2,2,2,2,32,512]{5,4,3,2,1,0:T(8,128)(2,1)S(1)} %slice.23), channel_id=1, source_target_pairs={{0,2},{8,24},{2,4},{10,26},{4,6},{12,28},{6,0},{14,30},{16,18},{24... | collective-permute-start | bytes 1572872 | tf_op jit(solution)/shard_map/ppermute | solution.py:337
  51.0 16.0 %collective-permute-start.15 = (bf16[4,4,2,32,512]{4,3,2,1,0:T(8,128)(2,1)S(1)}, bf16[4,4,2,32,512]{4,3,2,1,0:T(8,128)(2,1)S(1)}, u32[]{:S(2)}, u32[]{:S(2)}) collective-permute-start(bf16[4,4,2,32,512]{4,3,2,1,0:T(8,128)(2,1)S(1)} %get-tuple-element.78), channel_id=1, source_target_pairs={{0,1},{8,24},{2,3},{10,26},{4,5},{12,28},{6,7},{14,30},{16,17},{24... | collective-permute-start | bytes 3145736 | tf_op jit(solution)/shard_map/ppermute | solution.py:337
  51.0 16.0 %collective-permute-start.16 = (bf16[4,4,2,32,512]{4,3,2,1,0:T(8,128)(2,1)S(1)}, bf16[4,4,2,32,512]{4,3,2,1,0:T(8,128)(2,1)S(1)}, u32[]{:S(2)}, u32[]{:S(2)}) collective-permute-start(bf16[4,4,2,32,512]{4,3,2,1,0:T(8,128)(2,1)S(1)} %get-tuple-element.79), channel_id=1, source_target_pairs={{0,65},{8,56},{2,67},{10,58},{4,69},{12,60},{6,71},{14,62},{16,81}... | collective-permute-start | bytes 3145736 | tf_op jit(solution)/shard_map/ppermute | solution.py:337
  59.6 12.1 %collective-permute-start.12 = (bf16[4,2,2,4,2,32,512]{6,5,4,3,2,1,0:T(8,128)(2,1)S(1)}, bf16[4,2,2,4,2,32,512]{6,5,4,3,2,1,0:T(8,128)(2,1)S(1)}, u32[]{:S(2)}, u32[]{:S(2)}) collective-permute-start(bf16[4,2,2,4,2,32,512]{6,5,4,3,2,1,0:T(8,128)(2,1)S(1)} %assemble.1.weights.own), channel_id=1, source_target_pairs={{0,8},{8,0},{1,9},{9,1},{2,10},{10,2},{3,11},{11,3},{4,12},{12,4},... | collective-permute-start | bytes 12582920 | tf_op jit(solution)/shard_map/ppermute | solution.py:345
  67.4 8.7 %collective-permute-start.17 = (bf16[4,2,32,512]{3,2,1,0:T(8,128)(2,1)S(1)}, bf16[4,2,32,512]{3,2,1,0:T(8,128)(2,1)S(1)}, u32[]{:S(2)}, u32[]{:S(2)}) collective-permute-start(bf16[4,2,32,512]{3,2,1,0:T(8,128)(2,1)S(1)} %get-tuple-element.81), channel_id=1, source_target_pairs={{0,32},{8,72},{2,34},{10,74},{4,36},{12,76},{6,38},{14,78},{16,48}... | collective-permute-start | bytes 786440 | tf_op jit(solution)/shard_map/ppermute | solution.py:337
  69.0 8.3 %collective-permute-start.18 = (bf16[4,2,32,512]{3,2,1,0:T(8,128)(2,1)S(1)}, bf16[4,2,32,512]{3,2,1,0:T(8,128)(2,1)S(1)}, u32[]{:S(2)}, u32[]{:S(2)}) collective-permute-start(bf16[4,2,32,512]{3,2,1,0:T(8,128)(2,1)S(1)} %get-tuple-element.82), channel_id=1, source_target_pairs={{0,16},{8,9},{2,18},{10,11},{4,20},{12,13},{6,22},{14,15},{16,32},... | collective-permute-start | bytes 786440 | tf_op jit(solution)/shard_map/ppermute | solution.py:337
  70.4 6.9 %collective-permute-start.19 = (bf16[4,2,32,512]{3,2,1,0:T(8,128)(2,1)S(1)}, bf16[4,2,32,512]{3,2,1,0:T(8,128)(2,1)S(1)}, u32[]{:S(2)}, u32[]{:S(2)}) collective-permute-start(bf16[4,2,32,512]{3,2,1,0:T(8,128)(2,1)S(1)} %get-tuple-element.83), channel_id=1, source_target_pairs={{0,48},{8,73},{2,50},{10,75},{4,52},{12,77},{6,54},{14,79},{16,0},... | collective-permute-start | bytes 786440 | tf_op jit(solution)/shard_map/ppermute | solution.py:337
  77.4 14.8 %collective-permute-start.20 = (bf16[2,32,512]{2,1,0:T(8,128)(2,1)S(1)}, bf16[2,32,512]{2,1,0:T(8,128)(2,1)S(1)}, u32[]{:S(2)}, u32[]{:S(2)}) collective-permute-start(bf16[2,32,512]{2,1,0:T(8,128)(2,1)S(1)} %get-tuple-element.90), channel_id=1, source_target_pairs={{0,4},{8,12},{2,6},{10,14},{4,0},{12,8},{6,2},{14,10},{16,20},{24,... | collective-permute-start | bytes 196616 | tf_op jit(solution)/shard_map/ppermute | solution.py:337
  80.8 11.4 %collective-permute-start.21 = (bf16[2,32,512]{2,1,0:T(8,128)(2,1)S(1)}, bf16[2,32,512]{2,1,0:T(8,128)(2,1)S(1)}, u32[]{:S(2)}, u32[]{:S(2)}) collective-permute-start(bf16[2,32,512]{2,1,0:T(8,128)(2,1)S(1)} %get-tuple-element.91), channel_id=1, source_target_pairs={{0,2},{8,10},{2,4},{10,12},{4,6},{12,14},{6,0},{14,8},{16,18},{24,... | collective-permute-start | bytes 196616 | tf_op jit(solution)/shard_map/ppermute | solution.py:337
  81.6 10.7 %collective-permute-start.22 = (bf16[2,32,512]{2,1,0:T(8,128)(2,1)S(1)}, bf16[2,32,512]{2,1,0:T(8,128)(2,1)S(1)}, u32[]{:S(2)}, u32[]{:S(2)}) collective-permute-start(bf16[2,32,512]{2,1,0:T(8,128)(2,1)S(1)} %get-tuple-element.92), channel_id=1, source_target_pairs={{0,6},{8,14},{2,0},{10,8},{4,2},{12,10},{6,4},{14,12},{16,22},{24,... | collective-permute-start | bytes 196616 | tf_op jit(solution)/shard_map/ppermute | solution.py:337
  92.3 1.3 %collective-permute-start.23 = (f32[32,512]{1,0:T(8,128)S(1)}, f32[32,512]{1,0:T(8,128)S(1)}, u32[]{:S(2)}, u32[]{:S(2)}) collective-permute-start(f32[32,512]{1,0:T(8,128)S(1)} %get-tuple-element.106), channel_id=1, source_target_pairs={{0,8},{8,0},{1,9},{9,1},{2,10},{10,2},{3,11},{11,3},{4,12},{12,4},... | collective-permute-start | bytes 196616 | tf_op jit(solution)/shard_map/ppermute | solution.py:345

commit v4 on v3

--- a/solution.py
+++ b/solution.py
@@ -300,23 +300,24 @@
 
 
 def grad_kernel(core, normed, dpre, inv, coef, own, other, grad):
-    j = pl.program_id(0)
-    for half, weights in ((core[0], own), (1 - core[0], other)):
-        here = weights[j // 2, :, j % 2].reshape(KV, LANES)
-        back = jnp.dot(dpre[...], here, preferred_element_type=F32)
-        for k in range(LANES // 128):
-            cols = slice(k * 128, (k + 1) * 128)
-            into = pl.ds(pl.multiple_of(half * LANES + k * 128, 128), 128)
-            less = normed[half, j, :, cols].astype(F32) * coef[...]
-            grad[:, into] = ((back[:, cols] - less) * inv[...]).astype(BF16)
+    for t in range(2):
+        j = 2 * pl.program_id(0) + t
+        for half, weights in ((core[0], own), (1 - core[0], other)):
+            here = weights[j // 2, :, t].reshape(KV, LANES)
+            back = jnp.dot(dpre[...], here, preferred_element_type=F32)
+            for k in range(LANES // 128):
+                cols = slice(k * 128, (k + 1) * 128)
+                into = pl.ds(pl.multiple_of((2 * t + half) * LANES + k * 128, 128), 128)
+                less = normed[half, j, :, cols].astype(F32) * coef[...]
+                grad[:, into] = ((back[:, cols] - less) * inv[...]).astype(BF16)
 
 
 def grad_call(core, normed, dpre, inv, coef, own, other):
     return pl.pallas_call(
         grad_kernel,
-        grid=(STEPS,),
+        grid=(STEPS // 2,),
         in_specs=[SMEM] + [VMEM] * 6,
-        out_specs=pl.BlockSpec((ROWS, 2 * LANES), lambda j: (0, j)),
+        out_specs=pl.BlockSpec((ROWS, 4 * LANES), lambda j: (0, j)),
         out_shape=jax.ShapeDtypeStruct((ROWS, D), BF16),
         compiler_params=params(16),
         cost_estimate=pl.CostEstimate(flops=2 * ROWS * D * KV, bytes_accessed=18 * MIB, transcendentals=0),
@@ -390,10 +391,10 @@
     others = swap_cores(barrier((weights, so_far))[0])
     keys, coef = keys_call(core, normed, dpre, cosine, sine, others, so_far)
     cut = sum_cut(core, x, y, arrived)
-    arrived = [cut[0]] + [hop(cut[r], Y, X, r) for r in (2, 1, 3)]
+    arrived = [cut[0]] + [hop(cut[r], Y, X, r) for r in (1, 3, 2)]
     arrived, coef = barrier((arrived, coef))
     cut = cut_call(z, arrived)
-    arrived = [cut[0]] + [hop(cut[r], Z, Z, r) for r in (2, 1, 3)]
+    arrived = [cut[0]] + [hop(cut[r], Z, Z, r) for r in (1, 3, 2)]
     grad = grad_call(core, normed, dpre, inv, coef, weights, others)
     arrived, grad = barrier((arrived, grad))
     total = sum(part.astype(F32) for part in arrived) * (1.0 / 256.0)

time: 94.5 us -> 93.2 us (0.986)
  starting transfers between devices: 33.9 us -> 31.7 us
  waiting for transfers between devices: 23.3 us -> 24.6 us
    ppermute x20, starting transfers between devices: 29 us -> 26.7 us  [hop(): return lax.ppermute(value, AXES, pairs)]
    ppermute x20, waiting for transfers between devices: 20.8 us -> 22.1 us  [hop(): return lax.ppermute(value, AXES, pairs)]
where the time goes in v4:
time: 93.2 us; the launch traced here: 93 us
  Pallas kernels  33.1 us (36%)
  starting transfers between devices  31.7 us (34%)
  waiting for transfers between devices  24.6 us (26%)
  other arithmetic  2.73 us (3%)
    ppermute x20, starting transfers between devices, hop(): return lax.ppermute(value, AXES, pairs)  26.7 us
    ppermute x20, waiting for transfers between devices, hop(): return lax.ppermute(value, AXES, pairs)  22.1 us
    pallas_call x1, Pallas kernels, grad_call(): pl.pallas_call(grad_kernel, grid=(STEPS // 2,), in_specs=[SMEM] + [VMEM]...  8.39 us
    pallas_call x2, Pallas kernels, terms_call(): pl.pallas_call(kernel, in_specs=[SMEM, VMEM, VMEM], out_specs=VMEM, out_s...  7.02 us
    pallas_call x1, Pallas kernels, prepare_call(): pl.pallas_call(prepare_kernel, grid=(ROWS // 128,), in_specs=[rows(D), ro...  6.88 us
    ppermute x4, starting transfers between devices, swap_cores(): return lax.ppermute(value, 'c', [(0, 1), (1, 0)])  4.94 us
    pallas_call x1, Pallas kernels, keys_call(): pl.pallas_call(keys_kernel, in_specs=[SMEM] + [VMEM] * 6, out_specs=[VMEM...  4.4 us
    pallas_call x1, Pallas kernels, own_call(): pl.pallas_call(own_kernel, in_specs=[SMEM] + [VMEM] * 2, out_specs=VMEM,...  3.02 us
  transfers between devices with their start and end apart: 24, of which 9 were waited for; matrix products, arithmetic and copies ran while one was open for 1% of the time, Pallas kernels for 35%

profile of v4, /device:TPU:1, one launch (start us, length us, event | category | flops | bytes accessed | tf_op | source)
XLA Modules:
  0.0 93.0 jit_solution(9179555028454072995)
XLA Ops:
  0.6 0.8 slice_bitcast_fusion
  1.4 1.5 %collective-permute-start = (bf16[32,512]{1,0:T(8,128)(2,1)S(1)}, bf16[32,512]{1,0:T(8,128)(2,1)S(1)}, u32[]{:S(2)}, u32[]{:S(2)}) collective-permute-start(bf16[32,512]{1,0:T(8,128)(2,1)S(1)} %get-tuple-element.108), channel_id=1, source_target_pairs={{0,8},{8,0},{1,9},{9,1},{2,10},{10,2},{3,11},{11,3},{4,12},{12,4},... | collective-permute-start | bytes 98312 | tf_op jit(solution)/shard_map/ppermute | solution.py:346
  2.9 1.0 %multiply_sine_fusion = (f32[512,64]{1,0:T(8,128)S(1)}, f32[512,64]{1,0:T(8,128)S(1)}) fusion(f32[64]{0:T(128)S(1)} %multiply_exponential_fusion, f32[512]{0:T(512)S(1)} %fusion.2), kind=kLoop, calls=%fused_computation.1 | loop fusion | flops 32768 | bytes 264448 | tf_op jit(solution)/shard_map/sin | solution.py:31
  3.9 0.0 collective-permute-done
  4.0 2.6 %collective-permute-start.1 = (bf16[2,32,512]{2,1,0:T(8,128)(2,1)S(1)}, bf16[2,32,512]{2,1,0:T(8,128)(2,1)S(1)}, u32[]{:S(2)}, u32[]{:S(2)}) collective-permute-start(bf16[2,32,512]{2,1,0:T(8,128)(2,1)S(1)} %maximum_select_fusion.1), channel_id=1, source_target_pairs={{0,65},{8,73},{2,67},{10,75},{4,69},{12,77},{6,71},{14,79},{16,81}... | collective-permute-start | bytes 196616 | tf_op jit(solution)/shard_map/ppermute | solution.py:338
  6.6 0.5 collective-permute-start.2
  7.1 0.6 collective-permute-start.3
  7.7 6.9 %row_scales.1 = (bf16[2,8,512,512]{3,2,1,0:T(8,128)(2,1)S(1)}, f32[512,128]{1,0:T(8,128)S(1)}, bf16[512,512]{1,0:T(8,128)(2,1)S(1)}, bf16[512,512]{1,0:T(8,128)(2,1)S(1)}) custom-call(bf16[512,8192]{1,0:T(8,128)(2,1)} %x, bf16[512,512]{1,0:T(8,128)(2,1)} %cot.1, f32[512,64]{1,0:T(8,128)S(1)} %get-tuple-element.57.cosine, f32[512,64]{1,0:T(8,128)S(1)} %get-tuple-element.58.sine), custom_call_target="tpu_custom_call" | custom-call | flops 41943040 | bytes 18874368 | tf_op jit(solution)/shard_map/row_scales/pallas_call | solution.py:80
  14.7 1.7 %collective-permute-start.6 = (bf16[2,2,2,32,512]{4,3,2,1,0:T(8,128)(2,1)S(1)}, bf16[2,2,2,32,512]{4,3,2,1,0:T(8,128)(2,1)S(1)}, u32[]{:S(2)}, u32[]{:S(2)}) collective-permute-start(bf16[2,2,2,32,512]{4,3,2,1,0:T(8,128)(2,1)S(1)} %bitcast.29), channel_id=1, source_target_pairs={{0,16},{8,10},{2,18},{10,12},{4,20},{12,14},{6,22},{14,8},{16,32},... | collective-permute-start | bytes 786440 | tf_op jit(solution)/shard_map/ppermute | solution.py:338
  16.4 3.3 %collective-permute-start.5 = (bf16[2,2,2,32,512]{4,3,2,1,0:T(8,128)(2,1)S(1)}, bf16[2,2,2,32,512]{4,3,2,1,0:T(8,128)(2,1)S(1)}, u32[]{:S(2)}, u32[]{:S(2)}) collective-permute-start(bf16[2,2,2,32,512]{4,3,2,1,0:T(8,128)(2,1)S(1)} %bitcast.30), channel_id=1, source_target_pairs={{0,32},{8,12},{2,34},{10,14},{4,36},{12,8},{6,38},{14,10},{16,48},... | collective-permute-start | bytes 786440 | tf_op jit(solution)/shard_map/ppermute | solution.py:338
  19.7 0.7 collective-permute-start.4
  20.5 3.5 %send_half.1 = bf16[8,16,32,512]{3,2,1,0:T(8,128)(2,1)S(1)} custom-call(s32[1]{0:T(128)} %bitcast.4.core, bf16[2,8,512,512]{3,2,1,0:T(8,128)(2,1)S(1)} %get-tuple-element.60.normed, bf16[512,512]{1,0:T(8,128)(2,1)S(1)} %get-tuple-element.65.dpre_t), custom_call_target="tpu_custom_call" | custom-call | flops 2147483648 | bytes 9437184 | tf_op jit(solution)/shard_map/send_half/pallas_call | solution.py:111
  24.0 2.6 %collective-permute-done.5 = bf16[2,2,2,32,512]{4,3,2,1,0:T(8,128)(2,1)S(1)} collective-permute-done((bf16[2,2,2,32,512]{4,3,2,1,0:T(8,128)(2,1)S(1)}, bf16[2,2,2,32,512]{4,3,2,1,0:T(8,128)(2,1)S(1)}, u32[]{:S(2)}, u32[]{:S(2)}) %collective-permute-start.5) | collective-permute-done | bytes 262176 | tf_op jit(solution)/shard_map/ppermute | solution.py:338
  26.6 0.1 pad_maximum_fusion.refs_0_
  26.7 0.9 collective-permute-start.9
  27.7 2.0 %collective-permute-start.7 = (bf16[4,2,2,2,32,512]{5,4,3,2,1,0:T(8,128)(2,1)S(1)}, bf16[4,2,2,2,32,512]{5,4,3,2,1,0:T(8,128)(2,1)S(1)}, u32[]{:S(2)}, u32[]{:S(2)}) collective-permute-start(bf16[4,2,2,2,32,512]{5,4,3,2,1,0:T(8,128)(2,1)S(1)} %pad_maximum_fusion.refs_0_), channel_id=1, source_target_pairs={{0,6},{8,56},{2,0},{10,58},{4,2},{12,60},{6,4},{14,62},{16,22},{24... | collective-permute-start | bytes 3145736 | tf_op jit(solution)/shard_map/ppermute | solution.py:338
  29.7 3.5 %keep_half.1.kept = bf16[8,16,32,512]{3,2,1,0:T(8,128)(2,1)S(1)} custom-call(s32[1]{0:T(128)} %bitcast.4.core, bf16[2,8,512,512]{3,2,1,0:T(8,128)(2,1)S(1)} %get-tuple-element.60.normed, bf16[512,512]{1,0:T(8,128)(2,1)S(1)} %get-tuple-element.65.dpre_t), custom_call_target="tpu_custom_call" | custom-call | flops 2147483648 | bytes 9437184 | tf_op jit(solution)/shard_map/keep_half/pallas_call | solution.py:111
  33.2 1.3 %collective-permute-done.9.came = bf16[8,16,32,512]{3,2,1,0:T(8,128)(2,1)S(1)} collective-permute-done((bf16[8,16,32,512]{3,2,1,0:T(8,128)(2,1)S(1)}, bf16[8,16,32,512]{3,2,1,0:T(8,128)(2,1)S(1)}, u32[]{:S(2)}, u32[]{:S(2)}) %collective-permute-start.9) | collective-permute-done | bytes 4194336 | tf_op jit(solution)/shard_map/ppermute | solution.py:346
  34.5 1.6 %add_cores.1 = (bf16[4,4,2,32,512]{4,3,2,1,0:T(8,128)(2,1)S(1)}, bf16[4,4,2,32,512]{4,3,2,1,0:T(8,128)(2,1)S(1)}, bf16[4,4,2,32,512]{4,3,2,1,0:T(8,128)(2,1)S(1)...) custom-call(s32[1]{0:T(128)} %bitcast.4.core, s32[1]{0:T(128)} %bitcast.7.x, s32[1]{0:T(128)} %bitcast.5.y, ...), custom_call_target="tpu_custom_call" | custom-call | bytes 12582912 | tf_op jit(solution)/shard_map/add_cores/pallas_call | solution.py:148
  36.0 1.4 %collective-permute-start.13 = (bf16[2,4,2,32,512]{4,3,2,1,0:T(8,128)(2,1)S(1)}, bf16[2,4,2,32,512]{4,3,2,1,0:T(8,128)(2,1)S(1)}, u32[]{:S(2)}, u32[]{:S(2)}) collective-permute-start(bf16[2,4,2,32,512]{4,3,2,1,0:T(8,128)(2,1)S(1)} %get-tuple-element.76), channel_id=1, source_target_pairs={{0,1},{8,24},{2,3},{10,26},{4,5},{12,28},{6,7},{14,30},{16,17},{24... | collective-permute-start | bytes 1572872 | tf_op jit(solution)/shard_map/ppermute | solution.py:338
  37.5 1.3 %collective-permute-start.14 = (bf16[2,4,2,32,512]{4,3,2,1,0:T(8,128)(2,1)S(1)}, bf16[2,4,2,32,512]{4,3,2,1,0:T(8,128)(2,1)S(1)}, u32[]{:S(2)}, u32[]{:S(2)}) collective-permute-start(bf16[2,4,2,32,512]{4,3,2,1,0:T(8,128)(2,1)S(1)} %get-tuple-element.77), channel_id=1, source_target_pairs={{0,65},{8,56},{2,67},{10,58},{4,69},{12,60},{6,71},{14,62},{16,81}... | collective-permute-start | bytes 1572872 | tf_op jit(solution)/shard_map/ppermute | solution.py:338
  38.8 2.8 %collective-permute-done.7.refs_1_ = bf16[4,2,2,2,32,512]{5,4,3,2,1,0:T(8,128)(2,1)S(1)} collective-permute-done((bf16[4,2,2,2,32,512]{5,4,3,2,1,0:T(8,128)(2,1)S(1)}, bf16[4,2,2,2,32,512]{5,4,3,2,1,0:T(8,128)(2,1)S(1)}, u32[]{:S(2)}, u32[]{:S(2)}) %collective-permute-start.7) | collective-permute-done | bytes 1048608 | tf_op jit(solution)/shard_map/ppermute | solution.py:338
  41.6 3.2 %collective-permute-done.8.refs_2_ = bf16[4,2,2,2,32,512]{5,4,3,2,1,0:T(8,128)(2,1)S(1)} collective-permute-done((bf16[4,2,2,2,32,512]{5,4,3,2,1,0:T(8,128)(2,1)S(1)}, bf16[4,2,2,2,32,512]{5,4,3,2,1,0:T(8,128)(2,1)S(1)}, u32[]{:S(2)}, u32[]{:S(2)}) %collective-permute-start.8) | collective-permute-done | bytes 1048608 | tf_op jit(solution)/shard_map/ppermute | solution.py:338
  44.9 0.1 collective-permute-start.10
  45.0 1.5 %collective-permute-start.11 = (bf16[2,2,2,2,32,512]{5,4,3,2,1,0:T(8,128)(2,1)S(1)}, bf16[2,2,2,2,32,512]{5,4,3,2,1,0:T(8,128)(2,1)S(1)}, u32[]{:S(2)}, u32[]{:S(2)}) collective-permute-start(bf16[2,2,2,2,32,512]{5,4,3,2,1,0:T(8,128)(2,1)S(1)} %slice.23), channel_id=1, source_target_pairs={{0,2},{8,24},{2,4},{10,26},{4,6},{12,28},{6,0},{14,30},{16,18},{24... | collective-permute-start | bytes 1572872 | tf_op jit(solution)/shard_map/ppermute | solution.py:338
  46.5 3.6 %collective-permute-done.13.from_below = bf16[2,4,2,32,512]{4,3,2,1,0:T(8,128)(2,1)S(1)} collective-permute-done((bf16[2,4,2,32,512]{4,3,2,1,0:T(8,128)(2,1)S(1)}, bf16[2,4,2,32,512]{4,3,2,1,0:T(8,128)(2,1)S(1)}, u32[]{:S(2)}, u32[]{:S(2)}) %collective-permute-start.13) | collective-permute-done | bytes 524320 | tf_op jit(solution)/shard_map/ppermute | solution.py:338
  50.2 0.8 pass_on.1
  51.0 0.1 collective-permute-start.15
  51.0 2.7 %collective-permute-start.16 = (bf16[4,4,2,32,512]{4,3,2,1,0:T(8,128)(2,1)S(1)}, bf16[4,4,2,32,512]{4,3,2,1,0:T(8,128)(2,1)S(1)}, u32[]{:S(2)}, u32[]{:S(2)}) collective-permute-start(bf16[4,4,2,32,512]{4,3,2,1,0:T(8,128)(2,1)S(1)} %get-tuple-element.79), channel_id=1, source_target_pairs={{0,65},{8,56},{2,67},{10,58},{4,69},{12,60},{6,71},{14,62},{16,81}... | collective-permute-start | bytes 3145736 | tf_op jit(solution)/shard_map/ppermute | solution.py:338
  53.7 2.3 %collective-permute-done.11.refs_4_ = bf16[2,2,2,2,32,512]{5,4,3,2,1,0:T(8,128)(2,1)S(1)} collective-permute-done((bf16[2,2,2,2,32,512]{5,4,3,2,1,0:T(8,128)(2,1)S(1)}, bf16[2,2,2,2,32,512]{5,4,3,2,1,0:T(8,128)(2,1)S(1)}, u32[]{:S(2)}, u32[]{:S(2)}) %collective-permute-start.11) | collective-permute-done | bytes 524320 | tf_op jit(solution)/shard_map/ppermute | solution.py:338
  56.1 0.5 assemble.1.weights.own
  56.6 3.0 %keys_own_half.1.so_far = f32[512,512]{1,0:T(8,128)S(1)} custom-call(s32[1]{0:T(128)} %bitcast.4.core, bf16[2,8,512,512]{3,2,1,0:T(8,128)(2,1)S(1)} %get-tuple-element.60.normed, bf16[4,2,2,4,2,32,512]{6,5,4,3,2,1,0:T(8,128)(2,1)S(1)} %assemble.1.weights.own), custom_call_target="tpu_custom_call" | custom-call | flops 6442450944 | bytes 12582912 | tf_op jit(solution)/shard_map/keys_own_half/pallas_call | solution.py:262
  59.6 2.4 %collective-permute-start.12 = (bf16[4,2,2,4,2,32,512]{6,5,4,3,2,1,0:T(8,128)(2,1)S(1)}, bf16[4,2,2,4,2,32,512]{6,5,4,3,2,1,0:T(8,128)(2,1)S(1)}, u32[]{:S(2)}, u32[]{:S(2)}) collective-permute-start(bf16[4,2,2,4,2,32,512]{6,5,4,3,2,1,0:T(8,128)(2,1)S(1)} %assemble.1.weights.own), channel_id=1, source_target_pairs={{0,8},{8,0},{1,9},{9,1},{2,10},{10,2},{3,11},{11,3},{4,12},{12,4},... | collective-permute-start | bytes 12582920 | tf_op jit(solution)/shard_map/ppermute | solution.py:346
  62.0 5.0 %collective-permute-done.15.one = bf16[4,4,2,32,512]{4,3,2,1,0:T(8,128)(2,1)S(1)} collective-permute-done((bf16[4,4,2,32,512]{4,3,2,1,0:T(8,128)(2,1)S(1)}, bf16[4,4,2,32,512]{4,3,2,1,0:T(8,128)(2,1)S(1)}, u32[]{:S(2)}, u32[]{:S(2)}) %collective-permute-start.15) | collective-permute-done | bytes 1048608 | tf_op jit(solution)/shard_map/ppermute | solution.py:338
  67.0 0.4 sum_first.1
  67.4 1.6 %collective-permute-start.17 = (bf16[4,2,32,512]{3,2,1,0:T(8,128)(2,1)S(1)}, bf16[4,2,32,512]{3,2,1,0:T(8,128)(2,1)S(1)}, u32[]{:S(2)}, u32[]{:S(2)}) collective-permute-start(bf16[4,2,32,512]{3,2,1,0:T(8,128)(2,1)S(1)} %get-tuple-element.81), channel_id=1, source_target_pairs={{0,16},{8,9},{2,18},{10,11},{4,20},{12,13},{6,22},{14,15},{16,32},... | collective-permute-start | bytes 786440 | tf_op jit(solution)/shard_map/ppermute | solution.py:338
  69.0 1.2 %collective-permute-start.18 = (bf16[4,2,32,512]{3,2,1,0:T(8,128)(2,1)S(1)}, bf16[4,2,32,512]{3,2,1,0:T(8,128)(2,1)S(1)}, u32[]{:S(2)}, u32[]{:S(2)}) collective-permute-start(bf16[4,2,32,512]{3,2,1,0:T(8,128)(2,1)S(1)} %get-tuple-element.82), channel_id=1, source_target_pairs={{0,48},{8,73},{2,50},{10,75},{4,52},{12,77},{6,54},{14,79},{16,0},... | collective-permute-start | bytes 786440 | tf_op jit(solution)/shard_map/ppermute | solution.py:338
  70.1 0.9 collective-permute-start.19
  71.0 4.4 %keys.1 = (bf16[512,512]{1,0:T(8,128)(2,1)}, f32[512,128]{1,0:T(8,128)S(1)}) custom-call(s32[1]{0:T(128)} %bitcast.4.core, bf16[2,8,512,512]{3,2,1,0:T(8,128)(2,1)S(1)} %get-tuple-element.60.normed, bf16[512,512]{1,0:T(8,128)(2,1)S(1)} %get-tuple-element.61.dpre, f32[512,64]{1,0:T(8,128)S(1)} %get-tuple-element.57.cosine, ...), custom_call_target="tpu_custom_call" | custom-call | flops 2147483648 | bytes 9437184 | tf_op jit(solution)/shard_map/keys/pallas_call | solution.py:287
  75.4 2.4 %collective-permute-done.19.four = bf16[4,2,32,512]{3,2,1,0:T(8,128)(2,1)S(1)} collective-permute-done((bf16[4,2,32,512]{3,2,1,0:T(8,128)(2,1)S(1)}, bf16[4,2,32,512]{3,2,1,0:T(8,128)(2,1)S(1)}, u32[]{:S(2)}, u32[]{:S(2)}) %collective-permute-start.19) | collective-permute-done | bytes 262176 | tf_op jit(solution)/shard_map/ppermute | solution.py:338
  77.9 0.1 sum_second.1
  78.0 1.1 %collective-permute-start.20 = (bf16[2,32,512]{2,1,0:T(8,128)(2,1)S(1)}, bf16[2,32,512]{2,1,0:T(8,128)(2,1)S(1)}, u32[]{:S(2)}, u32[]{:S(2)}) collective-permute-start(bf16[2,32,512]{2,1,0:T(8,128)(2,1)S(1)} %get-tuple-element.90), channel_id=1, source_target_pairs={{0,2},{8,10},{2,4},{10,12},{4,6},{12,14},{6,0},{14,8},{16,18},{24,... | collective-permute-start | bytes 196616 | tf_op jit(solution)/shard_map/ppermute | solution.py:338
  79.1 2.2 %collective-permute-start.21 = (bf16[2,32,512]{2,1,0:T(8,128)(2,1)S(1)}, bf16[2,32,512]{2,1,0:T(8,128)(2,1)S(1)}, u32[]{:S(2)}, u32[]{:S(2)}) collective-permute-start(bf16[2,32,512]{2,1,0:T(8,128)(2,1)S(1)} %get-tuple-element.91), channel_id=1, source_target_pairs={{0,6},{8,14},{2,0},{10,8},{4,2},{12,10},{6,4},{14,12},{16,22},{24,... | collective-permute-start | bytes 196616 | tf_op jit(solution)/shard_map/ppermute | solution.py:338
  81.3 1.2 %collective-permute-start.22 = (bf16[2,32,512]{2,1,0:T(8,128)(2,1)S(1)}, bf16[2,32,512]{2,1,0:T(8,128)(2,1)S(1)}, u32[]{:S(2)}, u32[]{:S(2)}) collective-permute-start(bf16[2,32,512]{2,1,0:T(8,128)(2,1)S(1)} %get-tuple-element.92), channel_id=1, source_target_pairs={{0,4},{8,12},{2,6},{10,14},{4,0},{12,8},{6,2},{14,10},{16,20},{24,... | collective-permute-start | bytes 196616 | tf_op jit(solution)/shard_map/ppermute | solution.py:338
  82.5 8.4 %input_gradient.1 = bf16[512,8192]{1,0:T(8,128)(2,1)} custom-call(s32[1]{0:T(128)} %bitcast.4.core, bf16[2,8,512,512]{3,2,1,0:T(8,128)(2,1)S(1)} %get-tuple-element.60.normed, bf16[512,512]{1,0:T(8,128)(2,1)S(1)} %get-tuple-element.61.dpre, f32[512,128]{1,0:T(8,128)S(1)} %get-tuple-element.93.inv, f32[512,128]{1,0:T(8,128)S(1)} %get-tuple-element.94.coef, ...), custom_call_target="tpu_custom_call" | custom-call | flops 4294967296 | bytes 18874368 | tf_op jit(solution)/shard_map/input_gradient/pallas_call | solution.py:316
  91.0 0.1 collective-permute-start.23
  91.1 1.2 %collective-permute-done.23 = f32[32,512]{1,0:T(8,128)S(1)} collective-permute-done((f32[32,512]{1,0:T(8,128)S(1)}, f32[32,512]{1,0:T(8,128)S(1)}, u32[]{:S(2)}, u32[]{:S(2)}) %collective-permute-start.23) | collective-permute-done | bytes 65568 | tf_op jit(solution)/shard_map/ppermute | solution.py:346
  92.3 0.7 fusion
  (24 shorter events, 0.3 us)
Async XLA Ops:
  1.4 2.5 %collective-permute-start = (bf16[32,512]{1,0:T(8,128)(2,1)S(1)}, bf16[32,512]{1,0:T(8,128)(2,1)S(1)}, u32[]{:S(2)}, u32[]{:S(2)}) collective-permute-start(bf16[32,512]{1,0:T(8,128)(2,1)S(1)} %get-tuple-element.108), channel_id=1, source_target_pairs={{0,8},{8,0},{1,9},{9,1},{2,10},{10,2},{3,11},{11,3},{4,12},{12,4},... | collective-permute-start | bytes 98312 | tf_op jit(solution)/shard_map/ppermute | solution.py:346
  4.0 10.6 %collective-permute-start.1 = (bf16[2,32,512]{2,1,0:T(8,128)(2,1)S(1)}, bf16[2,32,512]{2,1,0:T(8,128)(2,1)S(1)}, u32[]{:S(2)}, u32[]{:S(2)}) collective-permute-start(bf16[2,32,512]{2,1,0:T(8,128)(2,1)S(1)} %maximum_select_fusion.1), channel_id=1, source_target_pairs={{0,65},{8,73},{2,67},{10,75},{4,69},{12,77},{6,71},{14,79},{16,81}... | collective-permute-start | bytes 196616 | tf_op jit(solution)/shard_map/ppermute | solution.py:338
  6.6 8.0 %collective-permute-start.2 = (bf16[2,32,512]{2,1,0:T(8,128)(2,1)S(1)}, bf16[2,32,512]{2,1,0:T(8,128)(2,1)S(1)}, u32[]{:S(2)}, u32[]{:S(2)}) collective-permute-start(bf16[2,32,512]{2,1,0:T(8,128)(2,1)S(1)} %maximum_select_fusion.1), channel_id=1, source_target_pairs={{0,64},{8,72},{2,66},{10,74},{4,68},{12,76},{6,70},{14,78},{16,80}... | collective-permute-start | bytes 196616 | tf_op jit(solution)/shard_map/ppermute | solution.py:338
  7.1 7.5 %collective-permute-start.3 = (bf16[2,32,512]{2,1,0:T(8,128)(2,1)S(1)}, bf16[2,32,512]{2,1,0:T(8,128)(2,1)S(1)}, u32[]{:S(2)}, u32[]{:S(2)}) collective-permute-start(bf16[2,32,512]{2,1,0:T(8,128)(2,1)S(1)} %maximum_select_fusion.1), channel_id=1, source_target_pairs={{0,1},{8,9},{2,3},{10,11},{4,5},{12,13},{6,7},{14,15},{16,17},{24,... | collective-permute-start | bytes 196616 | tf_op jit(solution)/shard_map/ppermute | solution.py:338
  14.7 9.3 %collective-permute-start.6 = (bf16[2,2,2,32,512]{4,3,2,1,0:T(8,128)(2,1)S(1)}, bf16[2,2,2,32,512]{4,3,2,1,0:T(8,128)(2,1)S(1)}, u32[]{:S(2)}, u32[]{:S(2)}) collective-permute-start(bf16[2,2,2,32,512]{4,3,2,1,0:T(8,128)(2,1)S(1)} %bitcast.29), channel_id=1, source_target_pairs={{0,16},{8,10},{2,18},{10,12},{4,20},{12,14},{6,22},{14,8},{16,32},... | collective-permute-start | bytes 786440 | tf_op jit(solution)/shard_map/ppermute | solution.py:338
  16.4 10.2 %collective-permute-start.5 = (bf16[2,2,2,32,512]{4,3,2,1,0:T(8,128)(2,1)S(1)}, bf16[2,2,2,32,512]{4,3,2,1,0:T(8,128)(2,1)S(1)}, u32[]{:S(2)}, u32[]{:S(2)}) collective-permute-start(bf16[2,2,2,32,512]{4,3,2,1,0:T(8,128)(2,1)S(1)} %bitcast.30), channel_id=1, source_target_pairs={{0,32},{8,12},{2,34},{10,14},{4,36},{12,8},{6,38},{14,10},{16,48},... | collective-permute-start | bytes 786440 | tf_op jit(solution)/shard_map/ppermute | solution.py:338
  19.7 6.9 %collective-permute-start.4 = (bf16[2,2,2,32,512]{4,3,2,1,0:T(8,128)(2,1)S(1)}, bf16[2,2,2,32,512]{4,3,2,1,0:T(8,128)(2,1)S(1)}, u32[]{:S(2)}, u32[]{:S(2)}) collective-permute-start(bf16[2,2,2,32,512]{4,3,2,1,0:T(8,128)(2,1)S(1)} %bitcast.31), channel_id=1, source_target_pairs={{0,48},{8,14},{2,50},{10,8},{4,52},{12,10},{6,54},{14,12},{16,0},{... | collective-permute-start | bytes 786440 | tf_op jit(solution)/shard_map/ppermute | solution.py:338
  26.7 7.7 %collective-permute-start.9 = (bf16[8,16,32,512]{3,2,1,0:T(8,128)(2,1)S(1)}, bf16[8,16,32,512]{3,2,1,0:T(8,128)(2,1)S(1)}, u32[]{:S(2)}, u32[]{:S(2)}) collective-permute-start(bf16[8,16,32,512]{3,2,1,0:T(8,128)(2,1)S(1)} %send_half.1), channel_id=1, source_target_pairs={{0,8},{8,0},{1,9},{9,1},{2,10},{10,2},{3,11},{11,3},{4,12},{12,4},... | collective-permute-start | bytes 12582920 | tf_op jit(solution)/shard_map/ppermute | solution.py:346
  27.7 13.9 %collective-permute-start.7 = (bf16[4,2,2,2,32,512]{5,4,3,2,1,0:T(8,128)(2,1)S(1)}, bf16[4,2,2,2,32,512]{5,4,3,2,1,0:T(8,128)(2,1)S(1)}, u32[]{:S(2)}, u32[]{:S(2)}) collective-permute-start(bf16[4,2,2,2,32,512]{5,4,3,2,1,0:T(8,128)(2,1)S(1)} %pad_maximum_fusion.refs_0_), channel_id=1, source_target_pairs={{0,6},{8,56},{2,0},{10,58},{4,2},{12,60},{6,4},{14,62},{16,22},{24... | collective-permute-start | bytes 3145736 | tf_op jit(solution)/shard_map/ppermute | solution.py:338
  29.7 15.2 %collective-permute-start.8 = (bf16[4,2,2,2,32,512]{5,4,3,2,1,0:T(8,128)(2,1)S(1)}, bf16[4,2,2,2,32,512]{5,4,3,2,1,0:T(8,128)(2,1)S(1)}, u32[]{:S(2)}, u32[]{:S(2)}) collective-permute-start(bf16[4,2,2,2,32,512]{5,4,3,2,1,0:T(8,128)(2,1)S(1)} %pad_maximum_fusion.refs_0_), channel_id=1, source_target_pairs={{0,2},{8,24},{2,4},{10,26},{4,6},{12,28},{6,0},{14,30},{16,18},{24... | collective-permute-start | bytes 3145736 | tf_op jit(solution)/shard_map/ppermute | solution.py:338
  36.0 14.1 %collective-permute-start.13 = (bf16[2,4,2,32,512]{4,3,2,1,0:T(8,128)(2,1)S(1)}, bf16[2,4,2,32,512]{4,3,2,1,0:T(8,128)(2,1)S(1)}, u32[]{:S(2)}, u32[]{:S(2)}) collective-permute-start(bf16[2,4,2,32,512]{4,3,2,1,0:T(8,128)(2,1)S(1)} %get-tuple-element.76), channel_id=1, source_target_pairs={{0,1},{8,24},{2,3},{10,26},{4,5},{12,28},{6,7},{14,30},{16,17},{24... | collective-permute-start | bytes 1572872 | tf_op jit(solution)/shard_map/ppermute | solution.py:338
  37.5 12.7 %collective-permute-start.14 = (bf16[2,4,2,32,512]{4,3,2,1,0:T(8,128)(2,1)S(1)}, bf16[2,4,2,32,512]{4,3,2,1,0:T(8,128)(2,1)S(1)}, u32[]{:S(2)}, u32[]{:S(2)}) collective-permute-start(bf16[2,4,2,32,512]{4,3,2,1,0:T(8,128)(2,1)S(1)} %get-tuple-element.77), channel_id=1, source_target_pairs={{0,65},{8,56},{2,67},{10,58},{4,69},{12,60},{6,71},{14,62},{16,81}... | collective-permute-start | bytes 1572872 | tf_op jit(solution)/shard_map/ppermute | solution.py:338
  44.9 8.8 %collective-permute-start.10 = (bf16[2,2,2,2,32,512]{5,4,3,2,1,0:T(8,128)(2,1)S(1)}, bf16[2,2,2,2,32,512]{5,4,3,2,1,0:T(8,128)(2,1)S(1)}, u32[]{:S(2)}, u32[]{:S(2)}) collective-permute-start(bf16[2,2,2,2,32,512]{5,4,3,2,1,0:T(8,128)(2,1)S(1)} %slice.22), channel_id=1, source_target_pairs={{0,6},{8,56},{2,0},{10,58},{4,2},{12,60},{6,4},{14,62},{16,22},{24... | collective-permute-start | bytes 1572872 | tf_op jit(solution)/shard_map/ppermute | solution.py:338
  45.0 11.1 %collective-permute-start.11 = (bf16[2,2,2,2,32,512]{5,4,3,2,1,0:T(8,128)(2,1)S(1)}, bf16[2,2,2,2,32,512]{5,4,3,2,1,0:T(8,128)(2,1)S(1)}, u32[]{:S(2)}, u32[]{:S(2)}) collective-permute-start(bf16[2,2,2,2,32,512]{5,4,3,2,1,0:T(8,128)(2,1)S(1)} %slice.23), channel_id=1, source_target_pairs={{0,2},{8,24},{2,4},{10,26},{4,6},{12,28},{6,0},{14,30},{16,18},{24... | collective-permute-start | bytes 1572872 | tf_op jit(solution)/shard_map/ppermute | solution.py:338
  51.0 16.0 %collective-permute-start.15 = (bf16[4,4,2,32,512]{4,3,2,1,0:T(8,128)(2,1)S(1)}, bf16[4,4,2,32,512]{4,3,2,1,0:T(8,128)(2,1)S(1)}, u32[]{:S(2)}, u32[]{:S(2)}) collective-permute-start(bf16[4,4,2,32,512]{4,3,2,1,0:T(8,128)(2,1)S(1)} %get-tuple-element.78), channel_id=1, source_target_pairs={{0,1},{8,24},{2,3},{10,26},{4,5},{12,28},{6,7},{14,30},{16,17},{24... | collective-permute-start | bytes 3145736 | tf_op jit(solution)/shard_map/ppermute | solution.py:338
  51.0 16.0 %collective-permute-start.16 = (bf16[4,4,2,32,512]{4,3,2,1,0:T(8,128)(2,1)S(1)}, bf16[4,4,2,32,512]{4,3,2,1,0:T(8,128)(2,1)S(1)}, u32[]{:S(2)}, u32[]{:S(2)}) collective-permute-start(bf16[4,4,2,32,512]{4,3,2,1,0:T(8,128)(2,1)S(1)} %get-tuple-element.79), channel_id=1, source_target_pairs={{0,65},{8,56},{2,67},{10,58},{4,69},{12,60},{6,71},{14,62},{16,81}... | collective-permute-start | bytes 3145736 | tf_op jit(solution)/shard_map/ppermute | solution.py:338
  59.6 11.4 %collective-permute-start.12 = (bf16[4,2,2,4,2,32,512]{6,5,4,3,2,1,0:T(8,128)(2,1)S(1)}, bf16[4,2,2,4,2,32,512]{6,5,4,3,2,1,0:T(8,128)(2,1)S(1)}, u32[]{:S(2)}, u32[]{:S(2)}) collective-permute-start(bf16[4,2,2,4,2,32,512]{6,5,4,3,2,1,0:T(8,128)(2,1)S(1)} %assemble.1.weights.own), channel_id=1, source_target_pairs={{0,8},{8,0},{1,9},{9,1},{2,10},{10,2},{3,11},{11,3},{4,12},{12,4},... | collective-permute-start | bytes 12582920 | tf_op jit(solution)/shard_map/ppermute | solution.py:346
  67.4 8.0 %collective-permute-start.17 = (bf16[4,2,32,512]{3,2,1,0:T(8,128)(2,1)S(1)}, bf16[4,2,32,512]{3,2,1,0:T(8,128)(2,1)S(1)}, u32[]{:S(2)}, u32[]{:S(2)}) collective-permute-start(bf16[4,2,32,512]{3,2,1,0:T(8,128)(2,1)S(1)} %get-tuple-element.81), channel_id=1, source_target_pairs={{0,16},{8,9},{2,18},{10,11},{4,20},{12,13},{6,22},{14,15},{16,32},... | collective-permute-start | bytes 786440 | tf_op jit(solution)/shard_map/ppermute | solution.py:338
  69.0 6.4 %collective-permute-start.18 = (bf16[4,2,32,512]{3,2,1,0:T(8,128)(2,1)S(1)}, bf16[4,2,32,512]{3,2,1,0:T(8,128)(2,1)S(1)}, u32[]{:S(2)}, u32[]{:S(2)}) collective-permute-start(bf16[4,2,32,512]{3,2,1,0:T(8,128)(2,1)S(1)} %get-tuple-element.82), channel_id=1, source_target_pairs={{0,48},{8,73},{2,50},{10,75},{4,52},{12,77},{6,54},{14,79},{16,0},... | collective-permute-start | bytes 786440 | tf_op jit(solution)/shard_map/ppermute | solution.py:338
  70.1 7.7 %collective-permute-start.19 = (bf16[4,2,32,512]{3,2,1,0:T(8,128)(2,1)S(1)}, bf16[4,2,32,512]{3,2,1,0:T(8,128)(2,1)S(1)}, u32[]{:S(2)}, u32[]{:S(2)}) collective-permute-start(bf16[4,2,32,512]{3,2,1,0:T(8,128)(2,1)S(1)} %get-tuple-element.83), channel_id=1, source_target_pairs={{0,32},{8,72},{2,34},{10,74},{4,36},{12,76},{6,38},{14,78},{16,48}... | collective-permute-start | bytes 786440 | tf_op jit(solution)/shard_map/ppermute | solution.py:338
  78.0 12.9 %collective-permute-start.20 = (bf16[2,32,512]{2,1,0:T(8,128)(2,1)S(1)}, bf16[2,32,512]{2,1,0:T(8,128)(2,1)S(1)}, u32[]{:S(2)}, u32[]{:S(2)}) collective-permute-start(bf16[2,32,512]{2,1,0:T(8,128)(2,1)S(1)} %get-tuple-element.90), channel_id=1, source_target_pairs={{0,2},{8,10},{2,4},{10,12},{4,6},{12,14},{6,0},{14,8},{16,18},{24,... | collective-permute-start | bytes 196616 | tf_op jit(solution)/shard_map/ppermute | solution.py:338
  79.1 11.8 %collective-permute-start.21 = (bf16[2,32,512]{2,1,0:T(8,128)(2,1)S(1)}, bf16[2,32,512]{2,1,0:T(8,128)(2,1)S(1)}, u32[]{:S(2)}, u32[]{:S(2)}) collective-permute-start(bf16[2,32,512]{2,1,0:T(8,128)(2,1)S(1)} %get-tuple-element.91), channel_id=1, source_target_pairs={{0,6},{8,14},{2,0},{10,8},{4,2},{12,10},{6,4},{14,12},{16,22},{24,... | collective-permute-start | bytes 196616 | tf_op jit(solution)/shard_map/ppermute | solution.py:338
  81.3 9.6 %collective-permute-start.22 = (bf16[2,32,512]{2,1,0:T(8,128)(2,1)S(1)}, bf16[2,32,512]{2,1,0:T(8,128)(2,1)S(1)}, u32[]{:S(2)}, u32[]{:S(2)}) collective-permute-start(bf16[2,32,512]{2,1,0:T(8,128)(2,1)S(1)} %get-tuple-element.92), channel_id=1, source_target_pairs={{0,4},{8,12},{2,6},{10,14},{4,0},{12,8},{6,2},{14,10},{16,20},{24,... | collective-permute-start | bytes 196616 | tf_op jit(solution)/shard_map/ppermute | solution.py:338
  91.0 1.3 %collective-permute-start.23 = (f32[32,512]{1,0:T(8,128)S(1)}, f32[32,512]{1,0:T(8,128)S(1)}, u32[]{:S(2)}, u32[]{:S(2)}) collective-permute-start(f32[32,512]{1,0:T(8,128)S(1)} %get-tuple-element.106), channel_id=1, source_target_pairs={{0,8},{8,0},{1,9},{9,1},{2,10},{10,2},{3,11},{11,3},{4,12},{12,4},... | collective-permute-start | bytes 196616 | tf_op jit(solution)/shard_map/ppermute | solution.py:346

commit v5 on v4

--- a/solution.py
+++ b/solution.py
@@ -372,7 +372,8 @@
     near = jnp.stack(ring).reshape(2, 2, 2, 32, LANES)
 
     near, normed = barrier((near, normed))
-    line = jnp.stack([near] + [hop(near, Y, Z, -r) for r in (1, 2, 3)])
+    hops = {r: hop(near, Y, Z, -r) for r in (1, 3, 2)}
+    line = jnp.stack([near] + [hops[r] for r in (1, 2, 3)])
     send = terms_call(core, normed, dpre_t, True)
 
     line, send = barrier((line, send))

time: 93.2 us -> 93.2 us (level)
  no operation moved by 1% of the time
where the time goes in v5:
time: 93.2 us; the launch traced here: 93 us
  Pallas kernels  33.1 us (36%)
  starting transfers between devices  31.7 us (34%)
  waiting for transfers between devices  24.6 us (26%)
  other arithmetic  2.73 us (3%)
    ppermute x20, starting transfers between devices, hop(): return lax.ppermute(value, AXES, pairs)  26.7 us
    ppermute x20, waiting for transfers between devices, hop(): return lax.ppermute(value, AXES, pairs)  22.1 us
    pallas_call x1, Pallas kernels, grad_call(): pl.pallas_call(grad_kernel, grid=(STEPS // 2,), in_specs=[SMEM] + [VMEM]...  8.39 us
    pallas_call x2, Pallas kernels, terms_call(): pl.pallas_call(kernel, in_specs=[SMEM, VMEM, VMEM], out_specs=VMEM, out_s...  7.02 us
    pallas_call x1, Pallas kernels, prepare_call(): pl.pallas_call(prepare_kernel, grid=(ROWS // 128,), in_specs=[rows(D), ro...  6.88 us
    ppermute x4, starting transfers between devices, swap_cores(): return lax.ppermute(value, 'c', [(0, 1), (1, 0)])  4.94 us
    pallas_call x1, Pallas kernels, keys_call(): pl.pallas_call(keys_kernel, in_specs=[SMEM] + [VMEM] * 6, out_specs=[VMEM...  4.4 us
    pallas_call x1, Pallas kernels, own_call(): pl.pallas_call(own_kernel, in_specs=[SMEM] + [VMEM] * 2, out_specs=VMEM,...  3.02 us
  transfers between devices with their start and end apart: 24, of which 9 were waited for; matrix products, arithmetic and copies ran while one was open for 1% of the time, Pallas kernels for 35%

profile of v5, /device:TPU:1, one launch (start us, length us, event | category | flops | bytes accessed | tf_op | source)
XLA Modules:
  0.0 93.0 jit_solution(9179555028454072995)
XLA Ops:
  0.6 0.8 slice_bitcast_fusion
  1.4 1.5 %collective-permute-start = (bf16[32,512]{1,0:T(8,128)(2,1)S(1)}, bf16[32,512]{1,0:T(8,128)(2,1)S(1)}, u32[]{:S(2)}, u32[]{:S(2)}) collective-permute-start(bf16[32,512]{1,0:T(8,128)(2,1)S(1)} %get-tuple-element.108), channel_id=1, source_target_pairs={{0,8},{8,0},{1,9},{9,1},{2,10},{10,2},{3,11},{11,3},{4,12},{12,4},... | collective-permute-start | bytes 98312 | tf_op jit(solution)/shard_map/ppermute | solution.py:346
  2.9 1.0 %multiply_sine_fusion = (f32[512,64]{1,0:T(8,128)S(1)}, f32[512,64]{1,0:T(8,128)S(1)}) fusion(f32[64]{0:T(128)S(1)} %multiply_exponential_fusion, f32[512]{0:T(512)S(1)} %fusion.2), kind=kLoop, calls=%fused_computation.1 | loop fusion | flops 32768 | bytes 264448 | tf_op jit(solution)/shard_map/sin | solution.py:31
  3.9 0.0 collective-permute-done
  4.0 2.6 %collective-permute-start.1 = (bf16[2,32,512]{2,1,0:T(8,128)(2,1)S(1)}, bf16[2,32,512]{2,1,0:T(8,128)(2,1)S(1)}, u32[]{:S(2)}, u32[]{:S(2)}) collective-permute-start(bf16[2,32,512]{2,1,0:T(8,128)(2,1)S(1)} %maximum_select_fusion.1), channel_id=1, source_target_pairs={{0,65},{8,73},{2,67},{10,75},{4,69},{12,77},{6,71},{14,79},{16,81}... | collective-permute-start | bytes 196616 | tf_op jit(solution)/shard_map/ppermute | solution.py:338
  6.6 0.5 collective-permute-start.2
  7.1 0.6 collective-permute-start.3
  7.7 6.9 %row_scales.1 = (bf16[2,8,512,512]{3,2,1,0:T(8,128)(2,1)S(1)}, f32[512,128]{1,0:T(8,128)S(1)}, bf16[512,512]{1,0:T(8,128)(2,1)S(1)}, bf16[512,512]{1,0:T(8,128)(2,1)S(1)}) custom-call(bf16[512,8192]{1,0:T(8,128)(2,1)} %x, bf16[512,512]{1,0:T(8,128)(2,1)} %cot.1, f32[512,64]{1,0:T(8,128)S(1)} %get-tuple-element.57.cosine, f32[512,64]{1,0:T(8,128)S(1)} %get-tuple-element.58.sine), custom_call_target="tpu_custom_call" | custom-call | flops 41943040 | bytes 18874368 | tf_op jit(solution)/shard_map/row_scales/pallas_call | solution.py:80
  14.7 1.7 %collective-permute-start.6 = (bf16[2,2,2,32,512]{4,3,2,1,0:T(8,128)(2,1)S(1)}, bf16[2,2,2,32,512]{4,3,2,1,0:T(8,128)(2,1)S(1)}, u32[]{:S(2)}, u32[]{:S(2)}) collective-permute-start(bf16[2,2,2,32,512]{4,3,2,1,0:T(8,128)(2,1)S(1)} %bitcast.29), channel_id=1, source_target_pairs={{0,16},{8,10},{2,18},{10,12},{4,20},{12,14},{6,22},{14,8},{16,32},... | collective-permute-start | bytes 786440 | tf_op jit(solution)/shard_map/ppermute | solution.py:338
  16.4 3.3 %collective-permute-start.5 = (bf16[2,2,2,32,512]{4,3,2,1,0:T(8,128)(2,1)S(1)}, bf16[2,2,2,32,512]{4,3,2,1,0:T(8,128)(2,1)S(1)}, u32[]{:S(2)}, u32[]{:S(2)}) collective-permute-start(bf16[2,2,2,32,512]{4,3,2,1,0:T(8,128)(2,1)S(1)} %bitcast.30), channel_id=1, source_target_pairs={{0,32},{8,12},{2,34},{10,14},{4,36},{12,8},{6,38},{14,10},{16,48},... | collective-permute-start | bytes 786440 | tf_op jit(solution)/shard_map/ppermute | solution.py:338
  19.7 0.7 collective-permute-start.4
  20.5 3.5 %send_half.1 = bf16[8,16,32,512]{3,2,1,0:T(8,128)(2,1)S(1)} custom-call(s32[1]{0:T(128)} %bitcast.4.core, bf16[2,8,512,512]{3,2,1,0:T(8,128)(2,1)S(1)} %get-tuple-element.60.normed, bf16[512,512]{1,0:T(8,128)(2,1)S(1)} %get-tuple-element.65.dpre_t), custom_call_target="tpu_custom_call" | custom-call | flops 2147483648 | bytes 9437184 | tf_op jit(solution)/shard_map/send_half/pallas_call | solution.py:111
  24.0 2.6 %collective-permute-done.5 = bf16[2,2,2,32,512]{4,3,2,1,0:T(8,128)(2,1)S(1)} collective-permute-done((bf16[2,2,2,32,512]{4,3,2,1,0:T(8,128)(2,1)S(1)}, bf16[2,2,2,32,512]{4,3,2,1,0:T(8,128)(2,1)S(1)}, u32[]{:S(2)}, u32[]{:S(2)}) %collective-permute-start.5) | collective-permute-done | bytes 262176 | tf_op jit(solution)/shard_map/ppermute | solution.py:338
  26.6 0.1 pad_maximum_fusion.refs_0_
  26.7 0.9 collective-permute-start.9
  27.7 2.0 %collective-permute-start.7 = (bf16[4,2,2,2,32,512]{5,4,3,2,1,0:T(8,128)(2,1)S(1)}, bf16[4,2,2,2,32,512]{5,4,3,2,1,0:T(8,128)(2,1)S(1)}, u32[]{:S(2)}, u32[]{:S(2)}) collective-permute-start(bf16[4,2,2,2,32,512]{5,4,3,2,1,0:T(8,128)(2,1)S(1)} %pad_maximum_fusion.refs_0_), channel_id=1, source_target_pairs={{0,6},{8,56},{2,0},{10,58},{4,2},{12,60},{6,4},{14,62},{16,22},{24... | collective-permute-start | bytes 3145736 | tf_op jit(solution)/shard_map/ppermute | solution.py:338
  29.7 3.5 %keep_half.1.kept = bf16[8,16,32,512]{3,2,1,0:T(8,128)(2,1)S(1)} custom-call(s32[1]{0:T(128)} %bitcast.4.core, bf16[2,8,512,512]{3,2,1,0:T(8,128)(2,1)S(1)} %get-tuple-element.60.normed, bf16[512,512]{1,0:T(8,128)(2,1)S(1)} %get-tuple-element.65.dpre_t), custom_call_target="tpu_custom_call" | custom-call | flops 2147483648 | bytes 9437184 | tf_op jit(solution)/shard_map/keep_half/pallas_call | solution.py:111
  33.2 1.3 %collective-permute-done.9.came = bf16[8,16,32,512]{3,2,1,0:T(8,128)(2,1)S(1)} collective-permute-done((bf16[8,16,32,512]{3,2,1,0:T(8,128)(2,1)S(1)}, bf16[8,16,32,512]{3,2,1,0:T(8,128)(2,1)S(1)}, u32[]{:S(2)}, u32[]{:S(2)}) %collective-permute-start.9) | collective-permute-done | bytes 4194336 | tf_op jit(solution)/shard_map/ppermute | solution.py:346
  34.5 1.6 %add_cores.1 = (bf16[4,4,2,32,512]{4,3,2,1,0:T(8,128)(2,1)S(1)}, bf16[4,4,2,32,512]{4,3,2,1,0:T(8,128)(2,1)S(1)}, bf16[4,4,2,32,512]{4,3,2,1,0:T(8,128)(2,1)S(1)...) custom-call(s32[1]{0:T(128)} %bitcast.4.core, s32[1]{0:T(128)} %bitcast.7.x, s32[1]{0:T(128)} %bitcast.5.y, ...), custom_call_target="tpu_custom_call" | custom-call | bytes 12582912 | tf_op jit(solution)/shard_map/add_cores/pallas_call | solution.py:148
  36.0 1.4 %collective-permute-start.13 = (bf16[2,4,2,32,512]{4,3,2,1,0:T(8,128)(2,1)S(1)}, bf16[2,4,2,32,512]{4,3,2,1,0:T(8,128)(2,1)S(1)}, u32[]{:S(2)}, u32[]{:S(2)}) collective-permute-start(bf16[2,4,2,32,512]{4,3,2,1,0:T(8,128)(2,1)S(1)} %get-tuple-element.76), channel_id=1, source_target_pairs={{0,1},{8,24},{2,3},{10,26},{4,5},{12,28},{6,7},{14,30},{16,17},{24... | collective-permute-start | bytes 1572872 | tf_op jit(solution)/shard_map/ppermute | solution.py:338
  37.5 1.3 %collective-permute-start.14 = (bf16[2,4,2,32,512]{4,3,2,1,0:T(8,128)(2,1)S(1)}, bf16[2,4,2,32,512]{4,3,2,1,0:T(8,128)(2,1)S(1)}, u32[]{:S(2)}, u32[]{:S(2)}) collective-permute-start(bf16[2,4,2,32,512]{4,3,2,1,0:T(8,128)(2,1)S(1)} %get-tuple-element.77), channel_id=1, source_target_pairs={{0,65},{8,56},{2,67},{10,58},{4,69},{12,60},{6,71},{14,62},{16,81}... | collective-permute-start | bytes 1572872 | tf_op jit(solution)/shard_map/ppermute | solution.py:338
  38.8 2.8 %collective-permute-done.7.refs_1_ = bf16[4,2,2,2,32,512]{5,4,3,2,1,0:T(8,128)(2,1)S(1)} collective-permute-done((bf16[4,2,2,2,32,512]{5,4,3,2,1,0:T(8,128)(2,1)S(1)}, bf16[4,2,2,2,32,512]{5,4,3,2,1,0:T(8,128)(2,1)S(1)}, u32[]{:S(2)}, u32[]{:S(2)}) %collective-permute-start.7) | collective-permute-done | bytes 1048608 | tf_op jit(solution)/shard_map/ppermute | solution.py:338
  41.6 3.2 %collective-permute-done.8.refs_2_ = bf16[4,2,2,2,32,512]{5,4,3,2,1,0:T(8,128)(2,1)S(1)} collective-permute-done((bf16[4,2,2,2,32,512]{5,4,3,2,1,0:T(8,128)(2,1)S(1)}, bf16[4,2,2,2,32,512]{5,4,3,2,1,0:T(8,128)(2,1)S(1)}, u32[]{:S(2)}, u32[]{:S(2)}) %collective-permute-start.8) | collective-permute-done | bytes 1048608 | tf_op jit(solution)/shard_map/ppermute | solution.py:338
  44.9 0.1 collective-permute-start.10
  45.0 1.5 %collective-permute-start.11 = (bf16[2,2,2,2,32,512]{5,4,3,2,1,0:T(8,128)(2,1)S(1)}, bf16[2,2,2,2,32,512]{5,4,3,2,1,0:T(8,128)(2,1)S(1)}, u32[]{:S(2)}, u32[]{:S(2)}) collective-permute-start(bf16[2,2,2,2,32,512]{5,4,3,2,1,0:T(8,128)(2,1)S(1)} %slice.23), channel_id=1, source_target_pairs={{0,2},{8,24},{2,4},{10,26},{4,6},{12,28},{6,0},{14,30},{16,18},{24... | collective-permute-start | bytes 1572872 | tf_op jit(solution)/shard_map/ppermute | solution.py:338
  46.5 3.6 %collective-permute-done.13.from_below = bf16[2,4,2,32,512]{4,3,2,1,0:T(8,128)(2,1)S(1)} collective-permute-done((bf16[2,4,2,32,512]{4,3,2,1,0:T(8,128)(2,1)S(1)}, bf16[2,4,2,32,512]{4,3,2,1,0:T(8,128)(2,1)S(1)}, u32[]{:S(2)}, u32[]{:S(2)}) %collective-permute-start.13) | collective-permute-done | bytes 524320 | tf_op jit(solution)/shard_map/ppermute | solution.py:338
  50.2 0.8 pass_on.1
  51.0 0.1 collective-permute-start.15
  51.0 2.7 %collective-permute-start.16 = (bf16[4,4,2,32,512]{4,3,2,1,0:T(8,128)(2,1)S(1)}, bf16[4,4,2,32,512]{4,3,2,1,0:T(8,128)(2,1)S(1)}, u32[]{:S(2)}, u32[]{:S(2)}) collective-permute-start(bf16[4,4,2,32,512]{4,3,2,1,0:T(8,128)(2,1)S(1)} %get-tuple-element.79), channel_id=1, source_target_pairs={{0,65},{8,56},{2,67},{10,58},{4,69},{12,60},{6,71},{14,62},{16,81}... | collective-permute-start | bytes 3145736 | tf_op jit(solution)/shard_map/ppermute | solution.py:338
  53.7 2.3 %collective-permute-done.11.refs_4_ = bf16[2,2,2,2,32,512]{5,4,3,2,1,0:T(8,128)(2,1)S(1)} collective-permute-done((bf16[2,2,2,2,32,512]{5,4,3,2,1,0:T(8,128)(2,1)S(1)}, bf16[2,2,2,2,32,512]{5,4,3,2,1,0:T(8,128)(2,1)S(1)}, u32[]{:S(2)}, u32[]{:S(2)}) %collective-permute-start.11) | collective-permute-done | bytes 524320 | tf_op jit(solution)/shard_map/ppermute | solution.py:338
  56.1 0.5 assemble.1.weights.own
  56.6 3.0 %keys_own_half.1.so_far = f32[512,512]{1,0:T(8,128)S(1)} custom-call(s32[1]{0:T(128)} %bitcast.4.core, bf16[2,8,512,512]{3,2,1,0:T(8,128)(2,1)S(1)} %get-tuple-element.60.normed, bf16[4,2,2,4,2,32,512]{6,5,4,3,2,1,0:T(8,128)(2,1)S(1)} %assemble.1.weights.own), custom_call_target="tpu_custom_call" | custom-call | flops 6442450944 | bytes 12582912 | tf_op jit(solution)/shard_map/keys_own_half/pallas_call | solution.py:262
  59.6 2.4 %collective-permute-start.12 = (bf16[4,2,2,4,2,32,512]{6,5,4,3,2,1,0:T(8,128)(2,1)S(1)}, bf16[4,2,2,4,2,32,512]{6,5,4,3,2,1,0:T(8,128)(2,1)S(1)}, u32[]{:S(2)}, u32[]{:S(2)}) collective-permute-start(bf16[4,2,2,4,2,32,512]{6,5,4,3,2,1,0:T(8,128)(2,1)S(1)} %assemble.1.weights.own), channel_id=1, source_target_pairs={{0,8},{8,0},{1,9},{9,1},{2,10},{10,2},{3,11},{11,3},{4,12},{12,4},... | collective-permute-start | bytes 12582920 | tf_op jit(solution)/shard_map/ppermute | solution.py:346
  62.0 5.0 %collective-permute-done.15.one = bf16[4,4,2,32,512]{4,3,2,1,0:T(8,128)(2,1)S(1)} collective-permute-done((bf16[4,4,2,32,512]{4,3,2,1,0:T(8,128)(2,1)S(1)}, bf16[4,4,2,32,512]{4,3,2,1,0:T(8,128)(2,1)S(1)}, u32[]{:S(2)}, u32[]{:S(2)}) %collective-permute-start.15) | collective-permute-done | bytes 1048608 | tf_op jit(solution)/shard_map/ppermute | solution.py:338
  67.0 0.4 sum_first.1
  67.4 1.6 %collective-permute-start.17 = (bf16[4,2,32,512]{3,2,1,0:T(8,128)(2,1)S(1)}, bf16[4,2,32,512]{3,2,1,0:T(8,128)(2,1)S(1)}, u32[]{:S(2)}, u32[]{:S(2)}) collective-permute-start(bf16[4,2,32,512]{3,2,1,0:T(8,128)(2,1)S(1)} %get-tuple-element.81), channel_id=1, source_target_pairs={{0,16},{8,9},{2,18},{10,11},{4,20},{12,13},{6,22},{14,15},{16,32},... | collective-permute-start | bytes 786440 | tf_op jit(solution)/shard_map/ppermute | solution.py:338
  69.0 1.2 %collective-permute-start.18 = (bf16[4,2,32,512]{3,2,1,0:T(8,128)(2,1)S(1)}, bf16[4,2,32,512]{3,2,1,0:T(8,128)(2,1)S(1)}, u32[]{:S(2)}, u32[]{:S(2)}) collective-permute-start(bf16[4,2,32,512]{3,2,1,0:T(8,128)(2,1)S(1)} %get-tuple-element.82), channel_id=1, source_target_pairs={{0,48},{8,73},{2,50},{10,75},{4,52},{12,77},{6,54},{14,79},{16,0},... | collective-permute-start | bytes 786440 | tf_op jit(solution)/shard_map/ppermute | solution.py:338
  70.1 0.9 collective-permute-start.19
  71.0 4.4 %keys.1 = (bf16[512,512]{1,0:T(8,128)(2,1)}, f32[512,128]{1,0:T(8,128)S(1)}) custom-call(s32[1]{0:T(128)} %bitcast.4.core, bf16[2,8,512,512]{3,2,1,0:T(8,128)(2,1)S(1)} %get-tuple-element.60.normed, bf16[512,512]{1,0:T(8,128)(2,1)S(1)} %get-tuple-element.61.dpre, f32[512,64]{1,0:T(8,128)S(1)} %get-tuple-element.57.cosine, ...), custom_call_target="tpu_custom_call" | custom-call | flops 2147483648 | bytes 9437184 | tf_op jit(solution)/shard_map/keys/pallas_call | solution.py:287
  75.4 2.4 %collective-permute-done.19.four = bf16[4,2,32,512]{3,2,1,0:T(8,128)(2,1)S(1)} collective-permute-done((bf16[4,2,32,512]{3,2,1,0:T(8,128)(2,1)S(1)}, bf16[4,2,32,512]{3,2,1,0:T(8,128)(2,1)S(1)}, u32[]{:S(2)}, u32[]{:S(2)}) %collective-permute-start.19) | collective-permute-done | bytes 262176 | tf_op jit(solution)/shard_map/ppermute | solution.py:338
  77.9 0.1 sum_second.1
  78.0 1.1 %collective-permute-start.20 = (bf16[2,32,512]{2,1,0:T(8,128)(2,1)S(1)}, bf16[2,32,512]{2,1,0:T(8,128)(2,1)S(1)}, u32[]{:S(2)}, u32[]{:S(2)}) collective-permute-start(bf16[2,32,512]{2,1,0:T(8,128)(2,1)S(1)} %get-tuple-element.90), channel_id=1, source_target_pairs={{0,2},{8,10},{2,4},{10,12},{4,6},{12,14},{6,0},{14,8},{16,18},{24,... | collective-permute-start | bytes 196616 | tf_op jit(solution)/shard_map/ppermute | solution.py:338
  79.1 2.2 %collective-permute-start.21 = (bf16[2,32,512]{2,1,0:T(8,128)(2,1)S(1)}, bf16[2,32,512]{2,1,0:T(8,128)(2,1)S(1)}, u32[]{:S(2)}, u32[]{:S(2)}) collective-permute-start(bf16[2,32,512]{2,1,0:T(8,128)(2,1)S(1)} %get-tuple-element.91), channel_id=1, source_target_pairs={{0,6},{8,14},{2,0},{10,8},{4,2},{12,10},{6,4},{14,12},{16,22},{24,... | collective-permute-start | bytes 196616 | tf_op jit(solution)/shard_map/ppermute | solution.py:338
  81.3 1.2 %collective-permute-start.22 = (bf16[2,32,512]{2,1,0:T(8,128)(2,1)S(1)}, bf16[2,32,512]{2,1,0:T(8,128)(2,1)S(1)}, u32[]{:S(2)}, u32[]{:S(2)}) collective-permute-start(bf16[2,32,512]{2,1,0:T(8,128)(2,1)S(1)} %get-tuple-element.92), channel_id=1, source_target_pairs={{0,4},{8,12},{2,6},{10,14},{4,0},{12,8},{6,2},{14,10},{16,20},{24,... | collective-permute-start | bytes 196616 | tf_op jit(solution)/shard_map/ppermute | solution.py:338
  82.5 8.4 %input_gradient.1 = bf16[512,8192]{1,0:T(8,128)(2,1)} custom-call(s32[1]{0:T(128)} %bitcast.4.core, bf16[2,8,512,512]{3,2,1,0:T(8,128)(2,1)S(1)} %get-tuple-element.60.normed, bf16[512,512]{1,0:T(8,128)(2,1)S(1)} %get-tuple-element.61.dpre, f32[512,128]{1,0:T(8,128)S(1)} %get-tuple-element.93.inv, f32[512,128]{1,0:T(8,128)S(1)} %get-tuple-element.94.coef, ...), custom_call_target="tpu_custom_call" | custom-call | flops 4294967296 | bytes 18874368 | tf_op jit(solution)/shard_map/input_gradient/pallas_call | solution.py:316
  91.0 0.1 collective-permute-start.23
  91.1 1.2 %collective-permute-done.23 = f32[32,512]{1,0:T(8,128)S(1)} collective-permute-done((f32[32,512]{1,0:T(8,128)S(1)}, f32[32,512]{1,0:T(8,128)S(1)}, u32[]{:S(2)}, u32[]{:S(2)}) %collective-permute-start.23) | collective-permute-done | bytes 65568 | tf_op jit(solution)/shard_map/ppermute | solution.py:346
  92.3 0.7 fusion
  (24 shorter events, 0.3 us)
Async XLA Ops:
  1.4 2.5 %collective-permute-start = (bf16[32,512]{1,0:T(8,128)(2,1)S(1)}, bf16[32,512]{1,0:T(8,128)(2,1)S(1)}, u32[]{:S(2)}, u32[]{:S(2)}) collective-permute-start(bf16[32,512]{1,0:T(8,128)(2,1)S(1)} %get-tuple-element.108), channel_id=1, source_target_pairs={{0,8},{8,0},{1,9},{9,1},{2,10},{10,2},{3,11},{11,3},{4,12},{12,4},... | collective-permute-start | bytes 98312 | tf_op jit(solution)/shard_map/ppermute | solution.py:346
  4.0 10.6 %collective-permute-start.1 = (bf16[2,32,512]{2,1,0:T(8,128)(2,1)S(1)}, bf16[2,32,512]{2,1,0:T(8,128)(2,1)S(1)}, u32[]{:S(2)}, u32[]{:S(2)}) collective-permute-start(bf16[2,32,512]{2,1,0:T(8,128)(2,1)S(1)} %maximum_select_fusion.1), channel_id=1, source_target_pairs={{0,65},{8,73},{2,67},{10,75},{4,69},{12,77},{6,71},{14,79},{16,81}... | collective-permute-start | bytes 196616 | tf_op jit(solution)/shard_map/ppermute | solution.py:338
  6.6 8.0 %collective-permute-start.2 = (bf16[2,32,512]{2,1,0:T(8,128)(2,1)S(1)}, bf16[2,32,512]{2,1,0:T(8,128)(2,1)S(1)}, u32[]{:S(2)}, u32[]{:S(2)}) collective-permute-start(bf16[2,32,512]{2,1,0:T(8,128)(2,1)S(1)} %maximum_select_fusion.1), channel_id=1, source_target_pairs={{0,64},{8,72},{2,66},{10,74},{4,68},{12,76},{6,70},{14,78},{16,80}... | collective-permute-start | bytes 196616 | tf_op jit(solution)/shard_map/ppermute | solution.py:338
  7.1 7.5 %collective-permute-start.3 = (bf16[2,32,512]{2,1,0:T(8,128)(2,1)S(1)}, bf16[2,32,512]{2,1,0:T(8,128)(2,1)S(1)}, u32[]{:S(2)}, u32[]{:S(2)}) collective-permute-start(bf16[2,32,512]{2,1,0:T(8,128)(2,1)S(1)} %maximum_select_fusion.1), channel_id=1, source_target_pairs={{0,1},{8,9},{2,3},{10,11},{4,5},{12,13},{6,7},{14,15},{16,17},{24,... | collective-permute-start | bytes 196616 | tf_op jit(solution)/shard_map/ppermute | solution.py:338
  14.7 9.3 %collective-permute-start.6 = (bf16[2,2,2,32,512]{4,3,2,1,0:T(8,128)(2,1)S(1)}, bf16[2,2,2,32,512]{4,3,2,1,0:T(8,128)(2,1)S(1)}, u32[]{:S(2)}, u32[]{:S(2)}) collective-permute-start(bf16[2,2,2,32,512]{4,3,2,1,0:T(8,128)(2,1)S(1)} %bitcast.29), channel_id=1, source_target_pairs={{0,16},{8,10},{2,18},{10,12},{4,20},{12,14},{6,22},{14,8},{16,32},... | collective-permute-start | bytes 786440 | tf_op jit(solution)/shard_map/ppermute | solution.py:338
  16.4 10.2 %collective-permute-start.5 = (bf16[2,2,2,32,512]{4,3,2,1,0:T(8,128)(2,1)S(1)}, bf16[2,2,2,32,512]{4,3,2,1,0:T(8,128)(2,1)S(1)}, u32[]{:S(2)}, u32[]{:S(2)}) collective-permute-start(bf16[2,2,2,32,512]{4,3,2,1,0:T(8,128)(2,1)S(1)} %bitcast.30), channel_id=1, source_target_pairs={{0,32},{8,12},{2,34},{10,14},{4,36},{12,8},{6,38},{14,10},{16,48},... | collective-permute-start | bytes 786440 | tf_op jit(solution)/shard_map/ppermute | solution.py:338
  19.7 6.9 %collective-permute-start.4 = (bf16[2,2,2,32,512]{4,3,2,1,0:T(8,128)(2,1)S(1)}, bf16[2,2,2,32,512]{4,3,2,1,0:T(8,128)(2,1)S(1)}, u32[]{:S(2)}, u32[]{:S(2)}) collective-permute-start(bf16[2,2,2,32,512]{4,3,2,1,0:T(8,128)(2,1)S(1)} %bitcast.31), channel_id=1, source_target_pairs={{0,48},{8,14},{2,50},{10,8},{4,52},{12,10},{6,54},{14,12},{16,0},{... | collective-permute-start | bytes 786440 | tf_op jit(solution)/shard_map/ppermute | solution.py:338
  26.7 7.7 %collective-permute-start.9 = (bf16[8,16,32,512]{3,2,1,0:T(8,128)(2,1)S(1)}, bf16[8,16,32,512]{3,2,1,0:T(8,128)(2,1)S(1)}, u32[]{:S(2)}, u32[]{:S(2)}) collective-permute-start(bf16[8,16,32,512]{3,2,1,0:T(8,128)(2,1)S(1)} %send_half.1), channel_id=1, source_target_pairs={{0,8},{8,0},{1,9},{9,1},{2,10},{10,2},{3,11},{11,3},{4,12},{12,4},... | collective-permute-start | bytes 12582920 | tf_op jit(solution)/shard_map/ppermute | solution.py:346
  27.7 13.9 %collective-permute-start.7 = (bf16[4,2,2,2,32,512]{5,4,3,2,1,0:T(8,128)(2,1)S(1)}, bf16[4,2,2,2,32,512]{5,4,3,2,1,0:T(8,128)(2,1)S(1)}, u32[]{:S(2)}, u32[]{:S(2)}) collective-permute-start(bf16[4,2,2,2,32,512]{5,4,3,2,1,0:T(8,128)(2,1)S(1)} %pad_maximum_fusion.refs_0_), channel_id=1, source_target_pairs={{0,6},{8,56},{2,0},{10,58},{4,2},{12,60},{6,4},{14,62},{16,22},{24... | collective-permute-start | bytes 3145736 | tf_op jit(solution)/shard_map/ppermute | solution.py:338
  29.7 15.2 %collective-permute-start.8 = (bf16[4,2,2,2,32,512]{5,4,3,2,1,0:T(8,128)(2,1)S(1)}, bf16[4,2,2,2,32,512]{5,4,3,2,1,0:T(8,128)(2,1)S(1)}, u32[]{:S(2)}, u32[]{:S(2)}) collective-permute-start(bf16[4,2,2,2,32,512]{5,4,3,2,1,0:T(8,128)(2,1)S(1)} %pad_maximum_fusion.refs_0_), channel_id=1, source_target_pairs={{0,2},{8,24},{2,4},{10,26},{4,6},{12,28},{6,0},{14,30},{16,18},{24... | collective-permute-start | bytes 3145736 | tf_op jit(solution)/shard_map/ppermute | solution.py:338
  36.0 14.1 %collective-permute-start.13 = (bf16[2,4,2,32,512]{4,3,2,1,0:T(8,128)(2,1)S(1)}, bf16[2,4,2,32,512]{4,3,2,1,0:T(8,128)(2,1)S(1)}, u32[]{:S(2)}, u32[]{:S(2)}) collective-permute-start(bf16[2,4,2,32,512]{4,3,2,1,0:T(8,128)(2,1)S(1)} %get-tuple-element.76), channel_id=1, source_target_pairs={{0,1},{8,24},{2,3},{10,26},{4,5},{12,28},{6,7},{14,30},{16,17},{24... | collective-permute-start | bytes 1572872 | tf_op jit(solution)/shard_map/ppermute | solution.py:338
  37.5 12.7 %collective-permute-start.14 = (bf16[2,4,2,32,512]{4,3,2,1,0:T(8,128)(2,1)S(1)}, bf16[2,4,2,32,512]{4,3,2,1,0:T(8,128)(2,1)S(1)}, u32[]{:S(2)}, u32[]{:S(2)}) collective-permute-start(bf16[2,4,2,32,512]{4,3,2,1,0:T(8,128)(2,1)S(1)} %get-tuple-element.77), channel_id=1, source_target_pairs={{0,65},{8,56},{2,67},{10,58},{4,69},{12,60},{6,71},{14,62},{16,81}... | collective-permute-start | bytes 1572872 | tf_op jit(solution)/shard_map/ppermute | solution.py:338
  44.9 8.8 %collective-permute-start.10 = (bf16[2,2,2,2,32,512]{5,4,3,2,1,0:T(8,128)(2,1)S(1)}, bf16[2,2,2,2,32,512]{5,4,3,2,1,0:T(8,128)(2,1)S(1)}, u32[]{:S(2)}, u32[]{:S(2)}) collective-permute-start(bf16[2,2,2,2,32,512]{5,4,3,2,1,0:T(8,128)(2,1)S(1)} %slice.22), channel_id=1, source_target_pairs={{0,6},{8,56},{2,0},{10,58},{4,2},{12,60},{6,4},{14,62},{16,22},{24... | collective-permute-start | bytes 1572872 | tf_op jit(solution)/shard_map/ppermute | solution.py:338
  45.0 11.1 %collective-permute-start.11 = (bf16[2,2,2,2,32,512]{5,4,3,2,1,0:T(8,128)(2,1)S(1)}, bf16[2,2,2,2,32,512]{5,4,3,2,1,0:T(8,128)(2,1)S(1)}, u32[]{:S(2)}, u32[]{:S(2)}) collective-permute-start(bf16[2,2,2,2,32,512]{5,4,3,2,1,0:T(8,128)(2,1)S(1)} %slice.23), channel_id=1, source_target_pairs={{0,2},{8,24},{2,4},{10,26},{4,6},{12,28},{6,0},{14,30},{16,18},{24... | collective-permute-start | bytes 1572872 | tf_op jit(solution)/shard_map/ppermute | solution.py:338
  51.0 16.0 %collective-permute-start.15 = (bf16[4,4,2,32,512]{4,3,2,1,0:T(8,128)(2,1)S(1)}, bf16[4,4,2,32,512]{4,3,2,1,0:T(8,128)(2,1)S(1)}, u32[]{:S(2)}, u32[]{:S(2)}) collective-permute-start(bf16[4,4,2,32,512]{4,3,2,1,0:T(8,128)(2,1)S(1)} %get-tuple-element.78), channel_id=1, source_target_pairs={{0,1},{8,24},{2,3},{10,26},{4,5},{12,28},{6,7},{14,30},{16,17},{24... | collective-permute-start | bytes 3145736 | tf_op jit(solution)/shard_map/ppermute | solution.py:338
  51.0 16.0 %collective-permute-start.16 = (bf16[4,4,2,32,512]{4,3,2,1,0:T(8,128)(2,1)S(1)}, bf16[4,4,2,32,512]{4,3,2,1,0:T(8,128)(2,1)S(1)}, u32[]{:S(2)}, u32[]{:S(2)}) collective-permute-start(bf16[4,4,2,32,512]{4,3,2,1,0:T(8,128)(2,1)S(1)} %get-tuple-element.79), channel_id=1, source_target_pairs={{0,65},{8,56},{2,67},{10,58},{4,69},{12,60},{6,71},{14,62},{16,81}... | collective-permute-start | bytes 3145736 | tf_op jit(solution)/shard_map/ppermute | solution.py:338
  59.6 11.4 %collective-permute-start.12 = (bf16[4,2,2,4,2,32,512]{6,5,4,3,2,1,0:T(8,128)(2,1)S(1)}, bf16[4,2,2,4,2,32,512]{6,5,4,3,2,1,0:T(8,128)(2,1)S(1)}, u32[]{:S(2)}, u32[]{:S(2)}) collective-permute-start(bf16[4,2,2,4,2,32,512]{6,5,4,3,2,1,0:T(8,128)(2,1)S(1)} %assemble.1.weights.own), channel_id=1, source_target_pairs={{0,8},{8,0},{1,9},{9,1},{2,10},{10,2},{3,11},{11,3},{4,12},{12,4},... | collective-permute-start | bytes 12582920 | tf_op jit(solution)/shard_map/ppermute | solution.py:346
  67.4 8.0 %collective-permute-start.17 = (bf16[4,2,32,512]{3,2,1,0:T(8,128)(2,1)S(1)}, bf16[4,2,32,512]{3,2,1,0:T(8,128)(2,1)S(1)}, u32[]{:S(2)}, u32[]{:S(2)}) collective-permute-start(bf16[4,2,32,512]{3,2,1,0:T(8,128)(2,1)S(1)} %get-tuple-element.81), channel_id=1, source_target_pairs={{0,16},{8,9},{2,18},{10,11},{4,20},{12,13},{6,22},{14,15},{16,32},... | collective-permute-start | bytes 786440 | tf_op jit(solution)/shard_map/ppermute | solution.py:338
  69.0 6.4 %collective-permute-start.18 = (bf16[4,2,32,512]{3,2,1,0:T(8,128)(2,1)S(1)}, bf16[4,2,32,512]{3,2,1,0:T(8,128)(2,1)S(1)}, u32[]{:S(2)}, u32[]{:S(2)}) collective-permute-start(bf16[4,2,32,512]{3,2,1,0:T(8,128)(2,1)S(1)} %get-tuple-element.82), channel_id=1, source_target_pairs={{0,48},{8,73},{2,50},{10,75},{4,52},{12,77},{6,54},{14,79},{16,0},... | collective-permute-start | bytes 786440 | tf_op jit(solution)/shard_map/ppermute | solution.py:338
  70.1 7.7 %collective-permute-start.19 = (bf16[4,2,32,512]{3,2,1,0:T(8,128)(2,1)S(1)}, bf16[4,2,32,512]{3,2,1,0:T(8,128)(2,1)S(1)}, u32[]{:S(2)}, u32[]{:S(2)}) collective-permute-start(bf16[4,2,32,512]{3,2,1,0:T(8,128)(2,1)S(1)} %get-tuple-element.83), channel_id=1, source_target_pairs={{0,32},{8,72},{2,34},{10,74},{4,36},{12,76},{6,38},{14,78},{16,48}... | collective-permute-start | bytes 786440 | tf_op jit(solution)/shard_map/ppermute | solution.py:338
  78.0 12.9 %collective-permute-start.20 = (bf16[2,32,512]{2,1,0:T(8,128)(2,1)S(1)}, bf16[2,32,512]{2,1,0:T(8,128)(2,1)S(1)}, u32[]{:S(2)}, u32[]{:S(2)}) collective-permute-start(bf16[2,32,512]{2,1,0:T(8,128)(2,1)S(1)} %get-tuple-element.90), channel_id=1, source_target_pairs={{0,2},{8,10},{2,4},{10,12},{4,6},{12,14},{6,0},{14,8},{16,18},{24,... | collective-permute-start | bytes 196616 | tf_op jit(solution)/shard_map/ppermute | solution.py:338
  79.1 11.8 %collective-permute-start.21 = (bf16[2,32,512]{2,1,0:T(8,128)(2,1)S(1)}, bf16[2,32,512]{2,1,0:T(8,128)(2,1)S(1)}, u32[]{:S(2)}, u32[]{:S(2)}) collective-permute-start(bf16[2,32,512]{2,1,0:T(8,128)(2,1)S(1)} %get-tuple-element.91), channel_id=1, source_target_pairs={{0,6},{8,14},{2,0},{10,8},{4,2},{12,10},{6,4},{14,12},{16,22},{24,... | collective-permute-start | bytes 196616 | tf_op jit(solution)/shard_map/ppermute | solution.py:338
  81.3 9.6 %collective-permute-start.22 = (bf16[2,32,512]{2,1,0:T(8,128)(2,1)S(1)}, bf16[2,32,512]{2,1,0:T(8,128)(2,1)S(1)}, u32[]{:S(2)}, u32[]{:S(2)}) collective-permute-start(bf16[2,32,512]{2,1,0:T(8,128)(2,1)S(1)} %get-tuple-element.92), channel_id=1, source_target_pairs={{0,4},{8,12},{2,6},{10,14},{4,0},{12,8},{6,2},{14,10},{16,20},{24,... | collective-permute-start | bytes 196616 | tf_op jit(solution)/shard_map/ppermute | solution.py:338
  91.0 1.3 %collective-permute-start.23 = (f32[32,512]{1,0:T(8,128)S(1)}, f32[32,512]{1,0:T(8,128)S(1)}, u32[]{:S(2)}, u32[]{:S(2)}) collective-permute-start(f32[32,512]{1,0:T(8,128)S(1)} %get-tuple-element.106), channel_id=1, source_target_pairs={{0,8},{8,0},{1,9},{9,1},{2,10},{10,2},{3,11},{11,3},{4,12},{12,4},... | collective-permute-start | bytes 196616 | tf_op jit(solution)/shard_map/ppermute | solution.py:346
